TPU v7x, 32 devices: a whole 2x2x4 slice. The times are simulated.
32 devices in a mesh: outer: 16 (over z, x, core), inner: 2 (over y).
Axes of the slice: x: 2, y: 2, z: 4, core: 2. Of those that a mesh axis runs over, the one named last changes fastest.
Arguments:
- qkv: bfloat16 [2048, 8, 10, 128], P(('outer', 'inner')), may hold values from -96 to 96
- key_codes: int32 [2048, 8, 16], P('outer', 'inner'), may hold values from 0 to 255
- codebooks: bfloat16 [8, 256, 128], P('inner'), may hold values from -4 to 4
- value_codes: bfloat16 [2048, 8, 128], P('outer', 'inner'), may hold values from -4 to 4
- value_scales: float32 [2048, 8], P('outer', 'inner'), may hold values from 0.25 to 4
- block_ids: int32 [16], P('outer'), may hold values from 0 to 15, each once
Outputs:
- attended: bfloat16 [2048, 8, 8, 128], P(('outer', 'inner'))
All inputs are finite; a program needn't handle non-finite values.
Results may differ from a plain program's by a relative error of at most 0.011.
Values may be sent and summed in bfloat16 or wider, within the bound.
No kernel may reach another device: no remote copies, remote signals or barrier semaphores. Data moves between devices by JAX's collectives and lax.ppermute only.
A program may use at most 64 MiB of HBM per device.

v0:
```python
import math

import jax
import jax.numpy as jnp
from jax import lax
from jax.sharding import PartitionSpec as P

rope_base = 500000.0


def rotate(tensor, position):
    half_dim = tensor.shape[-1] // 2
    ladder = jnp.arange(half_dim, dtype=jnp.float32)
    inverse = jnp.exp(ladder * jnp.float32(-2.0 * math.log(rope_base) / tensor.shape[-1]))
    angles = position.astype(jnp.float32)[:, None] * inverse[None, :]
    target = (position.shape[0],) + (1,) * (tensor.ndim - 2) + (half_dim,)
    cosine = jnp.cos(angles).reshape(target)
    sine_part = jnp.sin(angles).reshape(target)
    floats = tensor.astype(jnp.float32)
    first_half = floats[..., :half_dim]
    second_half = floats[..., half_dim:]
    return jnp.concatenate(
        [
            first_half * cosine - second_half * sine_part,
            second_half * cosine + first_half * sine_part,
        ],
        axis=-1,
    )


def decode_block(key_codes, codebooks):
    block_rows, kv_local, group_count = key_codes.shape
    entries = codebooks.shape[1]
    head_dim = codebooks.shape[2]
    ladder = lax.broadcasted_iota(jnp.int32, (1, 1, 1, entries), 3).astype(jnp.float32)
    one_hot = (key_codes.astype(jnp.float32)[..., None] == ladder).astype(jnp.bfloat16)
    code_table = codebooks.reshape(kv_local, entries, group_count, head_dim // group_count)
    decoded = jnp.einsum("bkgc,kcgd->bkgd", one_hot, code_table, preferred_element_type=jnp.float32)
    return decoded.reshape(block_rows, kv_local, head_dim)


def span_of():
    return 1024


def absorb(state, queries, key_rows, value_rows, allowed):
    running_max, running_sum, weighted = state
    scores = jnp.einsum(
        "tkgd,nkd->tkgn", queries, key_rows, preferred_element_type=jnp.float32
    ) * queries.shape[-1] ** (-0.5)
    if allowed is not None:
        scores = jnp.where(allowed[:, None, None, :], scores, -jnp.inf)
    new_max = jnp.maximum(running_max, jnp.max(scores, axis=-1))
    decay_factor = jnp.exp(running_max - new_max)
    weights = jnp.exp(scores - new_max[..., None])
    running_sum = running_sum * decay_factor + jnp.sum(weights, axis=-1)
    weighted = weighted * decay_factor[..., None] + jnp.einsum(
        "tkgn,nkd->tkgd",
        weights.astype(jnp.bfloat16),
        value_rows,
        preferred_element_type=jnp.float32,
    )
    return (new_max, running_sum, weighted)


def shards(qkv, key_codes, codebooks, value_codes, value_scales, block_ids):
    group_heads = qkv.shape[2] - 2
    head_dim = qkv.shape[3]
    block_rows = key_codes.shape[0]
    prefix_len = block_rows * lax.axis_size("outer")
    prefix_values = (value_codes.astype(jnp.float32) * value_scales[:, :, None]).astype(
        jnp.bfloat16
    )
    exchanged = lax.all_to_all(qkv, "inner", split_axis=1, concat_axis=0, tiled=True)
    stretch_rows = exchanged.shape[0]
    kv_local = exchanged.shape[1]
    local_pos = jnp.arange(stretch_rows, dtype=jnp.int32)
    stretch_pos = prefix_len + local_pos
    queries = rotate(exchanged[:, :, :group_heads, :], stretch_pos).astype(jnp.bfloat16)
    stretch_keys = rotate(exchanged[:, :, group_heads, :], stretch_pos).astype(jnp.bfloat16)
    stretch_values = exchanged[:, :, group_heads + 1, :]
    initial = (
        jnp.full((stretch_rows, kv_local, group_heads), -1e30, jnp.float32),
        jnp.zeros((stretch_rows, kv_local, group_heads), jnp.float32),
        jnp.zeros((stretch_rows, kv_local, group_heads, head_dim), jnp.float32),
    )
    own_pos = block_ids[0] * block_rows + jnp.arange(block_rows, dtype=jnp.int32)
    prefix_keys = rotate(decode_block(key_codes, codebooks), own_pos).astype(jnp.bfloat16)
    key_rows = lax.all_gather(prefix_keys, "outer", axis=0, tiled=True)
    value_rows = lax.all_gather(prefix_values, "outer", axis=0, tiled=True)
    length = key_rows.shape[0]
    span_rows = span_of()

    def advance(step_index, inner_state):
        first_row = step_index * span_rows
        key_part = lax.dynamic_slice_in_dim(key_rows, first_row, span_rows, 0)
        value_part = lax.dynamic_slice_in_dim(value_rows, first_row, span_rows, 0)
        return absorb(inner_state, queries, key_part, value_part, None)

    allowed = local_pos[None, :] <= local_pos[:, None]
    final_state = lax.fori_loop(
        0,
        length // span_rows,
        advance,
        absorb(initial, queries, stretch_keys, stretch_values, allowed),
    )
    running_max, running_sum, weighted = final_state
    outputs = (weighted / running_sum[..., None]).astype(jnp.bfloat16)
    return lax.all_to_all(outputs, "inner", split_axis=0, concat_axis=1, tiled=True)


def solution(mesh):
    return jax.shard_map(
        shards,
        mesh=mesh,
        in_specs=(
            P(("outer", "inner"), None, None, None),
            P("outer", "inner", None),
            P("inner", None, None),
            P("outer", "inner", None),
            P("outer", "inner"),
            P("outer"),
        ),
        out_specs=P(("outer", "inner"), None, None, None),
        check_vma=False,
    )
```

profile of v0, /device:TPU:0, one launch (start us, length us, event | category | flops | bytes accessed | tf_op | source)
XLA Modules:
  0.0 176.5 jit_solution(13336004903232090280)
XLA Ops:
  6.5 0.0 all-gather.5.cloned.1.call-start
  6.5 1.0 copy.56
  7.6 1.4 multiply_convert_fusion
  8.9 0.0 all-gather.5.cloned.1.call-update
  9.0 0.0 copy-start.3
  9.0 0.0 copy-start.2
  9.0 2.8 %copy.50 = bf16[64,8,10,128]{3,0,2,1:T(8,128)(2,1)} copy(bf16[64,8,10,128]{3,1,2,0:T(8,128)(2,1)} %param.8) | data formatting | bytes 2621440 | tf_op args[0]
  11.8 4.2 %all-to-all-start = ((bf16[64,8,10,128]{3,0,2,1:T(8,128)(2,1)}), bf16[64,8,10,128]{3,0,2,1:T(8,128)(2,1)S(1)}, u32[]{:S(2)}, u32[]{:S(2)}) async-start(bf16[64,8,10,128]{3,0,2,1:T(8,128)(2,1)} %copy.50), calls=%async_computation | async-start | bytes 2621440 | tf_op jit(solution)/shard_map/all_to_all | solution.py:74
  16.0 0.0 all-gather.3.cloned.1.call-start
  16.0 0.0 copy-done.3
  16.0 0.0 copy-done.2
  16.0 0.1 copy.53
  16.2 1.4 fusion.23
  18.3 0.1 copy.68
  18.4 0.1 copy.67
  18.6 0.5 multiply_cosine_fusion
  19.1 14.2 %all-to-all-done = bf16[64,8,10,128]{3,0,2,1:T(8,128)(2,1)S(1)} async-done(((bf16[64,8,10,128]{3,0,2,1:T(8,128)(2,1)}), bf16[64,8,10,128]{3,0,2,1:T(8,128)(2,1)S(1)}, u32[]{:S(2)}, u32[]{:S(2)}) %all-to-all-start) | async-done | bytes 1310752 | tf_op jit(solution)/shard_map/all_to_all | solution.py:74
  33.3 0.0 copy-start.1
  33.3 1.1 copy-done.1
  34.4 1.4 copy.51
  35.9 0.2 subtract_convert_fusion.1
  36.1 0.8 pad_maximum_fusion.1
  36.8 0.0 all-gather.3.cloned.1.call-update
  36.9 0.2 slice_convert_fusion
  37.1 0.8 subtract_convert_fusion
  37.9 0.6 pad_maximum_fusion
  38.5 0.5 fusion.35
  39.0 0.4 fusion.22
  39.5 2.2 %bitcast_add_fusion.1 = f32[128,4,8,128]{3,0,2,1:T(8,128)} fusion(f32[128,4,8,128]{0,3,2,1:T(8,128)S(1)} %get-tuple-element.202, f32[128,4,8]{0,2,1:T(8,128)S(1)} %get-tuple-element.193, f32[128,4,8]{0,2,1:T(8,128)S(1)} %broadcast_maximum_fusion, bf16[128,4,10,128]{3,0,2,1:T(8,128)(2,1)S(1)} %bitcast.82), kind=kOutput, calls=%fused_computation.23 | convolution fusion | flops 135790592 | bytes 4358144 | tf_op jit(solution)/shard_map/tkgn,nkd->tkgd/dot_general | solution.py:57
  41.7 1.9 %copy.57 = f32[128,4,8,128]{0,3,2,1:T(8,128)S(1)} copy(f32[128,4,8,128]{3,0,2,1:T(8,128)} %bitcast_add_fusion.1) | data formatting | bytes 4194304 | tf_op jit(solution)/shard_map/while | solution.py:101
  43.6 9.9 %all-gather.5.cloned.1.call-done = bf16[2048,4,128]{0,2,1:T(8,128)(2,1)} async-done(((bf16[128,4,128]{0,2,1:T(8,128)(2,1)}), bf16[2048,4,128]{0,2,1:T(8,128)(2,1)}) %all-gather.5.cloned.1.call-update) | async-done | bytes 2097168 | tf_op jit(solution)/shard_map/all_gather | solution.py:90
  53.5 42.5 %all-gather.3.cloned.1.call-done = bf16[2048,4,128]{2,0,1:T(8,128)(2,1)} async-done(((bf16[128,4,128]{2,0,1:T(8,128)(2,1)}), bf16[2048,4,128]{2,0,1:T(8,128)(2,1)}) %all-gather.3.cloned.1.call-update) | async-done | bytes 2097168 | tf_op jit(solution)/shard_map/all_gather | solution.py:89
  96.1 51.6 %while.17 = (s32[]{:T(128)}, f32[128,4,8]{0,2,1:T(8,128)S(1)}, f32[128,4,8]{0,2,1:T(8,128)S(1)}, f32[128,4,8,128]{0,3,2,1:T(8,128)S(1)}, bf16[2048,4,128]{2,0,1:...) while((s32[]{:T(128)}, f32[128,4,8]{0,2,1:T(8,128)S(1)}, ...), condition=%wide.region_5.6_spmd, body=%wide.region_2.5_spmd.sunk | while | flops 2182094848 | bytes 66322624 | solution.py:101
  96.1 9.3 %bitcast_reduce_fusion.2 = (f32[128,4,8]{0,2,1:T(8,128)S(1)}, f32[4,1024,128,8]{2,1,3,0:T(8,128)}) fusion(bf16[128,4,8,128]{3,0,2,1:T(8,128)(2,1)S(1)} %get-tuple-element.283, bf16[2048,4,128]{2,0,1:T(8,128)(2,1)} %get-tuple-element.282, s32[]{:T(128)S(6)} %select_n.15), kind=kOutput, calls=%fused_computation.1.clone.1 | convolution fusion | flops 1082126336 | bytes 18890756 | tf_op jit(solution)/shard_map/while/body/eval_jaxpr/tkgd,nkd->tkgn/dot_general | solution.py:48
  105.4 0.0 copy-start
  105.4 8.9 %fusion.45 = f32[128,4,8]{0,2,1:T(8,128)S(1)} fusion(f32[4,1024,128,8]{2,1,3,0:T(8,128)} %get-tuple-element.253, f32[128,4,8]{0,2,1:T(8,128)S(1)} %max.8), kind=kLoop, calls=%fused_computation.4.clone.1 | loop fusion | flops 12578816 | bytes 16809984 | tf_op jit(solution)/shard_map/while/body/eval_jaxpr/reduce_sum | solution.py:56
  114.3 0.0 copy-done
  114.3 7.5 %bitcast_add_fusion.3 = f32[128,4,8,128]{0,3,2,1:T(8,128)S(1)} fusion(f32[128,4,8,128]{0,3,2,1:T(8,128)S(1)} %get-tuple-element.270, f32[4,1024,128,8]{2,1,3,0:T(8,128)} %get-tuple-element.253, f32[128,4,8]{0,2,1:T(8,128)S(1)} %max.8, bf16[2048,4,128]{0,2,1:T(8,128)(2,1)S(1)} %copy-done, s32[]{:T(128)S(6)} %select_n.15, ...), kind=kOutput, calls=%fused_computation.8.clone.1 | convolution fusion | flops 1087373312 | bytes 22052868 | tf_op jit(solution)/shard_map/while/body/eval_jaxpr/tkgn,nkd->tkgd/dot_general | solution.py:57
  121.8 9.3 %bitcast_reduce_fusion.2 = (f32[128,4,8]{0,2,1:T(8,128)S(1)}, f32[4,1024,128,8]{2,1,3,0:T(8,128)}) fusion(bf16[128,4,8,128]{3,0,2,1:T(8,128)(2,1)S(1)} %get-tuple-element.283, bf16[2048,4,128]{2,0,1:T(8,128)(2,1)} %get-tuple-element.282, s32[]{:T(128)S(6)} %select_n.15), kind=kOutput, calls=%fused_computation.1.clone.1 | convolution fusion | flops 1082126336 | bytes 18890756 | tf_op jit(solution)/shard_map/while/body/eval_jaxpr/tkgd,nkd->tkgn/dot_general | solution.py:48
  131.2 0.0 copy-start
  131.2 8.9 %fusion.45 = f32[128,4,8]{0,2,1:T(8,128)S(1)} fusion(f32[4,1024,128,8]{2,1,3,0:T(8,128)} %get-tuple-element.253, f32[128,4,8]{0,2,1:T(8,128)S(1)} %max.8), kind=kLoop, calls=%fused_computation.4.clone.1 | loop fusion | flops 12578816 | bytes 16809984 | tf_op jit(solution)/shard_map/while/body/eval_jaxpr/reduce_sum | solution.py:56
  140.1 0.0 copy-done
  140.1 7.5 %bitcast_add_fusion.3 = f32[128,4,8,128]{0,3,2,1:T(8,128)S(1)} fusion(f32[128,4,8,128]{0,3,2,1:T(8,128)S(1)} %get-tuple-element.270, f32[4,1024,128,8]{2,1,3,0:T(8,128)} %get-tuple-element.253, f32[128,4,8]{0,2,1:T(8,128)S(1)} %max.8, bf16[2048,4,128]{0,2,1:T(8,128)(2,1)S(1)} %copy-done, s32[]{:T(128)S(6)} %select_n.15, ...), kind=kOutput, calls=%fused_computation.8.clone.1 | convolution fusion | flops 1087373312 | bytes 22052868 | tf_op jit(solution)/shard_map/while/body/eval_jaxpr/tkgn,nkd->tkgd/dot_general | solution.py:57
  147.6 0.1 copy.58
  147.8 2.1 %copy.59 = f32[128,4,8,128]{3,2,1,0:T(8,128)} copy(f32[128,4,8,128]{0,3,2,1:T(8,128)S(1)} %get-tuple-element.130) | data formatting | bytes 4194304 | tf_op jit(solution)/shard_map/while | solution.py:101
  149.9 1.9 %divide_convert_fusion = bf16[128,4,8,128]{3,2,1,0:T(8,128)(2,1)S(1)} fusion(f32[128,4,8,128]{3,2,1,0:T(8,128)} %copy.59, f32[128,4,8]{2,1,0:T(4,128)S(1)} %copy.58), kind=kLoop, calls=%fused_computation.25 | loop fusion | flops 1048576 | bytes 3162112 | tf_op jit(solution)/shard_map/convert_element_type | solution.py:108
  151.8 16.8 %all_to_all.36 = bf16[128,4,8,128]{3,2,1,0:T(8,128)(2,1)S(1)} all-to-all(bf16[128,4,8,128]{3,2,1,0:T(8,128)(2,1)S(1)} %divide_convert_fusion), channel_id=1, replica_groups=mesh['outer'=16,'inner'=2] {'inner'}, dimensions={0} | all-to-all | bytes 2097152 | tf_op jit(solution)/shard_map/all_to_all | solution.py:109
  168.6 1.1 copy.60
  (16 shorter events, 0.1 us)
Async XLA Ops:
  6.5 47.0 %all-gather.5.cloned.1.call-start = ((), (), s32[]{:S(2)}) async-start(), calls=%async_computation.3 | async-start | bytes 2228224 | tf_op jit(solution)/shard_map/all_gather | solution.py:90
  9.0 7.0 %copy-start.3 = (s32[128,4,16]{0,2,1:T(8,128)S(1)}, s32[128,4,16]{0,2,1:T(8,128)}, u32[]{:S(2)}) copy-start(s32[128,4,16]{0,2,1:T(8,128)} %param.9) | copy-start | bytes 98308
  9.0 7.0 %copy-start.2 = (bf16[4,256,128]{2,1,0:T(8,128)(2,1)S(1)}, bf16[4,256,128]{2,1,0:T(8,128)(2,1)}, u32[]{:S(2)}) copy-start(bf16[4,256,128]{2,1,0:T(8,128)(2,1)} %param.10) | copy-start | bytes 786436
  11.8 21.5 %all-to-all-start = ((bf16[64,8,10,128]{3,0,2,1:T(8,128)(2,1)}), bf16[64,8,10,128]{3,0,2,1:T(8,128)(2,1)S(1)}, u32[]{:S(2)}, u32[]{:S(2)}) async-start(bf16[64,8,10,128]{3,0,2,1:T(8,128)(2,1)} %copy.50), calls=%async_computation | async-start | bytes 2621440 | tf_op jit(solution)/shard_map/all_to_all | solution.py:74
  16.0 80.0 %all-gather.3.cloned.1.call-start = ((), (), s32[]{:S(2)}) async-start(), calls=%async_computation.2 | async-start | bytes 2228224 | tf_op jit(solution)/shard_map/all_gather | solution.py:89
  33.3 1.1 copy-start.1
  105.4 8.9 %copy-start = (bf16[2048,4,128]{0,2,1:T(8,128)(2,1)S(1)}, bf16[2048,4,128]{0,2,1:T(8,128)(2,1)}, u32[]{:S(2)}) copy-start(bf16[2048,4,128]{0,2,1:T(8,128)(2,1)} %get-tuple-element.284) | copy-start | bytes 6291460 | tf_op jit(solution)/shard_map/while
  131.2 8.9 %copy-start = (bf16[2048,4,128]{0,2,1:T(8,128)(2,1)S(1)}, bf16[2048,4,128]{0,2,1:T(8,128)(2,1)}, u32[]{:S(2)}) copy-start(bf16[2048,4,128]{0,2,1:T(8,128)(2,1)} %get-tuple-element.284) | copy-start | bytes 6291460 | tf_op jit(solution)/shard_map/while
Sparse Core Ops, SparseCore 0:
  9.5 43.9 all-gather.4
  55.7 40.2 all-gather.2
where the time goes:
time: 177 us
  waiting for transfers between devices  66.6 us (38%)
  matrix products  37.9 us (21%)
  other arithmetic  24.7 us (14%)
  blocking collectives  16.8 us (9%)
  between operations  14.2 us (8%)
  local copies, waits for them, and re-layouts  12 us (7%)
  starting transfers between devices  4.24 us (2%)
    all_gather x1, waiting for transfers between devices, shards(): key_rows = lax.all_gather(prefix_keys, 'outer', axis=0, tiled=True)  42.5 us
    dot_general x3, matrix products, absorb(): jnp.einsum('tkgd,nkd->tkgn', queries, key_rows, preferred_element_type=jn...  19.1 us
    reduce_sum x3, other arithmetic, absorb(): running_sum = running_sum * decay_factor + jnp.sum(weights, axis=-1)  18.1 us
    dot_general x3, matrix products, absorb(): jnp.einsum('tkgn,nkd->tkgd', weights.astype(jnp.bfloat16), value_rows, pr...  17.3 us
    all_to_all x1, blocking collectives, shards(): lax.all_to_all(outputs, 'inner', split_axis=0, concat_axis=1, tiled=True)  16.8 us
    all_to_all x1, waiting for transfers between devices, shards(): lax.all_to_all(qkv, 'inner', split_axis=1, concat_axis=0, tiled=True)  14.2 us
    all_gather x1, waiting for transfers between devices, shards(): value_rows = lax.all_gather(prefix_values, 'outer', axis=0, tiled=True)  9.91 us
    unnamed x11, local copies, waits for them, and re-layouts  5.31 us
  transfers between devices with their start and end apart: 3, of which 3 were waited for; matrix products, arithmetic and copies ran while one was open for 8% of the time, Pallas kernels for 0%

commit v1 on v0

--- a/solution.py
+++ b/solution.py
@@ -1,11 +1,420 @@
+import functools
 import math
 
 import jax
 import jax.numpy as jnp
+import numpy as np
 from jax import lax
+from jax.experimental import pallas as pl
+from jax.experimental.pallas import tpu as pltpu
 from jax.sharding import PartitionSpec as P
 
 rope_base = 500000.0
+axes = ("outer", "inner")
+bf16 = jnp.bfloat16
+f32 = jnp.float32
+
+
+def frequencies(head_dim):
+    ladder = np.arange(head_dim // 2, dtype=np.float32)
+    return np.exp(ladder * np.float32(-2.0 * math.log(rope_base) / head_dim)).astype(np.float32)
+
+
+def angle_table(positions, head_dim):
+    return frequencies(head_dim)[:, None] * positions.astype(np.float32)[None, :]
+
+
+def whole(memory=pltpu.VMEM):
+    return pl.BlockSpec(memory_space=memory)
+
+
+def params(megabytes=48):
+    return pltpu.CompilerParams(vmem_limit_bytes=megabytes * 2**20)
+
+
+def pack_prefix(place, ids, codes, values, scales, half):
+    rows, kv_local, groups = codes.shape
+    head_dim = values.shape[-1]
+    extent = half * (rows + groups)
+
+    def kernel(place, ids, codes, values, scales, keep, send):
+        core = place[0]
+        block = jnp.full((16, head_dim), ids[0], jnp.int32).astype(f32).astype(bf16)
+        lane = lax.broadcasted_iota(jnp.int32, scales.shape, 1)
+        factors = scales[...]
+        for target, which in ((send, 1 - core), (keep, core)):
+            for k in range(half):
+                head = which * half + k
+                factor = jnp.sum(jnp.where(lane == head, factors, 0.0), axis=1, keepdims=True)
+                target[k * rows : (k + 1) * rows, :] = (values[head].astype(f32) * factor).astype(bf16)
+                first = half * rows + k * groups
+                target[first : first + groups, :] = codes[head].astype(f32).astype(bf16)
+        send[extent:, :] = block
+
+    return pl.pallas_call(
+        kernel,
+        out_shape=(
+            jax.ShapeDtypeStruct((extent, head_dim), bf16),
+            jax.ShapeDtypeStruct((extent + 16, head_dim), bf16),
+        ),
+        in_specs=[whole(pltpu.SMEM), whole(pltpu.SMEM), whole(), whole(), whole()],
+        out_specs=(whole(), whole()),
+        compiler_params=params(),
+        name="pack_prefix",
+    )(place, ids, codes.transpose(1, 2, 0), values.transpose(1, 0, 2), scales)
+
+
+def rotate_stretch(heads, cosine, sine, qkv, half_heads):
+    tokens, _, slots, head_dim = qkv.shape
+    group = slots - 2
+    rows = tokens * group + 2 * tokens
+
+    def kernel(heads, cosine, sine, qkv, keep, send):
+        step = pl.program_id(0)
+        cos, sin = cosine[...], sine[...]
+        q = qkv[:, 0, :group, :].astype(f32)
+        turned = q * cos[:, None, :] + pltpu.roll(q, head_dim // 2, 2) * sin[:, None, :]
+        turned = turned.reshape(tokens * group, head_dim).astype(bf16)
+        key = qkv[:, 0, group, :].astype(f32)
+        key = (key * cos + pltpu.roll(key, head_dim // 2, 1) * sin).astype(bf16)
+        value = qkv[:, 0, group + 1, :]
+
+        def put(target):
+            target[0, : tokens * group, :] = turned
+            target[0, tokens * group : tokens * (group + 1), :] = key
+            target[0, tokens * (group + 1) :, :] = value
+
+        @pl.when(step < half_heads)
+        def _():
+            put(send)
+
+        @pl.when(step >= half_heads)
+        def _():
+            put(keep)
+
+    shape = jax.ShapeDtypeStruct((half_heads, rows, head_dim), bf16)
+    return pl.pallas_call(
+        kernel,
+        out_shape=(shape, shape),
+        grid_spec=pltpu.PrefetchScalarGridSpec(
+            num_scalar_prefetch=1,
+            grid=(2 * half_heads,),
+            in_specs=[
+                pl.BlockSpec((tokens, head_dim), lambda i, h: (0, 0)),
+                pl.BlockSpec((tokens, head_dim), lambda i, h: (0, 0)),
+                pl.BlockSpec((tokens, 1, slots, head_dim), lambda i, h: (0, h[i], 0, 0)),
+            ],
+            out_specs=[
+                pl.BlockSpec((1, rows, head_dim), lambda i, h: (jnp.maximum(i - half_heads, 0), 0, 0)),
+                pl.BlockSpec((1, rows, head_dim), lambda i, h: (jnp.minimum(i, half_heads - 1), 0, 0)),
+            ],
+        ),
+        compiler_params=params(),
+        name="rotate_stretch",
+    )(heads, cosine, sine, qkv)
+
+
+def attend(place, pieces, tables, book, queries, stretch, state, heads, sizes, final):
+    half, rows, groups, tokens, group, head_dim, codes = sizes
+    n_blocks = sum(len(blocks) for _, blocks in pieces)
+    length = n_blocks * rows
+    q_rows = tokens * group
+    all_rows = 2 * q_rows
+    tile = min(256, q_rows)
+    scale = head_dim**-0.5 * math.log2(math.e)
+    n_pieces = len(pieces)
+    gd = head_dim // groups
+    half_dim = head_dim // 2
+    book_array, book_start = book
+
+    operands = [a for a, _ in pieces] + list(tables) + [book_array, queries[0], queries[1]]
+    if stretch is not None:
+        operands.append(stretch[0])
+    n_plain = len(operands) + 1
+    if state is not None:
+        operands += list(state)
+
+    def kernel(place, *refs):
+        refs = list(refs)
+        piece_refs = [refs.pop(0) for _ in range(n_pieces)]
+        cos_tok, sin_tok, cos_blk, sin_blk = [refs.pop(0) for _ in range(4)]
+        book_ref, q0, q1 = [refs.pop(0) for _ in range(3)]
+        other = refs.pop(0) if stretch is not None else None
+        before = [refs.pop(0) for _ in range(3)] if state is not None else None
+        if final:
+            outs = refs.pop(0)
+            after = None
+        else:
+            after = [refs.pop(0) for _ in range(3)]
+        kt, vv, tab = [refs.pop(0) for _ in range(3)]
+        core, inner = place[0], place[1]
+
+        for k in range(half):
+            if book_start is None:
+                entries = book_ref[core * half + k]
+            else:
+                entries = book_ref[book_start + k * codes : book_start + (k + 1) * codes, :]
+            tab[k] = entries.astype(f32).T
+
+        index = 0
+        for ref, (_, blocks) in zip(piece_refs, pieces):
+            for value_row, code_row, id_row in blocks:
+                block = ref[id_row - id_row % 16 : id_row - id_row % 16 + 16, :].astype(f32)
+                block = block[id_row % 16 : id_row % 16 + 8].astype(jnp.int32)
+                block = jnp.broadcast_to(block[None], (half_dim // 8, 8, head_dim)).reshape(half_dim, head_dim)
+                cb = jnp.take_along_axis(cos_blk[...], block, axis=1, mode="promise_in_bounds")
+                sb = jnp.take_along_axis(sin_blk[...], block, axis=1, mode="promise_in_bounds")
+                ct, st = cos_tok[...], sin_tok[...]
+                cos = cb * ct - sb * st
+                sin = sb * ct + cb * st
+                for k in range(half):
+                    code = ref[code_row + k * groups : code_row + (k + 1) * groups, :].astype(f32).astype(jnp.int32)
+                    code = jnp.broadcast_to(code[:, None, :], (groups, gd, rows)).reshape(head_dim, rows)
+                    low = code & 127
+                    key = jnp.take_along_axis(tab[k, :, :128], low, axis=1, mode="promise_in_bounds")
+                    for part in range(1, codes // 128):
+                        more = jnp.take_along_axis(tab[k, :, part * 128 : (part + 1) * 128], low, axis=1, mode="promise_in_bounds")
+                        key = jnp.where(code >= part * 128, more, key)
+                    a, b = key[:half_dim], key[half_dim:]
+                    key = jnp.concatenate([a * cos - b * sin, b * cos + a * sin], axis=0).astype(bf16)
+                    span = slice(index * rows, (index + 1) * rows)
+                    kt[k, :head_dim, span] = key
+                    kt[k, head_dim:, span] = key
+                    vv[k, span, :] = ref[value_row + k * rows : value_row + (k + 1) * rows, :]
+                index += 1
+
+        def soft(score, m, l, total, value):
+            new_m = jnp.maximum(m, jnp.max(score, axis=1, keepdims=True))
+            weight = jnp.exp2(score - new_m)
+            part = weight[:, :128]
+            for i in range(1, weight.shape[1] // 128):
+                part = part + weight[:, i * 128 : (i + 1) * 128]
+            mixed = jnp.dot(weight.astype(bf16), value, preferred_element_type=f32)
+            if m is None:
+                return new_m, part, mixed
+            decay = jnp.exp2(m - new_m)
+            return new_m, l * decay + part, total * decay + mixed
+
+        per_head = q_rows // tile
+
+        def body(which, query, i):
+            k = i // per_head
+            rr = pl.multiple_of((i % per_head) * tile, tile)
+            out_row = pl.multiple_of(which * q_rows + rr, tile)
+            hk = heads[0] + k
+            q = query[hk, pl.ds(rr, tile), :]
+            scaled = q.astype(f32) * scale
+            hi = scaled.astype(bf16)
+            lo = (scaled - hi.astype(f32)).astype(bf16)
+            q = jnp.concatenate([hi, lo], axis=1)
+            if before is not None:
+                at = (k, pl.ds(out_row, tile), slice(None))
+                m, l, total = before[0][at][:, :1], before[1][at], before[2][at]
+            else:
+                m = jnp.full((tile, 1), -1e30, f32)
+                l = jnp.zeros((tile, 128), f32)
+                total = jnp.zeros((tile, head_dim), f32)
+            score = jnp.dot(q, kt[k], preferred_element_type=f32)
+            m, l, total = soft(score, m, l, total, vv[k])
+            if stretch is not None:
+                first, per = stretch[1], 2 * tokens
+                mate = (heads[0] + half) % (2 * half)
+                base = pl.multiple_of(first + (which * 2 * half + mate + k) * per, 2 * tokens)
+                key_other = other[pl.ds(base, tokens), :]
+                value_other = other[pl.ds(base + tokens, tokens), :]
+                key_own = query[hk, q_rows : q_rows + tokens, :]
+                value_own = query[hk, q_rows + tokens :, :]
+                key = jnp.concatenate([key_other, key_own], axis=0)
+                key = jnp.concatenate([key, key], axis=1)
+                value = jnp.concatenate([value_other, value_own], axis=0)
+                score = lax.dot_general(q, key, (((1,), (1,)), ((), ())), preferred_element_type=f32)
+                column = lax.broadcasted_iota(jnp.int32, score.shape, 1)
+                row = (lax.broadcasted_iota(jnp.int32, score.shape, 0) + rr) // group
+                allowed = (column - tokens <= row) & (column >= tokens * (1 - inner))
+                score = jnp.where(allowed, score, -jnp.inf)
+                m, l, total = soft(score, m, l, total, value)
+            at = (k, pl.ds(out_row, tile), slice(None))
+            if final:
+                denominator = jnp.sum(l, axis=1, keepdims=True)
+                outs[at] = (total / denominator).astype(bf16)
+            else:
+                after[0][at] = jnp.broadcast_to(m, (tile, 128))
+                after[1][at] = l
+                after[2][at] = total
+
+        for which, query in enumerate((q0, q1)):
+
+            @pl.loop(0, half * per_head)
+            def _(i, which=which, query=query):
+                body(which, query, i)
+
+    wide = jax.ShapeDtypeStruct((half, all_rows, 128), f32)
+    if final:
+        out_shape = jax.ShapeDtypeStruct((half, all_rows, head_dim), bf16)
+        out_specs = whole()
+        alias = {}
+    else:
+        out_shape = (wide, wide, wide)
+        out_specs = (whole(),) * 3
+        alias = {n_plain + j: j for j in range(3)} if state is not None else {}
+    flops = 4 * half * all_rows * length * head_dim
+    return pl.pallas_call(
+        kernel,
+        out_shape=out_shape,
+        in_specs=[whole(pltpu.SMEM)] + [whole() for _ in operands],
+        out_specs=out_specs,
+        scratch_shapes=[
+            pltpu.VMEM((half, 2 * head_dim, length), bf16),
+            pltpu.VMEM((half, length, head_dim), bf16),
+            pltpu.VMEM((half, head_dim, codes), f32),
+        ],
+        input_output_aliases=alias,
+        compiler_params=params(),
+        cost_estimate=pl.CostEstimate(
+            flops=2 * flops, bytes_accessed=4 * 2**20, transcendentals=half * all_rows * length
+        ),
+        name="attend",
+    )(place, *operands)
+
+
+def lay_out(heads, own, received, tokens, group):
+    arrays = [a for a, _ in own] + [a for a, _ in received]
+    half = arrays[0].shape[0]
+    head_dim = arrays[0].shape[2]
+    n_heads = half * len(arrays)
+    q_rows = tokens * group
+    blocks = [b for _, b in own] + [b for _, b in received]
+
+    def kernel(heads, *refs):
+        step = pl.program_id(0)
+        out = refs[-1]
+        for j, ref in enumerate(refs[:-1]):
+
+            @pl.when(step // half == j)
+            def _(ref=ref):
+                out[:, 0, :, :] = ref[0].reshape(tokens, group, head_dim)
+
+    def pick(j, block):
+        return lambda i, h: (jnp.clip(i - j * half, 0, half - 1), block, 0)
+
+    return pl.pallas_call(
+        kernel,
+        out_shape=jax.ShapeDtypeStruct((tokens, n_heads, group, head_dim), bf16),
+        grid_spec=pltpu.PrefetchScalarGridSpec(
+            num_scalar_prefetch=1,
+            grid=(n_heads,),
+            in_specs=[pl.BlockSpec((1, q_rows, head_dim), pick(j, b)) for j, b in enumerate(blocks)],
+            out_specs=pl.BlockSpec((tokens, 1, group, head_dim), lambda i, h: (0, h[i], 0, 0)),
+        ),
+        compiler_params=params(),
+        name="lay_out",
+    )(heads, *arrays)
+
+
+def paired(qkv, key_codes, codebooks, value_codes, value_scales, block_ids, *, n_outer):
+    tokens, n_heads, slots, head_dim = qkv.shape
+    group = slots - 2
+    rows, kv_local, groups = key_codes.shape
+    codes = codebooks.shape[1]
+    half = kv_local // 2
+    n_far = n_outer // 4
+    prefix = rows * n_outer
+    outer, inner = lax.axis_index("outer"), lax.axis_index("inner")
+    core = outer % 2
+    place = jnp.stack([core, inner]).astype(jnp.int32)
+    extent = half * (rows + groups)
+
+    def swap(x, outer_bits, inner_bits=0):
+        return lax.ppermute(
+            x,
+            axes,
+            [
+                (2 * o + i, 2 * (o ^ outer_bits) + (i ^ inner_bits))
+                for o in range(n_outer)
+                for i in range(2)
+            ],
+        )
+
+    keep, send = pack_prefix(place, block_ids, key_codes, value_codes, value_scales, half)
+    mate = swap(send, 1)
+
+    own_first = jnp.stack([inner, 1 - inner]).astype(jnp.int32)
+
+    def order(which):
+        return (own_first[:, None] * kv_local + which * half + jnp.arange(half)[None, :]).reshape(-1).astype(jnp.int32)
+
+    cosine = np.cos(angle_table(np.arange(2 * tokens) + prefix, head_dim)).T
+    sine = np.sin(angle_table(np.arange(2 * tokens) + prefix, head_dim)).T
+    cosine = jnp.asarray(np.concatenate([cosine, cosine], axis=1))
+    sine = jnp.asarray(np.concatenate([-sine, sine], axis=1))
+    cosine = lax.dynamic_slice_in_dim(cosine, inner * tokens, tokens, 0)
+    sine = lax.dynamic_slice_in_dim(sine, inner * tokens, tokens, 0)
+    q_keep, q_send = rotate_stretch(
+        jnp.concatenate([order(1 - core), order(core)]), cosine, sine, qkv, 2 * half
+    )
+    q_mate = swap(q_send, 1)
+
+    own_id = jnp.full((8, head_dim), block_ids[0].astype(bf16))
+    pack = jnp.concatenate([keep, mate[:extent], own_id, mate[extent + 8 :]], axis=0)
+    size = pack.shape[0]
+
+    def blocks_of(base, count=1):
+        out = []
+        for j in range(count):
+            b = base + j * size
+            out.append((b, b + half * rows, b + 2 * extent))
+            out.append((b + extent, b + extent + half * rows, b + 2 * extent + 8))
+        return out
+
+    def far(x):
+        return [swap(x, 4 * j) for j in range(1, n_far)]
+
+    z_packs = far(pack)
+    diag = swap(pack, 2, 1)
+    x_pack = swap(pack, 2)
+    my_books = lax.dynamic_slice_in_dim(codebooks, core * half, half, 0).reshape(half * codes, head_dim)
+    q_rows = tokens * group
+    kv_own = jnp.concatenate([q_keep[:, q_rows:], q_mate[:, q_rows:]], axis=0).reshape(-1, head_dim)
+    y_send = jnp.concatenate([pack, my_books, kv_own], axis=0)
+    y_pack = swap(y_send, 0, 1)
+    book_row = size
+    stretch_row = size + half * codes
+
+    z_all = jnp.concatenate(z_packs, axis=0)
+    y_far = swap(z_all, 0, 1)
+    diag_far = far(diag)
+    x_far = swap(z_all, 2)
+
+    positions = np.arange(rows)
+    cos_tok, sin_tok = np.cos(angle_table(positions, head_dim)), np.sin(angle_table(positions, head_dim))
+    starts = np.arange(128) * rows
+    cos_blk, sin_blk = np.cos(angle_table(starts, head_dim)), np.sin(angle_table(starts, head_dim))
+    tables = [jnp.asarray(t.astype(np.float32)) for t in (cos_tok, sin_tok, cos_blk, sin_blk)]
+    sizes = (half, rows, groups, tokens, group, head_dim, codes)
+    queries = (q_keep, q_mate)
+    call = functools.partial(attend, place, tables=tables, queries=queries, sizes=sizes)
+
+    one = blocks_of(0)
+    many = blocks_of(0, n_far - 1)
+    own_state = call(
+        [(pack, one)] + [(p, one) for p in z_packs] + [(x_pack, one)],
+        book=(codebooks, None), stretch=(y_pack, stretch_row), state=None, heads=(0,), final=False,
+    )
+    own_out = call([(x_far, many)], book=(codebooks, None), stretch=None, state=own_state, heads=(0,), final=True)
+    own_mate = swap(own_out[:, q_rows:], 1)
+    other_state = call(
+        [(y_pack, one), (diag, one)] + [(p, one) for p in diag_far],
+        book=(y_pack, book_row), stretch=(y_pack, stretch_row), state=None, heads=(half,), final=False,
+    )
+    other_out = call([(y_far, many)], book=(y_pack, book_row), stretch=None, state=other_state, heads=(half,), final=True)
+    other_mate = swap(other_out[:, q_rows:], 1)
+    return lay_out(
+        jnp.concatenate([order(core), order(1 - core)]),
+        [(own_out, 0), (other_out, 0)],
+        [(own_mate, 0), (other_mate, 0)],
+        tokens,
+        group,
+    )
 
 
 def rotate(tensor, position):
@@ -110,8 +519,33 @@
 
 
 def solution(mesh):
+    n_outer, n_inner = mesh.shape["outer"], mesh.shape["inner"]
+
+    def body(qkv, key_codes, codebooks, value_codes, value_scales, block_ids):
+        arrays = (qkv, key_codes, codebooks, value_codes, value_scales, block_ids)
+        head_dim = qkv.shape[3]
+        far = n_outer // 4
+        fits = (
+            n_inner == 2
+            and n_outer % 4 == 0
+            and 1 < far
+            and far & (far - 1) == 0
+            and n_outer <= 128
+            and key_codes.shape[1] % 2 == 0
+            and key_codes.shape[0] == 128
+            and head_dim == 128
+            and head_dim // key_codes.shape[2] == 8
+            and key_codes.shape[2] % 16 == 0
+            and codebooks.shape[1] % 128 == 0
+            and qkv.shape[2] == 10
+            and qkv.shape[0] % 32 == 0
+        )
+        if fits:
+            return paired(*arrays, n_outer=n_outer)
+        return shards(*arrays)
+
     return jax.shard_map(
-        shards,
+        body,
         mesh=mesh,
         in_specs=(
             P(("outer", "inner"), None, None, None),

time: 177 us -> 90.3 us (0.51)
  waiting for transfers between devices: 66.6 us -> 21.9 us
  Pallas kernels: 0 us -> 41.4 us
  matrix products: 37.9 us -> 0 us
  other arithmetic: 24.7 us -> 0.41 us
  blocking collectives: 16.8 us -> 0 us
  starting transfers between devices: 4.24 us -> 20.4 us
  between operations: 14.2 us -> 0.95 us
  local copies, waits for them, and re-layouts: 12 us -> 4.81 us
    all_gather x2 -> x0, waiting for transfers between devices: 52.4 us -> none  [the longest x1 42.5 us: shards(): key_rows = lax.all_gather(prefix_keys, 'outer', axis=0, tiled=True)]
    pallas_call x0 -> x7, Pallas kernels: none -> 41.4 us  [the longest x4 33.6 us: attend(): pl.pallas_call(kernel, out_shape=out_shape, in_specs=[whole(pltpu.SMEM)]...]
    dot_general x7 -> x0, matrix products: 37.9 us -> none  [the longest x3 19.1 us: absorb(): jnp.einsum('tkgd,nkd->tkgn', queries, key_rows, preferred_element_type=jn...]
    ppermute x0 -> x15, waiting for transfers between devices: none -> 21.9 us  [swap(): lax.ppermute(x, axes, [(2 * o + i, 2 * (o ^ outer_bits) + (i ^ inner_bits...]
    ppermute x0 -> x15, starting transfers between devices: none -> 20.4 us  [swap(): lax.ppermute(x, axes, [(2 * o + i, 2 * (o ^ outer_bits) + (i ^ inner_bits...]
    reduce_sum x3 -> x0, other arithmetic: 18.1 us -> none  [absorb(): running_sum = running_sum * decay_factor + jnp.sum(weights, axis=-1)]
    all_to_all x1 -> x0, blocking collectives: 16.8 us -> none  [shards(): lax.all_to_all(outputs, 'inner', split_axis=0, concat_axis=1, tiled=True)]
    all_to_all x1 -> x0, waiting for transfers between devices: 14.2 us -> none  [shards(): lax.all_to_all(qkv, 'inner', split_axis=1, concat_axis=0, tiled=True)]
  transfers between devices with their start and end apart: 3 -> 15, of which waited for: 3 -> 4; matrix products, arithmetic and copies ran while one was open for 8% -> 3% of each run, Pallas kernels for 0% -> 42%
where the time goes in v1:
time: 90.3 us; the launch traced here: 90 us
  Pallas kernels  41.4 us (46%)
  waiting for transfers between devices  21.9 us (24%)
  starting transfers between devices  20.4 us (23%)
  local copies, waits for them, and re-layouts  4.81 us (5%)
  between operations  0.95 us (1%)
    pallas_call x4, Pallas kernels, attend(): pl.pallas_call(kernel, out_shape=out_shape, in_specs=[whole(pltpu.SMEM)]...  33.6 us
    ppermute x15, waiting for transfers between devices, swap(): lax.ppermute(x, axes, [(2 * o + i, 2 * (o ^ outer_bits) + (i ^ inner_bits...  21.9 us
    ppermute x15, starting transfers between devices, swap(): lax.ppermute(x, axes, [(2 * o + i, 2 * (o ^ outer_bits) + (i ^ inner_bits...  20.4 us
    unnamed x26, local copies, waits for them, and re-layouts  4.5 us
    pallas_call x1, Pallas kernels, rotate_stretch(): pl.pallas_call(kernel, out_shape=(shape, shape), grid_spec=pltpu.Prefetch...  3.89 us
    pallas_call x1, Pallas kernels, lay_out(): pl.pallas_call(kernel, out_shape=jax.ShapeDtypeStruct((tokens, n_heads, g...  3.31 us
  transfers between devices with their start and end apart: 15, of which 4 were waited for; matrix products, arithmetic and copies ran while one was open for 3% of the time, Pallas kernels for 42%

profile of v1, /device:TPU:0, one launch (start us, length us, event | category | flops | bytes accessed | tf_op | source)
XLA Modules:
  0.0 90.0 jit_solution(7849270862707636587)
XLA Ops:
  0.0 0.0 copy-start.6
  0.0 0.0 copy-start.7
  0.7 0.9 %copy.17 = bf16[128,4,128]{2,0,1:T(8,128)(2,1)S(1)} copy(bf16[128,4,128]{2,1,0:T(4,128)(2,1)} %param.15) | data formatting | bytes 262144 | tf_op args[3]
  1.6 0.8 copy.14.scales
  2.4 0.1 pad_add_fusion.1.place
  2.5 0.0 copy-start.5
  2.5 0.8 copy-done.5
  3.2 0.7 pack_prefix.1
  3.9 0.5 collective-permute-start
  4.5 0.1 broadcast_add_fusion
  4.5 0.1 iota_add_fusion.1
  4.6 0.1 add.91
  4.7 0.1 iota_add_fusion
  4.8 0.1 add.97
  4.9 1.9 %copy.15.qkv = bf16[64,8,10,128]{3,2,1,0:T(8,128)(2,1)S(1)} copy(bf16[64,8,10,128]{3,1,2,0:T(8,128)(2,1)} %param.12) | data formatting | bytes 2621440 | tf_op args[0]
  6.8 0.0 copy-start
  6.8 0.1 pad_add_fusion.2
  6.8 0.0 copy-done.6
  6.8 0.0 copy-done.7
  6.9 3.9 %rotate_stretch.1 = (bf16[4,640,128]{2,1,0:T(8,128)(2,1)S(1)}, bf16[4,640,128]{2,1,0:T(8,128)(2,1)}) custom-call(s32[8]{0:T(128)S(1)} %get-tuple-element.29.heads, f32[64,128]{1,0:T(8,128)S(1)} %get-tuple-element.34.cosine, f32[64,128]{1,0:T(8,128)S(1)} %get-tuple-element.33.sine, bf16[64,8,10,128]{3,2,1,0:T(8,128)(2,1)S(1)} %copy.15.qkv), custom_call_target="tpu_custom_call" | custom-call | tf_op jit(solution)/shard_map/rotate_stretch/pallas_call | solution.py:96
  10.8 0.0 copy-start.1
  10.8 0.0 copy-start.2
  10.8 0.0 copy-start.3
  10.8 0.0 copy-start.4
  10.8 0.1 collective-permute-start.5
  10.9 0.0 copy-done
  11.0 0.0 collective-permute-done
  11.1 3.1 %collective-permute-start.1 = (bf16[592,128]{1,0:T(8,128)(2,1)S(1)}, bf16[592,128]{1,0:T(8,128)(2,1)S(1)}, u32[]{:S(2)}, u32[]{:S(2)}) collective-permute-start(bf16[592,128]{1,0:T(8,128)(2,1)S(1)} %pad_maximum_fusion.1.refs_0_), channel_id=1, source_target_pairs={{0,8},{1,9},{2,10},{3,11},{4,12},{5,13},{6,14},{7,15},{8,0},{9,1},... | collective-permute-start | bytes 454664 | tf_op jit(solution)/shard_map/ppermute | solution.py:328
  14.1 2.6 %collective-permute-start.2 = (bf16[592,128]{1,0:T(8,128)(2,1)S(1)}, bf16[592,128]{1,0:T(8,128)(2,1)S(1)}, u32[]{:S(2)}, u32[]{:S(2)}) collective-permute-start(bf16[592,128]{1,0:T(8,128)(2,1)S(1)} %pad_maximum_fusion.1.refs_0_), channel_id=1, source_target_pairs={{0,16},{1,17},{2,18},{3,19},{4,20},{5,21},{6,22},{7,23},{8,24},{9,... | collective-permute-start | bytes 454664 | tf_op jit(solution)/shard_map/ppermute | solution.py:328
  16.7 0.0 collective-permute-start.3
  16.8 0.0 collective-permute-done.5.refs_11_.refs_7_
  16.9 1.8 %collective-permute-start.7 = (bf16[2128,128]{1,0:T(8,128)(2,1)S(1)}, bf16[2128,128]{1,0:T(8,128)(2,1)S(1)}, u32[]{:S(2)}, u32[]{:S(2)}) collective-permute-start(bf16[2128,128]{1,0:T(8,128)(2,1)S(1)} %constant_dynamic-update-slice_fusion.3), channel_id=1, source_target_pairs={{0,1},{1,0},{2,3},{3,2},{4,5},{5,4},{6,7},{7,6},{8,9},{9,8},{10,11... | collective-permute-start | bytes 1634312 | tf_op jit(solution)/shard_map/ppermute | solution.py:328
  18.7 2.0 %collective-permute-done.1.refs_1_ = bf16[592,128]{1,0:T(8,128)(2,1)S(1)} collective-permute-done((bf16[592,128]{1,0:T(8,128)(2,1)S(1)}, bf16[592,128]{1,0:T(8,128)(2,1)S(1)}, u32[]{:S(2)}, u32[]{:S(2)}) %collective-permute-start.1) | collective-permute-done | bytes 151584 | tf_op jit(solution)/shard_map/ppermute | solution.py:328
  20.6 7.7 %collective-permute-done.2.refs_2_ = bf16[592,128]{1,0:T(8,128)(2,1)S(1)} collective-permute-done((bf16[592,128]{1,0:T(8,128)(2,1)S(1)}, bf16[592,128]{1,0:T(8,128)(2,1)S(1)}, u32[]{:S(2)}, u32[]{:S(2)}) %collective-permute-start.2) | collective-permute-done | bytes 151584 | tf_op jit(solution)/shard_map/ppermute | solution.py:328
  28.4 0.0 collective-permute-done.3.refs_3_
  28.4 1.6 %collective-permute-start.4 = (bf16[1776,128]{1,0:T(8,128)(2,1)S(1)}, bf16[1776,128]{1,0:T(8,128)(2,1)S(1)}, u32[]{:S(2)}, u32[]{:S(2)}) collective-permute-start(bf16[1776,128]{1,0:T(8,128)(2,1)S(1)} %constant_dynamic-update-slice_fusion), channel_id=1, source_target_pairs={{0,4},{1,5},{2,6},{3,7},{4,0},{5,1},{6,2},{7,3},{8,12},{9,13},{10,... | collective-permute-start | bytes 1363976 | tf_op jit(solution)/shard_map/ppermute | solution.py:328
  30.0 1.5 %collective-permute-start.9 = (bf16[592,128]{1,0:T(8,128)(2,1)S(1)}, bf16[592,128]{1,0:T(8,128)(2,1)S(1)}, u32[]{:S(2)}, u32[]{:S(2)}) collective-permute-start(bf16[592,128]{1,0:T(8,128)(2,1)S(1)} %pad_maximum_fusion.1.refs_0_), channel_id=1, source_target_pairs={{0,5},{1,4},{2,7},{3,6},{4,1},{5,0},{6,3},{7,2},{8,13},{9,12},{10,... | collective-permute-start | bytes 454664 | tf_op jit(solution)/shard_map/ppermute | solution.py:328
  31.5 1.5 %collective-permute-start.6 = (bf16[592,128]{1,0:T(8,128)(2,1)S(1)}, bf16[592,128]{1,0:T(8,128)(2,1)S(1)}, u32[]{:S(2)}, u32[]{:S(2)}) collective-permute-start(bf16[592,128]{1,0:T(8,128)(2,1)S(1)} %pad_maximum_fusion.1.refs_0_), channel_id=1, source_target_pairs={{0,4},{1,5},{2,6},{3,7},{4,0},{5,1},{6,2},{7,3},{8,12},{9,13},{10,... | collective-permute-start | bytes 454664 | tf_op jit(solution)/shard_map/ppermute | solution.py:328
  33.0 0.5 collective-permute-start.8
  33.5 11.1 %collective-permute-done.9.refs_1_ = bf16[592,128]{1,0:T(8,128)(2,1)S(1)} collective-permute-done((bf16[592,128]{1,0:T(8,128)(2,1)S(1)}, bf16[592,128]{1,0:T(8,128)(2,1)S(1)}, u32[]{:S(2)}, u32[]{:S(2)}) %collective-permute-start.9) | collective-permute-done | bytes 151584 | tf_op jit(solution)/shard_map/ppermute | solution.py:328
  44.6 3.7 %collective-permute-start.10 = (bf16[592,128]{1,0:T(8,128)(2,1)S(1)}, bf16[592,128]{1,0:T(8,128)(2,1)S(1)}, u32[]{:S(2)}, u32[]{:S(2)}) collective-permute-start(bf16[592,128]{1,0:T(8,128)(2,1)S(1)} %collective-permute-done.9.refs_1_), channel_id=1, source_target_pairs={{0,8},{1,9},{2,10},{3,11},{4,12},{5,13},{6,14},{7,15},{8,0},{9,1},... | collective-permute-start | bytes 454664 | tf_op jit(solution)/shard_map/ppermute | solution.py:328
  48.3 0.0 collective-permute-done.6.refs_4_
  48.3 1.7 %collective-permute-start.11 = (bf16[592,128]{1,0:T(8,128)(2,1)S(1)}, bf16[592,128]{1,0:T(8,128)(2,1)S(1)}, u32[]{:S(2)}, u32[]{:S(2)}) collective-permute-start(bf16[592,128]{1,0:T(8,128)(2,1)S(1)} %collective-permute-done.9.refs_1_), channel_id=1, source_target_pairs={{0,16},{1,17},{2,18},{3,19},{4,20},{5,21},{6,22},{7,23},{8,24},{9,... | collective-permute-start | bytes 454664 | tf_op jit(solution)/shard_map/ppermute | solution.py:328
  49.9 0.0 collective-permute-done.7.refs_12_.refs_0_.refs_9_.refs_5_
  49.9 1.3 %collective-permute-start.12 = (bf16[592,128]{1,0:T(8,128)(2,1)S(1)}, bf16[592,128]{1,0:T(8,128)(2,1)S(1)}, u32[]{:S(2)}, u32[]{:S(2)}) collective-permute-start(bf16[592,128]{1,0:T(8,128)(2,1)S(1)} %collective-permute-done.9.refs_1_), channel_id=1, source_target_pairs={{0,24},{1,25},{2,26},{3,27},{4,28},{5,29},{6,30},{7,31},{8,16},{9,... | collective-permute-start | bytes 454664 | tf_op jit(solution)/shard_map/ppermute | solution.py:328
  51.2 0.0 copy-done.1
  51.2 0.0 copy-done.2
  51.2 0.0 copy-done.3
  51.2 0.0 copy-done.4
  51.2 9.4 %attend.4 = (f32[2,1024,128]{2,1,0:T(8,128)S(1)}, f32[2,1024,128]{2,1,0:T(8,128)S(1)}, f32[2,1024,128]{2,1,0:T(8,128)S(1)}) custom-call(s32[2]{0:T(128)S(1)} %pad_add_fusion.1.place, bf16[592,128]{1,0:T(8,128)(2,1)S(1)} %pad_maximum_fusion.1.refs_0_, bf16[592,128]{1,0:T(8,128)(2,1)S(1)} %collective-permute-done.1.refs_1_, ...), custom_call_target="tpu_custom_call" | custom-call | flops 2684354560 | bytes 4194304 | tf_op jit(solution)/shard_map/attend/pallas_call | solution.py:261
  60.6 0.0 collective-permute-done.4.refs_0_
  60.6 7.4 %attend.5.refs_0_ = bf16[2,1024,128]{2,1,0:T(8,128)(2,1)S(1)} custom-call(s32[2]{0:T(128)S(1)} %pad_add_fusion.1.place, bf16[1776,128]{1,0:T(8,128)(2,1)S(1)} %collective-permute-done.4.refs_0_, f32[64,128]{1,0:T(8,128)S(1)} %copy-done.1, f32[64,128]{1,0:T(8,128)S(1)} %copy-done.2, f32[64,128]{1,0:T(8,128)S(1)} %copy-done.3, f32[64,128]{1,0:T(8,128)S(1)} %copy-done.4, ...), custom_call_target="tpu_custom_call" | custom-call | flops 1610612736 | bytes 4194304 | tf_op jit(solution)/shard_map/attend/pallas_call | solution.py:261
  68.0 0.1 collective-permute-start.13
  68.1 0.0 collective-permute-done.10.refs_2_
  68.1 0.0 collective-permute-done.11.refs_3_
  68.1 0.0 collective-permute-done.12.refs_4_
  68.1 9.4 %attend.6 = (f32[2,1024,128]{2,1,0:T(8,128)S(1)}, f32[2,1024,128]{2,1,0:T(8,128)S(1)}, f32[2,1024,128]{2,1,0:T(8,128)S(1)}) custom-call(s32[2]{0:T(128)S(1)} %pad_add_fusion.1.place, bf16[2128,128]{1,0:T(8,128)(2,1)S(1)} %collective-permute-done.7.refs_12_.refs_0_.refs_9_.refs_5_, bf16[592,128]{1,0:T(8,128)(2,1)S(1)} %collective-permute-done.9.refs_1_, ...), custom_call_target="tpu_custom_call" | custom-call | flops 2684354560 | bytes 4194304 | tf_op jit(solution)/shard_map/attend/pallas_call | solution.py:261
  77.5 0.0 collective-permute-done.8.refs_0_
  77.5 7.4 %attend.7.refs_1_ = bf16[2,1024,128]{2,1,0:T(8,128)(2,1)S(1)} custom-call(s32[2]{0:T(128)S(1)} %pad_add_fusion.1.place, bf16[1776,128]{1,0:T(8,128)(2,1)S(1)} %collective-permute-done.8.refs_0_, f32[64,128]{1,0:T(8,128)S(1)} %copy-done.1, f32[64,128]{1,0:T(8,128)S(1)} %copy-done.2, f32[64,128]{1,0:T(8,128)S(1)} %copy-done.3, f32[64,128]{1,0:T(8,128)S(1)} %copy-done.4, ...), custom_call_target="tpu_custom_call" | custom-call | flops 1610612736 | bytes 4194304 | tf_op jit(solution)/shard_map/attend/pallas_call | solution.py:261
  85.0 0.5 collective-permute-start.14
  85.5 0.0 collective-permute-done.13.refs_2_
  85.5 1.2 %collective-permute-done.14.refs_3_ = bf16[2,512,128]{2,1,0:T(8,128)(2,1)S(1)} collective-permute-done((bf16[2,512,128]{2,1,0:T(8,128)(2,1)S(1)}, bf16[2,512,128]{2,1,0:T(8,128)(2,1)S(1)}, u32[]{:S(2)}, u32[]{:S(2)}) %collective-permute-start.14) | collective-permute-done | bytes 262176 | tf_op jit(solution)/shard_map/ppermute | solution.py:328
  86.7 3.3 %lay_out.1 = bf16[64,8,8,128]{3,2,1,0:T(8,128)(2,1)} custom-call(s32[8]{0:T(128)S(1)} %get-tuple-element.30.heads, bf16[2,1024,128]{2,1,0:T(8,128)(2,1)S(1)} %attend.5.refs_0_, bf16[2,1024,128]{2,1,0:T(8,128)(2,1)S(1)} %attend.7.refs_1_, bf16[2,512,128]{2,1,0:T(8,128)(2,1)S(1)} %collective-permute-done.13.refs_2_, ...), custom_call_target="tpu_custom_call" | custom-call | tf_op jit(solution)/shard_map/lay_out/pallas_call | solution.py:300
  (18 shorter events, 0.3 us)
Async XLA Ops:
  0.0 6.8 %copy-start.6 = (f32[128,128]{1,0:T(8,128)S(1)}, f32[128,128]{1,0:T(8,128)}, u32[]{:S(2)}) copy-start(f32[128,128]{1,0:T(8,128)} %constant.43.clone) | copy-start | bytes 196612
  0.0 6.8 %copy-start.7 = (f32[128,128]{1,0:T(8,128)S(1)}, f32[128,128]{1,0:T(8,128)}, u32[]{:S(2)}) copy-start(f32[128,128]{1,0:T(8,128)} %constant.42.clone) | copy-start | bytes 196612
  2.5 0.8 copy-start.5
  3.9 7.0 %collective-permute-start = (bf16[304,128]{1,0:T(8,128)(2,1)S(1)}, bf16[304,128]{1,0:T(8,128)(2,1)S(1)}, u32[]{:S(2)}, u32[]{:S(2)}) collective-permute-start(bf16[304,128]{1,0:T(8,128)(2,1)S(1)} %get-tuple-element.16), channel_id=1, source_target_pairs={{0,2},{1,3},{2,0},{3,1},{4,6},{5,7},{6,4},{7,5},{8,10},{9,11},{10,... | collective-permute-start | bytes 233480 | tf_op jit(solution)/shard_map/ppermute | solution.py:328
  6.8 4.2 %copy-start = (bf16[4,256,128]{2,1,0:T(8,128)(2,1)S(1)}, bf16[4,256,128]{2,1,0:T(8,128)(2,1)}, u32[]{:S(2)}) copy-start(bf16[4,256,128]{2,1,0:T(8,128)(2,1)} %refs_5_.3) | copy-start | bytes 786436
  10.8 40.4 %copy-start.1 = (f32[64,128]{1,0:T(8,128)S(1)}, f32[64,128]{1,0:T(8,128)}, u32[]{:S(2)}) copy-start(f32[64,128]{1,0:T(8,128)} %constant.44.clone.refs_5_.refs_1_) | copy-start | bytes 98308
  10.8 40.4 %copy-start.2 = (f32[64,128]{1,0:T(8,128)S(1)}, f32[64,128]{1,0:T(8,128)}, u32[]{:S(2)}) copy-start(f32[64,128]{1,0:T(8,128)} %constant.45.clone.refs_6_.refs_2_) | copy-start | bytes 98308
  10.8 40.4 %copy-start.3 = (f32[64,128]{1,0:T(8,128)S(1)}, f32[64,128]{1,0:T(8,128)}, u32[]{:S(2)}) copy-start(f32[64,128]{1,0:T(8,128)} %constant.46.clone.refs_7_.refs_3_) | copy-start | bytes 98308
  10.8 40.4 %copy-start.4 = (f32[64,128]{1,0:T(8,128)S(1)}, f32[64,128]{1,0:T(8,128)}, u32[]{:S(2)}) copy-start(f32[64,128]{1,0:T(8,128)} %constant.47.clone.refs_8_.refs_4_) | copy-start | bytes 98308
  10.8 6.0 %collective-permute-start.5 = (bf16[4,640,128]{2,1,0:T(8,128)(2,1)}, bf16[4,640,128]{2,1,0:T(8,128)(2,1)S(1)}, u32[]{:S(2)}, u32[]{:S(2)}) collective-permute-start(bf16[4,640,128]{2,1,0:T(8,128)(2,1)} %get-tuple-element.18), channel_id=1, source_target_pairs={{0,2},{1,3},{2,0},{3,1},{4,6},{5,7},{6,4},{7,5},{8,10},{9,11},{10,... | collective-permute-start | bytes 1966088 | tf_op jit(solution)/shard_map/ppermute | solution.py:328
  11.1 9.6 %collective-permute-start.1 = (bf16[592,128]{1,0:T(8,128)(2,1)S(1)}, bf16[592,128]{1,0:T(8,128)(2,1)S(1)}, u32[]{:S(2)}, u32[]{:S(2)}) collective-permute-start(bf16[592,128]{1,0:T(8,128)(2,1)S(1)} %pad_maximum_fusion.1.refs_0_), channel_id=1, source_target_pairs={{0,8},{1,9},{2,10},{3,11},{4,12},{5,13},{6,14},{7,15},{8,0},{9,1},... | collective-permute-start | bytes 454664 | tf_op jit(solution)/shard_map/ppermute | solution.py:328
  14.1 14.2 %collective-permute-start.2 = (bf16[592,128]{1,0:T(8,128)(2,1)S(1)}, bf16[592,128]{1,0:T(8,128)(2,1)S(1)}, u32[]{:S(2)}, u32[]{:S(2)}) collective-permute-start(bf16[592,128]{1,0:T(8,128)(2,1)S(1)} %pad_maximum_fusion.1.refs_0_), channel_id=1, source_target_pairs={{0,16},{1,17},{2,18},{3,19},{4,20},{5,21},{6,22},{7,23},{8,24},{9,... | collective-permute-start | bytes 454664 | tf_op jit(solution)/shard_map/ppermute | solution.py:328
  16.7 11.7 %collective-permute-start.3 = (bf16[592,128]{1,0:T(8,128)(2,1)S(1)}, bf16[592,128]{1,0:T(8,128)(2,1)S(1)}, u32[]{:S(2)}, u32[]{:S(2)}) collective-permute-start(bf16[592,128]{1,0:T(8,128)(2,1)S(1)} %pad_maximum_fusion.1.refs_0_), channel_id=1, source_target_pairs={{0,24},{1,25},{2,26},{3,27},{4,28},{5,29},{6,30},{7,31},{8,16},{9,... | collective-permute-start | bytes 454664 | tf_op jit(solution)/shard_map/ppermute | solution.py:328
  16.9 33.1 %collective-permute-start.7 = (bf16[2128,128]{1,0:T(8,128)(2,1)S(1)}, bf16[2128,128]{1,0:T(8,128)(2,1)S(1)}, u32[]{:S(2)}, u32[]{:S(2)}) collective-permute-start(bf16[2128,128]{1,0:T(8,128)(2,1)S(1)} %constant_dynamic-update-slice_fusion.3), channel_id=1, source_target_pairs={{0,1},{1,0},{2,3},{3,2},{4,5},{5,4},{6,7},{7,6},{8,9},{9,8},{10,11... | collective-permute-start | bytes 1634312 | tf_op jit(solution)/shard_map/ppermute | solution.py:328
  28.4 32.2 %collective-permute-start.4 = (bf16[1776,128]{1,0:T(8,128)(2,1)S(1)}, bf16[1776,128]{1,0:T(8,128)(2,1)S(1)}, u32[]{:S(2)}, u32[]{:S(2)}) collective-permute-start(bf16[1776,128]{1,0:T(8,128)(2,1)S(1)} %constant_dynamic-update-slice_fusion), channel_id=1, source_target_pairs={{0,4},{1,5},{2,6},{3,7},{4,0},{5,1},{6,2},{7,3},{8,12},{9,13},{10,... | collective-permute-start | bytes 1363976 | tf_op jit(solution)/shard_map/ppermute | solution.py:328
  30.0 14.6 %collective-permute-start.9 = (bf16[592,128]{1,0:T(8,128)(2,1)S(1)}, bf16[592,128]{1,0:T(8,128)(2,1)S(1)}, u32[]{:S(2)}, u32[]{:S(2)}) collective-permute-start(bf16[592,128]{1,0:T(8,128)(2,1)S(1)} %pad_maximum_fusion.1.refs_0_), channel_id=1, source_target_pairs={{0,5},{1,4},{2,7},{3,6},{4,1},{5,0},{6,3},{7,2},{8,13},{9,12},{10,... | collective-permute-start | bytes 454664 | tf_op jit(solution)/shard_map/ppermute | solution.py:328
  31.5 16.8 %collective-permute-start.6 = (bf16[592,128]{1,0:T(8,128)(2,1)S(1)}, bf16[592,128]{1,0:T(8,128)(2,1)S(1)}, u32[]{:S(2)}, u32[]{:S(2)}) collective-permute-start(bf16[592,128]{1,0:T(8,128)(2,1)S(1)} %pad_maximum_fusion.1.refs_0_), channel_id=1, source_target_pairs={{0,4},{1,5},{2,6},{3,7},{4,0},{5,1},{6,2},{7,3},{8,12},{9,13},{10,... | collective-permute-start | bytes 454664 | tf_op jit(solution)/shard_map/ppermute | solution.py:328
  33.0 44.6 %collective-permute-start.8 = (bf16[1776,128]{1,0:T(8,128)(2,1)S(1)}, bf16[1776,128]{1,0:T(8,128)(2,1)S(1)}, u32[]{:S(2)}, u32[]{:S(2)}) collective-permute-start(bf16[1776,128]{1,0:T(8,128)(2,1)S(1)} %constant_dynamic-update-slice_fusion), channel_id=1, source_target_pairs={{0,1},{1,0},{2,3},{3,2},{4,5},{5,4},{6,7},{7,6},{8,9},{9,8},{10,11... | collective-permute-start | bytes 1363976 | tf_op jit(solution)/shard_map/ppermute | solution.py:328
  44.6 23.5 %collective-permute-start.10 = (bf16[592,128]{1,0:T(8,128)(2,1)S(1)}, bf16[592,128]{1,0:T(8,128)(2,1)S(1)}, u32[]{:S(2)}, u32[]{:S(2)}) collective-permute-start(bf16[592,128]{1,0:T(8,128)(2,1)S(1)} %collective-permute-done.9.refs_1_), channel_id=1, source_target_pairs={{0,8},{1,9},{2,10},{3,11},{4,12},{5,13},{6,14},{7,15},{8,0},{9,1},... | collective-permute-start | bytes 454664 | tf_op jit(solution)/shard_map/ppermute | solution.py:328
  48.3 19.8 %collective-permute-start.11 = (bf16[592,128]{1,0:T(8,128)(2,1)S(1)}, bf16[592,128]{1,0:T(8,128)(2,1)S(1)}, u32[]{:S(2)}, u32[]{:S(2)}) collective-permute-start(bf16[592,128]{1,0:T(8,128)(2,1)S(1)} %collective-permute-done.9.refs_1_), channel_id=1, source_target_pairs={{0,16},{1,17},{2,18},{3,19},{4,20},{5,21},{6,22},{7,23},{8,24},{9,... | collective-permute-start | bytes 454664 | tf_op jit(solution)/shard_map/ppermute | solution.py:328
  49.9 18.2 %collective-permute-start.12 = (bf16[592,128]{1,0:T(8,128)(2,1)S(1)}, bf16[592,128]{1,0:T(8,128)(2,1)S(1)}, u32[]{:S(2)}, u32[]{:S(2)}) collective-permute-start(bf16[592,128]{1,0:T(8,128)(2,1)S(1)} %collective-permute-done.9.refs_1_), channel_id=1, source_target_pairs={{0,24},{1,25},{2,26},{3,27},{4,28},{5,29},{6,30},{7,31},{8,16},{9,... | collective-permute-start | bytes 454664 | tf_op jit(solution)/shard_map/ppermute | solution.py:328
  68.0 17.5 %collective-permute-start.13 = (bf16[2,512,128]{2,1,0:T(8,128)(2,1)S(1)}, bf16[2,512,128]{2,1,0:T(8,128)(2,1)S(1)}, u32[]{:S(2)}, u32[]{:S(2)}) collective-permute-start(bf16[2,512,128]{2,1,0:T(8,128)(2,1)S(1)} %slice.27), channel_id=1, source_target_pairs={{0,2},{1,3},{2,0},{3,1},{4,6},{5,7},{6,4},{7,5},{8,10},{9,11},{10,... | collective-permute-start | bytes 786440 | tf_op jit(solution)/shard_map/ppermute | solution.py:328
  85.0 1.7 %collective-permute-start.14 = (bf16[2,512,128]{2,1,0:T(8,128)(2,1)S(1)}, bf16[2,512,128]{2,1,0:T(8,128)(2,1)S(1)}, u32[]{:S(2)}, u32[]{:S(2)}) collective-permute-start(bf16[2,512,128]{2,1,0:T(8,128)(2,1)S(1)} %slice.28), channel_id=1, source_target_pairs={{0,2},{1,3},{2,0},{3,1},{4,6},{5,7},{6,4},{7,5},{8,10},{9,11},{10,... | collective-permute-start | bytes 786440 | tf_op jit(solution)/shard_map/ppermute | solution.py:328

commit v2 on v0

--- a/solution.py
+++ b/solution.py
@@ -1,11 +1,461 @@
+import functools
 import math
 
 import jax
 import jax.numpy as jnp
+import numpy as np
 from jax import lax
+from jax.experimental import pallas as pl
+from jax.experimental.pallas import tpu as pltpu
 from jax.sharding import PartitionSpec as P
 
 rope_base = 500000.0
+axes = ("outer", "inner")
+bf16 = jnp.bfloat16
+f32 = jnp.float32
+
+
+def frequencies(head_dim):
+    ladder = np.arange(head_dim // 2, dtype=np.float32)
+    return np.exp(ladder * np.float32(-2.0 * math.log(rope_base) / head_dim)).astype(np.float32)
+
+
+def angle_table(positions, head_dim):
+    return frequencies(head_dim)[:, None] * positions.astype(np.float32)[None, :]
+
+
+def whole(memory=pltpu.VMEM):
+    return pl.BlockSpec(memory_space=memory)
+
+
+def params(megabytes=16):
+    return pltpu.CompilerParams(vmem_limit_bytes=megabytes * 2**20)
+
+
+def pack_prefix(place, ids, codes, values, scales, half):
+    rows, kv_local, groups = codes.shape
+    head_dim = values.shape[-1]
+    extent = half * (rows + groups)
+
+    def kernel(place, ids, codes, values, scales, keep, send):
+        core = place[0]
+        diagonal = lax.broadcasted_iota(jnp.int32, (rows, rows), 0) == lax.broadcasted_iota(jnp.int32, (rows, rows), 1)
+
+        def put(target, head, k):
+            factor = jnp.broadcast_to(scales[head : head + 1, :], (rows, rows))
+            factor = jnp.sum(jnp.where(diagonal, factor, 0.0), axis=1, keepdims=True)
+            target[k * rows : (k + 1) * rows, :] = (values[:, head, :].astype(f32) * factor).astype(bf16)
+            first = half * rows + k * groups
+            target[first : first + groups, :] = codes[head].astype(f32).astype(bf16)
+
+        for side in range(2):
+
+            @pl.when(core == side)
+            def _():
+                for k in range(half):
+                    put(send, (1 - side) * half + k, k)
+                    put(keep, side * half + k, k)
+
+        send[extent:, :] = jnp.full((16, head_dim), ids[0], jnp.int32).astype(f32).astype(bf16)
+
+    return pl.pallas_call(
+        kernel,
+        out_shape=(
+            jax.ShapeDtypeStruct((extent, head_dim), bf16),
+            jax.ShapeDtypeStruct((extent + 16, head_dim), bf16),
+        ),
+        in_specs=[whole(pltpu.SMEM), whole(pltpu.SMEM), whole(), whole(), whole()],
+        out_specs=(whole(), whole()),
+        compiler_params=params(),
+        name="pack_prefix",
+    )(place, ids, codes.transpose(1, 2, 0), values, scales.T)
+
+
+def rotate_stretch(heads, cosine, sine, qkv, half_heads):
+    tokens, n_heads, slots, head_dim = qkv.shape
+    group = slots - 2
+    q_rows = tokens * group
+    rows = q_rows + 2 * tokens
+
+    def kernel(heads, cosine, sine, qkv, keep, send, q_scratch, k_scratch, v_scratch):
+        cos, sin = cosine[...][:, None, :], sine[...][:, None, :]
+
+        def turn(x):
+            return x * cos + pltpu.roll(x, head_dim // 2, 2) * sin
+
+        spread = (tokens, 1, n_heads, head_dim)
+        for slot in range(group):
+            x = turn(qkv[:, slot, :, :].astype(f32))
+            q_scratch[:, slot : slot + 1, :, :] = x.reshape(spread)
+        k_scratch[...] = turn(qkv[:, group, :, :].astype(f32))
+        v_scratch[...] = qkv[:, group + 1, :, :].astype(f32)
+        q_flat = q_scratch.reshape(q_rows * n_heads, head_dim)
+        k_flat = k_scratch.reshape(tokens * n_heads, head_dim)
+        v_flat = v_scratch.reshape(tokens * n_heads, head_dim)
+        for step in range(2 * half_heads):
+            target = send if step < half_heads else keep
+            at = step % half_heads
+            head = heads[step]
+            target[at, :q_rows, :] = q_flat[pl.ds(head, q_rows, stride=n_heads), :].astype(bf16)
+            target[at, q_rows : q_rows + tokens, :] = k_flat[pl.ds(head, tokens, stride=n_heads), :].astype(bf16)
+            target[at, q_rows + tokens :, :] = v_flat[pl.ds(head, tokens, stride=n_heads), :].astype(bf16)
+
+    shape = jax.ShapeDtypeStruct((half_heads, rows, head_dim), bf16)
+    return pl.pallas_call(
+        kernel,
+        out_shape=(shape, shape),
+        in_specs=[whole(pltpu.SMEM), whole(), whole(), whole()],
+        out_specs=(whole(), whole()),
+        scratch_shapes=[
+            pltpu.VMEM((tokens, group, n_heads, head_dim), f32),
+            pltpu.VMEM((tokens, n_heads, head_dim), f32),
+            pltpu.VMEM((tokens, n_heads, head_dim), f32),
+        ],
+        compiler_params=params(),
+        name="rotate_stretch",
+    )(heads, cosine, sine, qkv.transpose(0, 2, 1, 3))
+
+
+def attend(place, groups_of, tables, queries, stretch, state, sizes, final, megabytes=32):
+    half, rows, groups, tokens, group, head_dim, codes = sizes
+    q_rows = tokens * group
+    scale = head_dim**-0.5 * math.log2(math.e)
+    gd = head_dim // groups
+    half_dim = head_dim // 2
+    n_heads = queries[0].shape[0]
+    lengths = [sum(len(blocks) for _, blocks in pieces) * rows for _, _, pieces, _ in groups_of]
+    extra = 2 * tokens if stretch is not None else 0
+    chunk = 768
+
+    operands, where = [], {}
+
+    def ref_of(array):
+        if id(array) not in where:
+            where[id(array)] = len(operands)
+            operands.append(array)
+        return where[id(array)]
+
+    plan = [
+        (first, ref_of(book), row, [(ref_of(array), blocks) for array, blocks in pieces])
+        for first, (book, row), pieces, _ in groups_of
+    ]
+    table_at = [ref_of(t) for t in tables]
+    query_at = [ref_of(q) for q in queries]
+    stretch_at = ref_of(stretch) if stretch is not None else None
+    n_plain = len(operands)
+    if state is not None:
+        operands += list(state)
+
+    def kernel(place, *refs):
+        refs = list(refs)
+        given = refs[:n_plain]
+        before = refs[n_plain : n_plain + 3] if state is not None else None
+        refs = refs[len(operands) :]
+        results = refs[: 2 if final else 3]
+        refs = refs[len(results) :]
+        kts, vvs = refs[: len(plan)], refs[len(plan) : 2 * len(plan)]
+        tab, slots = refs[2 * len(plan)], refs[2 * len(plan) + 1 :]
+        core, inner = place[0], place[1]
+        cos_tok, sin_tok, cos_blk, sin_blk = [given[i] for i in table_at]
+        requests = [given[i] for i in query_at]
+        other = given[stretch_at] if stretch is not None else None
+
+        def decode(group_index):
+            first, book_at, book_row, pieces = plan[group_index]
+            kt, vv, book = kts[group_index], vvs[group_index], given[book_at]
+            for k in range(half):
+                if book_row is None:
+                    entries = book[core * half + k]
+                else:
+                    entries = book[book_row + k * codes : book_row + (k + 1) * codes, :]
+                tab[k] = entries.astype(f32).T
+            index = 0
+            for at, blocks in pieces:
+                ref = given[at]
+                for value_row, code_row, id_row in blocks:
+                    base = id_row - id_row % 16
+                    block = ref[base : base + 16, :].astype(f32)
+                    block = block[id_row % 16 : id_row % 16 + 8].astype(jnp.int32)
+                    block = jnp.broadcast_to(block[None], (half_dim // 8, 8, head_dim)).reshape(half_dim, head_dim)
+                    cb = jnp.take_along_axis(cos_blk[...], block, axis=1, mode="promise_in_bounds")
+                    sb = jnp.take_along_axis(sin_blk[...], block, axis=1, mode="promise_in_bounds")
+                    ct, st = cos_tok[...], sin_tok[...]
+                    cos = cb * ct - sb * st
+                    sin = sb * ct + cb * st
+                    span = slice(index * rows, (index + 1) * rows)
+                    for k in range(half):
+                        code = ref[code_row + k * groups : code_row + (k + 1) * groups, :].astype(f32).astype(jnp.int32)
+                        code = jnp.broadcast_to(code[:, None, :], (groups, gd, rows)).reshape(head_dim, rows)
+                        low = code & 127
+                        key = jnp.take_along_axis(tab[k, :, :128], low, axis=1, mode="promise_in_bounds")
+                        for part in range(1, codes // 128):
+                            entries = tab[k, :, part * 128 : (part + 1) * 128]
+                            more = jnp.take_along_axis(entries, low, axis=1, mode="promise_in_bounds")
+                            key = jnp.where(code >= part * 128, more, key)
+                        a, b = key[:half_dim], key[half_dim:]
+                        key = jnp.concatenate([a * cos - b * sin, b * cos + a * sin], axis=0).astype(bf16)
+                        kt[k, :head_dim, span] = key
+                        kt[k, head_dim:, span] = key
+                        vv[k, span, :] = ref[value_row + k * rows : value_row + (k + 1) * rows, :]
+                    index += 1
+
+        for group_index in range(len(plan)):
+            decode(group_index)
+
+        works = [(g, k, e) for g in range(len(plan)) for k in range(half) for e in range(2)]
+
+        def parts(work):
+            return [(c, min(chunk, lengths[work[0]] - c)) for c in range(0, lengths[work[0]], chunk)]
+
+        def prepare(work):
+            g, k, e = work
+            scaled = requests[e][plan[g][0] + k, :q_rows, :].astype(f32) * scale
+            hi = scaled.astype(bf16)
+            lo = (scaled - hi.astype(f32)).astype(bf16)
+            return jnp.concatenate([hi, lo], axis=1)
+
+        def fold(top, score):
+            for i in range(score.shape[1] // 128):
+                piece = score[:, i * 128 : (i + 1) * 128]
+                top = piece if top is None else jnp.maximum(top, piece)
+            return top
+
+        def score_part(work, q, slot, top, c, width):
+            score = jnp.dot(q, kts[work[0]][work[1], :, c : c + width], preferred_element_type=f32)
+            slot[:, c : c + width] = score
+            return fold(top, score)
+
+        def stretch_rows(work, which):
+            g, k, e = work
+            head = plan[g][0] + k
+            base = (e * n_heads + (head + half) % n_heads) * 2 * tokens + which * tokens
+            mine = q_rows + which * tokens
+            return jnp.concatenate([other[base : base + tokens, :], requests[e][head, mine : mine + tokens, :]], axis=0)
+
+        def score_stretch(work, q, slot, top):
+            key = stretch_rows(work, 0)
+            key = jnp.concatenate([key, key], axis=1)
+            score = lax.dot_general(q, key, (((1,), (1,)), ((), ())), preferred_element_type=f32)
+            column = lax.broadcasted_iota(jnp.int32, score.shape, 1)
+            row = lax.broadcasted_iota(jnp.int32, score.shape, 0) // group
+            allowed = (column - tokens <= row) & (column >= tokens * (1 - inner))
+            score = jnp.where(allowed, score, -jnp.inf)
+            slot[:, lengths[work[0]] : lengths[work[0]] + extra] = score
+            return fold(top, score)
+
+        def weigh(slot, m, part, mixed, c, width, value):
+            weights = []
+            for i in range(c, c + width, 128):
+                weight = jnp.exp2(slot[:, i : i + 128] - m)
+                part = part + weight
+                weights.append(weight.astype(bf16))
+            weight = jnp.concatenate(weights, axis=1) if len(weights) > 1 else weights[0]
+            return part, mixed + jnp.dot(weight, value, preferred_element_type=f32)
+
+        def place_of(work):
+            g, k, e = work
+            return plan[g][0] + k, slice(e * q_rows, (e + 1) * q_rows), slice(None)
+
+        current = None
+        for t in range(len(works) + 1):
+            slot, old = slots[t % 2], slots[1 - t % 2]
+            work = works[t] if t < len(works) else None
+            top = None
+            if work is not None:
+                q = prepare(work)
+            if current is not None:
+                done, m, part, mixed = current
+            if stretch is not None:
+                if work is not None:
+                    top = score_stretch(work, q, slot, top)
+                if current is not None:
+                    part, mixed = weigh(old, m, part, mixed, lengths[done[0]], extra, stretch_rows(done, 1))
+            ahead = parts(work) if work is not None else []
+            behind = parts(done) if current is not None else []
+            for i in range(max(len(ahead), len(behind))):
+                if i < len(ahead):
+                    top = score_part(work, q, slot, top, *ahead[i])
+                if i < len(behind):
+                    c, width = behind[i]
+                    part, mixed = weigh(old, m, part, mixed, c, width, vvs[done[0]][done[1], c : c + width, :])
+            if current is not None:
+                if final:
+                    head = plan[done[0]][0] + done[1]
+                    results[done[2]][head] = (mixed / jnp.sum(part, axis=1, keepdims=True)).astype(bf16)
+                else:
+                    for ref, value in zip(results, (m, part, mixed)):
+                        ref[place_of(done)] = value
+            if work is not None:
+                m = jnp.broadcast_to(jnp.max(top, axis=1, keepdims=True), (q_rows, 128))
+                if not groups_of[work[0]][3]:
+                    part = jnp.zeros((q_rows, 128), f32)
+                    mixed = jnp.zeros((q_rows, head_dim), f32)
+                else:
+                    past = before[0][place_of(work)]
+                    m = jnp.maximum(past, m)
+                    decay = jnp.exp2(past - m)
+                    part = before[1][place_of(work)] * decay
+                    mixed = before[2][place_of(work)] * decay
+                current = (work, m, part, mixed)
+
+    if final:
+        out_shape = (jax.ShapeDtypeStruct((n_heads, q_rows, head_dim), bf16),) * 2
+    else:
+        out_shape = (jax.ShapeDtypeStruct((n_heads, 2 * q_rows, 128), f32),) * 3
+    alias = {1 + n_plain + j: j for j in range(3)} if state is not None and not final else {}
+    pairs = 2 * half * q_rows * (sum(lengths) + extra * len(plan))
+    slot = pltpu.VMEM((q_rows, max(lengths) + extra), f32)
+    return pl.pallas_call(
+        kernel,
+        out_shape=out_shape,
+        in_specs=[whole(pltpu.SMEM)] + [whole() for _ in operands],
+        out_specs=(whole(),) * len(out_shape),
+        scratch_shapes=[pltpu.VMEM((half, 2 * head_dim, n), bf16) for n in lengths]
+        + [pltpu.VMEM((half, n, head_dim), bf16) for n in lengths]
+        + [pltpu.VMEM((half, head_dim, codes), f32), slot, slot],
+        input_output_aliases=alias,
+        compiler_params=params(megabytes),
+        cost_estimate=pl.CostEstimate(flops=8 * pairs * head_dim, bytes_accessed=4 * 2**20, transcendentals=pairs),
+        name="attend",
+    )(place, *operands)
+
+
+def lay_out(heads, own, received, tokens, group):
+    arrays = list(own) + list(received)
+    half, _, head_dim = arrays[0].shape
+    q_rows = tokens * group
+
+    def kernel(heads, *refs):
+        out = refs[-1]
+        for j, ref in enumerate(refs[:-1]):
+            for k in range(half):
+                out[:, pl.ds(heads[j * half + k], 1), :, :] = ref[k, :q_rows, :].reshape(tokens, 1, group, head_dim)
+
+    return pl.pallas_call(
+        kernel,
+        out_shape=jax.ShapeDtypeStruct((tokens, half * len(arrays), group, head_dim), bf16),
+        in_specs=[whole(pltpu.SMEM)] + [whole()] * len(arrays),
+        out_specs=whole(),
+        compiler_params=params(),
+        name="lay_out",
+    )(heads, *arrays)
+
+
+def paired(qkv, key_codes, codebooks, value_codes, value_scales, block_ids, *, n_outer):
+    tokens, n_heads, slots, head_dim = qkv.shape
+    group = slots - 2
+    rows, kv_local, groups = key_codes.shape
+    codes = codebooks.shape[1]
+    half = kv_local // 2
+    n_far = n_outer // 4
+    prefix = rows * n_outer
+    outer, inner = lax.axis_index("outer"), lax.axis_index("inner")
+    core = outer % 2
+    place = jnp.stack([core, inner]).astype(jnp.int32)
+    extent = half * (rows + groups)
+
+    def swap(x, outer_bits, inner_bits=0):
+        return lax.ppermute(
+            x,
+            axes,
+            [
+                (2 * o + i, 2 * (o ^ outer_bits) + (i ^ inner_bits))
+                for o in range(n_outer)
+                for i in range(2)
+            ],
+        )
+
+    keep, send = pack_prefix(place, block_ids, key_codes, value_codes, value_scales, half)
+    mate = swap(send, 1)
+
+    own_id = jnp.full((8, head_dim), block_ids[0].astype(bf16))
+    pack = jnp.concatenate([keep, mate[:extent], own_id, mate[extent + 8 :]], axis=0)
+    size = pack.shape[0]
+
+    def blocks_of(base, count=1):
+        out = []
+        for j in range(count):
+            b = base + j * size
+            out.append((b, b + half * rows, b + 2 * extent))
+            out.append((b + extent, b + extent + half * rows, b + 2 * extent + 8))
+        return out
+
+    def along(parts, bits):
+        return swap(jnp.concatenate(parts, axis=0) if len(parts) > 1 else parts[0], 4 * bits)
+
+    my_books = lax.dynamic_slice_in_dim(codebooks, core * half, half, 0).reshape(half * codes, head_dim)
+    z_far = [along([pack], n_far // 2)]
+    diag = swap(pack, 2, 1)
+    x_pack = swap(pack, 2)
+    y_pack = swap(jnp.concatenate([pack, my_books], axis=0), 0, 1)
+    z_far[0], diag, x_pack = lax.optimization_barrier((z_far[0], diag, x_pack))
+    diag_far = [along([diag], n_far // 2)]
+    bits = n_far // 4
+    while bits:
+        z_far.append(along([pack] + z_far, bits))
+        bits //= 2
+
+    mate, qkv = lax.optimization_barrier((mate, qkv))
+    own_first = jnp.stack([inner, 1 - inner]).astype(jnp.int32)
+
+    def order(which):
+        return (own_first[:, None] * kv_local + which * half + jnp.arange(half)[None, :]).reshape(-1).astype(jnp.int32)
+
+    cosine = np.cos(angle_table(np.arange(2 * tokens) + prefix, head_dim)).T
+    sine = np.sin(angle_table(np.arange(2 * tokens) + prefix, head_dim)).T
+    cosine = jnp.asarray(np.concatenate([cosine, cosine], axis=1))
+    sine = jnp.asarray(np.concatenate([-sine, sine], axis=1))
+    cosine = lax.dynamic_slice_in_dim(cosine, inner * tokens, tokens, 0)
+    sine = lax.dynamic_slice_in_dim(sine, inner * tokens, tokens, 0)
+    q_keep, q_send = rotate_stretch(
+        jnp.concatenate([order(1 - core), order(core)]), cosine, sine, qkv, 2 * half
+    )
+    q_mate = swap(q_send, 1)
+
+    q_rows = tokens * group
+
+    positions = np.arange(rows)
+    cos_tok, sin_tok = np.cos(angle_table(positions, head_dim)), np.sin(angle_table(positions, head_dim))
+    starts = np.arange(128) * rows
+    cos_blk, sin_blk = np.cos(angle_table(starts, head_dim)), np.sin(angle_table(starts, head_dim))
+    tables = [jnp.asarray(t.astype(np.float32)) for t in (cos_tok, sin_tok, cos_blk, sin_blk)]
+    sizes = (half, rows, groups, tokens, group, head_dim, codes)
+    queries = (q_keep, q_mate)
+    call = functools.partial(attend, place, tables=tables, queries=queries, sizes=sizes)
+    own_book = (codebooks, None)
+
+    def pieces(*arrays):
+        return [(a, blocks_of(0, a.shape[0] // size)) for a in arrays]
+
+    state = call([(0, own_book, pieces(pack, x_pack, z_far[0]), False)], stretch=None, state=None, final=False)
+    kv_own = jnp.concatenate([q_keep[:, q_rows:], q_mate[:, q_rows:]], axis=0).reshape(-1, head_dim)
+    kv_own, y_pack, *state = lax.optimization_barrier((kv_own, y_pack, *state))
+    kv_pair = swap(kv_own, 0, 1)
+    other_book, y_near = (y_pack, size), [(y_pack, blocks_of(0))]
+    z_all = jnp.concatenate(z_far, axis=0)
+    y_far = swap(z_all, 0, 1)
+    x_far = swap(z_all, 2)
+    diag_far[0], kv_pair = lax.optimization_barrier((diag_far[0], kv_pair))
+    bits = n_far // 4
+    while bits:
+        diag_far.append(along([diag] + diag_far, bits))
+        bits //= 2
+    state = call(
+        [(0, own_book, pieces(*z_far[1:]), True), (half, other_book, y_near + pieces(diag, diag_far[0]), False)],
+        stretch=kv_pair, state=state, final=False,
+    )
+    out, out_send = call(
+        [(0, own_book, pieces(x_far), True), (half, other_book, pieces(*diag_far[1:], y_far), True)],
+        stretch=None, state=state, final=True,
+    )
+    out_mate = swap(out_send, 1)
+    return lay_out(
+        jnp.concatenate([order(core), order(1 - core)]),
+        [out],
+        [out_mate],
+        tokens,
+        group,
+    )
 
 
 def rotate(tensor, position):
@@ -110,8 +560,33 @@
 
 
 def solution(mesh):
+    n_outer, n_inner = mesh.shape["outer"], mesh.shape["inner"]
+
+    def body(qkv, key_codes, codebooks, value_codes, value_scales, block_ids):
+        arrays = (qkv, key_codes, codebooks, value_codes, value_scales, block_ids)
+        head_dim = qkv.shape[3]
+        far = n_outer // 4
+        fits = (
+            n_inner == 2
+            and n_outer % 4 == 0
+            and 1 < far
+            and far & (far - 1) == 0
+            and n_outer <= 128
+            and key_codes.shape[1] % 2 == 0
+            and key_codes.shape[0] == 128
+            and head_dim == 128
+            and head_dim // key_codes.shape[2] == 8
+            and key_codes.shape[2] % 16 == 0
+            and codebooks.shape[1] % 128 == 0
+            and qkv.shape[2] == 10
+            and qkv.shape[0] % 32 == 0
+        )
+        if fits:
+            return paired(*arrays, n_outer=n_outer)
+        return shards(*arrays)
+
     return jax.shard_map(
-        shards,
+        body,
         mesh=mesh,
         in_specs=(
             P(("outer", "inner"), None, None, None),

time: 177 us -> 57.7 us (0.33)
  waiting for transfers between devices: 66.6 us -> 15.1 us
  matrix products: 37.9 us -> 0 us
  other arithmetic: 24.7 us -> 0.44 us
  Pallas kernels: 0 us -> 22.5 us
  blocking collectives: 16.8 us -> 0 us
  between operations: 14.2 us -> 0.85 us
  starting transfers between devices: 4.24 us -> 13.7 us
  local copies, waits for them, and re-layouts: 12 us -> 4.87 us
    all_gather x2 -> x0, waiting for transfers between devices: 52.4 us -> none  [the longest x1 42.5 us: shards(): key_rows = lax.all_gather(prefix_keys, 'outer', axis=0, tiled=True)]
    dot_general x7 -> x0, matrix products: 37.9 us -> none  [the longest x3 19.1 us: absorb(): jnp.einsum('tkgd,nkd->tkgn', queries, key_rows, preferred_element_type=jn...]
    pallas_call x0 -> x6, Pallas kernels: none -> 22.5 us  [the longest x3 18 us: attend(): pl.pallas_call(kernel, out_shape=out_shape, in_specs=[whole(pltpu.SMEM)]...]
    reduce_sum x3 -> x0, other arithmetic: 18.1 us -> none  [absorb(): running_sum = running_sum * decay_factor + jnp.sum(weights, axis=-1)]
    all_to_all x1 -> x0, blocking collectives: 16.8 us -> none  [shards(): lax.all_to_all(outputs, 'inner', split_axis=0, concat_axis=1, tiled=True)]
    ppermute x0 -> x13, waiting for transfers between devices: none -> 15.1 us  [swap(): lax.ppermute(x, axes, [(2 * o + i, 2 * (o ^ outer_bits) + (i ^ inner_bits...]
    all_to_all x1 -> x0, waiting for transfers between devices: 14.2 us -> none  [shards(): lax.all_to_all(qkv, 'inner', split_axis=1, concat_axis=0, tiled=True)]
    ppermute x0 -> x13, starting transfers between devices: none -> 13.7 us  [swap(): lax.ppermute(x, axes, [(2 * o + i, 2 * (o ^ outer_bits) + (i ^ inner_bits...]
  transfers between devices with their start and end apart: 3 -> 13, of which waited for: 3 -> 9; matrix products, arithmetic and copies ran while one was open for 8% -> 3% of each run, Pallas kernels for 0% -> 17%
where the time goes in v2:
time: 57.7 us; the launch traced here: 57.4 us
  Pallas kernels  22.5 us (39%)
  waiting for transfers between devices  15.1 us (26%)
  starting transfers between devices  13.7 us (24%)
  local copies, waits for them, and re-layouts  4.87 us (8%)
  between operations  0.85 us (1%)
    pallas_call x3, Pallas kernels, attend(): pl.pallas_call(kernel, out_shape=out_shape, in_specs=[whole(pltpu.SMEM)]...  18 us
    ppermute x13, waiting for transfers between devices, swap(): lax.ppermute(x, axes, [(2 * o + i, 2 * (o ^ outer_bits) + (i ^ inner_bits...  15.1 us
    ppermute x13, starting transfers between devices, swap(): lax.ppermute(x, axes, [(2 * o + i, 2 * (o ^ outer_bits) + (i ^ inner_bits...  13.7 us
    unnamed x23, local copies, waits for them, and re-layouts  3.75 us
    pallas_call x1, Pallas kernels, lay_out(): pl.pallas_call(kernel, out_shape=jax.ShapeDtypeStruct((tokens, half * len...  1.82 us
    pallas_call x1, Pallas kernels, rotate_stretch(): pl.pallas_call(kernel, out_shape=(shape, shape), in_specs=[whole(pltpu.SM...  1.8 us
  transfers between devices with their start and end apart: 13, of which 9 were waited for; matrix products, arithmetic and copies ran while one was open for 3% of the time, Pallas kernels for 17%

profile of v2, /device:TPU:0, one launch (start us, length us, event | category | flops | bytes accessed | tf_op | source)
XLA Modules:
  0.0 57.4 jit_solution(12539063380143765653)
XLA Ops:
  0.7 0.1 pad_add_fusion.1
  0.7 0.0 copy-start.1
  0.7 0.9 %copy-done.1 = bf16[128,4,128]{2,1,0:T(4,128)(2,1)S(1)} copy-done((bf16[128,4,128]{2,1,0:T(4,128)(2,1)S(1)}, bf16[128,4,128]{2,1,0:T(4,128)(2,1)}, u32[]{:S(2)}) %copy-start.1) | copy-done | bytes 131096
  1.6 0.0 copy-start.3
  1.6 0.8 %copy-done.3 = s32[128,4,16]{0,2,1:T(8,128)S(1)} copy-done((s32[128,4,16]{0,2,1:T(8,128)S(1)}, s32[128,4,16]{0,2,1:T(8,128)}, u32[]{:S(2)}) %copy-start.3) | copy-done | bytes 32792
  2.4 0.0 copy-start.4
  2.4 0.7 %copy-done.4 = f32[128,4]{0,1:T(4,128)S(1)} copy-done((f32[128,4]{0,1:T(4,128)S(1)}, f32[128,4]{0,1:T(4,128)}, u32[]{:S(2)}) %copy-start.4) | copy-done | bytes 2072
  3.1 0.0 copy-start.2
  3.1 0.8 %pack_prefix.1 = (bf16[288,128]{1,0:T(8,128)(2,1)S(1)}, bf16[304,128]{1,0:T(8,128)(2,1)S(1)}) custom-call(s32[2]{0:T(128)S(1)} %get-tuple-element.63.place, s32[1]{0:T(128)S(6)} %copy.28.ids, s32[4,16,128]{2,1,0:T(8,128)S(1)} %bitcast.10, bf16[128,4,128]{2,1,0:T(4,128)(2,1)S(1)} %copy-done.1, f32[4,128]{1,0:T(4,128)S(1)} %bitcast.11), custom_call_target="tpu_custom_call" | custom-call | tf_op jit(solution)/shard_map/pack_prefix/pallas_call | solution.py:61
  3.9 0.6 %collective-permute-start = (bf16[304,128]{1,0:T(8,128)(2,1)S(1)}, bf16[304,128]{1,0:T(8,128)(2,1)S(1)}, u32[]{:S(2)}, u32[]{:S(2)}) collective-permute-start(bf16[304,128]{1,0:T(8,128)(2,1)S(1)} %get-tuple-element.29), channel_id=1, source_target_pairs={{0,2},{1,3},{2,0},{3,1},{4,6},{5,7},{6,4},{7,5},{8,10},{9,11},{10,... | collective-permute-start | bytes 233480 | tf_op jit(solution)/shard_map/ppermute | solution.py:358
  4.5 0.1 broadcast_add_fusion.1
  4.6 0.1 iota_add_fusion
  4.7 0.1 add.97
  4.8 0.1 iota_add_fusion.1
  4.9 0.1 add.91
  4.9 0.0 copy-start.5
  4.9 0.0 copy-start.6
  4.9 0.0 copy-start.7
  4.9 0.0 copy-start.8
  5.0 0.8 %constant_dynamic-slice_fusion.1 = (f32[64,128]{1,0:T(8,128)S(1)}, f32[64,128]{1,0:T(8,128)S(1)}) fusion(f32[128,128]{1,0:T(8,128)} %constant.43.clone, s32[]{:T(128)S(6)} %select_n.15, f32[128,128]{1,0:T(8,128)} %constant.42.clone), kind=kLoop, calls=%fused_computation.18 | loop fusion | bytes 131076 | tf_op jit(solution)/shard_map/dynamic_slice | solution.py:409
  5.8 0.1 pad_add_fusion.2
  5.9 0.0 collective-permute-done
  5.9 0.0 copy-start
  5.9 1.3 %copy-done = bf16[64,8,10,128]{3,1,2,0:T(8,128)(2,1)S(1)} copy-done((bf16[64,8,10,128]{3,1,2,0:T(8,128)(2,1)S(1)}, bf16[64,8,10,128]{3,1,2,0:T(8,128)(2,1)}, u32[]{:S(2)}) %copy-start) | copy-done | bytes 1310744
  7.2 1.8 %rotate_stretch.1 = (bf16[4,640,128]{2,1,0:T(8,128)(2,1)S(1)}, bf16[4,640,128]{2,1,0:T(8,128)(2,1)S(1)}) custom-call(s32[8]{0:T(128)S(1)} %get-tuple-element.61.heads, f32[64,128]{1,0:T(8,128)S(1)} %get-tuple-element.66.cosine, f32[64,128]{1,0:T(8,128)S(1)} %get-tuple-element.65.sine, bf16[64,10,8,128]{3,2,1,0:T(8,128)(2,1)S(1)} %bitcast.9), custom_call_target="tpu_custom_call" | custom-call | tf_op jit(solution)/shard_map/rotate_stretch/pallas_call | solution.py:104
  9.1 0.1 collective-permute-start.6
  9.2 4.0 %collective-permute-start.1 = (bf16[592,128]{1,0:T(8,128)(2,1)S(1)}, bf16[592,128]{1,0:T(8,128)(2,1)S(1)}, u32[]{:S(2)}, u32[]{:S(2)}) collective-permute-start(bf16[592,128]{1,0:T(8,128)(2,1)S(1)} %pad_maximum_fusion.2.refs_1_), channel_id=1, source_target_pairs={{0,16},{1,17},{2,18},{3,19},{4,20},{5,21},{6,22},{7,23},{8,24},{9,... | collective-permute-start | bytes 454664 | tf_op jit(solution)/shard_map/ppermute | solution.py:358
  13.2 2.4 %collective-permute-start.2 = (bf16[592,128]{1,0:T(8,128)(2,1)S(1)}, bf16[592,128]{1,0:T(8,128)(2,1)S(1)}, u32[]{:S(2)}, u32[]{:S(2)}) collective-permute-start(bf16[592,128]{1,0:T(8,128)(2,1)S(1)} %pad_maximum_fusion.2.refs_1_), channel_id=1, source_target_pairs={{0,5},{1,4},{2,7},{3,6},{4,1},{5,0},{6,3},{7,2},{8,13},{9,12},{10,... | collective-permute-start | bytes 454664 | tf_op jit(solution)/shard_map/ppermute | solution.py:358
  15.7 0.5 collective-permute-start.3
  16.2 0.0 copy-done.2
  16.2 0.6 %collective-permute-start.7 = (bf16[1104,128]{1,0:T(8,128)(2,1)S(1)}, bf16[1104,128]{1,0:T(8,128)(2,1)S(1)}, u32[]{:S(2)}, u32[]{:S(2)}) collective-permute-start(bf16[1104,128]{1,0:T(8,128)(2,1)S(1)} %constant_dynamic-update-slice_fusion.7), channel_id=1, source_target_pairs={{0,1},{1,0},{2,3},{3,2},{4,5},{5,4},{6,7},{7,6},{8,9},{9,8},{10,11... | collective-permute-start | bytes 847880 | tf_op jit(solution)/shard_map/ppermute | solution.py:358
  16.8 3.8 %collective-permute-done.1.refs_3_ = bf16[592,128]{1,0:T(8,128)(2,1)S(1)} collective-permute-done((bf16[592,128]{1,0:T(8,128)(2,1)S(1)}, bf16[592,128]{1,0:T(8,128)(2,1)S(1)}, u32[]{:S(2)}, u32[]{:S(2)}) %collective-permute-start.1) | collective-permute-done | bytes 151584 | tf_op jit(solution)/shard_map/ppermute | solution.py:358
  20.6 0.4 collective-permute-done.2.refs_3_
  21.0 2.0 %collective-permute-done.3.refs_2_ = bf16[592,128]{1,0:T(8,128)(2,1)S(1)} collective-permute-done((bf16[592,128]{1,0:T(8,128)(2,1)S(1)}, bf16[592,128]{1,0:T(8,128)(2,1)S(1)}, u32[]{:S(2)}, u32[]{:S(2)}) %collective-permute-start.3) | collective-permute-done | bytes 151584 | tf_op jit(solution)/shard_map/ppermute | solution.py:358
  23.0 1.6 %collective-permute-start.4 = (bf16[1184,128]{1,0:T(8,128)(2,1)S(1)}, bf16[1184,128]{1,0:T(8,128)(2,1)S(1)}, u32[]{:S(2)}, u32[]{:S(2)}) collective-permute-start(bf16[1184,128]{1,0:T(8,128)(2,1)S(1)} %get-tuple-element.51), channel_id=1, source_target_pairs={{0,8},{1,9},{2,10},{3,11},{4,12},{5,13},{6,14},{7,15},{8,0},{9,1},... | collective-permute-start | bytes 909320 | tf_op jit(solution)/shard_map/ppermute | solution.py:358
  24.7 0.0 collective-permute-done.6.refs_9_.refs_10_
  24.8 0.0 copy-done.5
  24.8 0.0 copy-done.6
  24.8 0.0 copy-done.7
  24.8 0.0 copy-done.8
  24.8 3.4 %attend.3 = (f32[4,1024,128]{2,1,0:T(8,128)S(1)}, f32[4,1024,128]{2,1,0:T(8,128)S(1)}, f32[4,1024,128]{2,1,0:T(8,128)S(1)}) custom-call(s32[2]{0:T(128)S(1)} %get-tuple-element.63.place, bf16[4,256,128]{2,1,0:T(8,128)(2,1)S(1)} %copy-done.2, bf16[592,128]{1,0:T(8,128)(2,1)S(1)} %pad_maximum_fusion.2.refs_1_, ...), custom_call_target="tpu_custom_call" | custom-call | flops 1610612736 | bytes 4194304 | tf_op jit(solution)/shard_map/attend/pallas_call | solution.py:308
  28.2 0.0 collective-permute-done.7.refs_2_
  28.2 0.6 %collective-permute-start.9 = (bf16[1024,128]{1,0:T(8,128)(2,1)S(1)}, bf16[1024,128]{1,0:T(8,128)(2,1)S(1)}, u32[]{:S(2)}, u32[]{:S(2)}) collective-permute-start(bf16[1024,128]{1,0:T(8,128)(2,1)S(1)} %bitcast.13), channel_id=1, source_target_pairs={{0,1},{1,0},{2,3},{3,2},{4,5},{5,4},{6,7},{7,6},{8,9},{9,8},{10,11... | collective-permute-start | bytes 786440 | tf_op jit(solution)/shard_map/ppermute | solution.py:358
  28.8 1.1 %collective-permute-start.8 = (bf16[592,128]{1,0:T(8,128)(2,1)S(1)}, bf16[592,128]{1,0:T(8,128)(2,1)S(1)}, u32[]{:S(2)}, u32[]{:S(2)}) collective-permute-start(bf16[592,128]{1,0:T(8,128)(2,1)S(1)} %collective-permute-done.2.refs_3_), channel_id=1, source_target_pairs={{0,16},{1,17},{2,18},{3,19},{4,20},{5,21},{6,22},{7,23},{8,24},{9,... | collective-permute-start | bytes 454664 | tf_op jit(solution)/shard_map/ppermute | solution.py:358
  29.9 2.3 %collective-permute-done.4.refs_1_ = bf16[1184,128]{1,0:T(8,128)(2,1)S(1)} collective-permute-done((bf16[1184,128]{1,0:T(8,128)(2,1)S(1)}, bf16[1184,128]{1,0:T(8,128)(2,1)S(1)}, u32[]{:S(2)}, u32[]{:S(2)}) %collective-permute-start.4) | collective-permute-done | bytes 303136 | tf_op jit(solution)/shard_map/ppermute | solution.py:358
  32.2 0.1 collective-permute-start.11
  32.3 1.6 %collective-permute-start.5 = (bf16[1776,128]{1,0:T(8,128)(2,1)S(1)}, bf16[1776,128]{1,0:T(8,128)(2,1)S(1)}, u32[]{:S(2)}, u32[]{:S(2)}) collective-permute-start(bf16[1776,128]{1,0:T(8,128)(2,1)S(1)} %constant_dynamic-update-slice_fusion.5), channel_id=1, source_target_pairs={{0,4},{1,5},{2,6},{3,7},{4,0},{5,1},{6,2},{7,3},{8,12},{9,13},{10,... | collective-permute-start | bytes 1363976 | tf_op jit(solution)/shard_map/ppermute | solution.py:358
  33.9 3.2 %collective-permute-done.8.refs_4_ = bf16[592,128]{1,0:T(8,128)(2,1)S(1)} collective-permute-done((bf16[592,128]{1,0:T(8,128)(2,1)S(1)}, bf16[592,128]{1,0:T(8,128)(2,1)S(1)}, u32[]{:S(2)}, u32[]{:S(2)}) %collective-permute-start.8) | collective-permute-done | bytes 151584 | tf_op jit(solution)/shard_map/ppermute | solution.py:358
  37.1 0.4 collective-permute-done.9.refs_11_
  37.6 0.3 collective-permute-start.10
  37.9 6.3 %attend.4 = (f32[4,1024,128]{2,1,0:T(8,128)S(1)}, f32[4,1024,128]{2,1,0:T(8,128)S(1)}, f32[4,1024,128]{2,1,0:T(8,128)S(1)}) custom-call(s32[2]{0:T(128)S(1)} %get-tuple-element.63.place, bf16[4,256,128]{2,1,0:T(8,128)(2,1)S(1)} %copy-done.2, ...), custom_call_target="tpu_custom_call", output_to_operand_aliasing={{0}: (13, {}), {1}: (14, {}), {2}: (15, {})} | custom-call | flops 3221225472 | bytes 4194304 | tf_op jit(solution)/shard_map/attend/pallas_call | solution.py:308
  44.2 0.7 %collective-permute-done.11.refs_4_ = bf16[1776,128]{1,0:T(8,128)(2,1)S(1)} collective-permute-done((bf16[1776,128]{1,0:T(8,128)(2,1)S(1)}, bf16[1776,128]{1,0:T(8,128)(2,1)S(1)}, u32[]{:S(2)}, u32[]{:S(2)}) %collective-permute-start.11) | collective-permute-done | bytes 454688 | tf_op jit(solution)/shard_map/ppermute | solution.py:358
  44.8 0.0 collective-permute-done.5.refs_1_
  44.8 0.4 collective-permute-done.10.refs_3_
  45.2 8.4 %attend.5 = (bf16[4,512,128]{2,1,0:T(8,128)(2,1)S(1)}, bf16[4,512,128]{2,1,0:T(8,128)(2,1)S(1)}) custom-call(s32[2]{0:T(128)S(1)} %get-tuple-element.63.place, bf16[4,256,128]{2,1,0:T(8,128)(2,1)S(1)} %copy-done.2, bf16[1776,128]{1,0:T(8,128)(2,1)S(1)} %collective-permute-done.5.refs_1_, bf16[1104,128]{1,0:T(8,128)(2,1)S(1)} %collective-permute-done.7.refs_2_, ...), custom_call_target="tpu_custom_call" | custom-call | flops 4294967296 | bytes 4194304 | tf_op jit(solution)/shard_map/attend/pallas_call | solution.py:308
  53.6 0.1 collective-permute-start.12
  53.7 1.9 %collective-permute-done.12.refs_1_ = bf16[4,512,128]{2,1,0:T(8,128)(2,1)S(1)} collective-permute-done((bf16[4,512,128]{2,1,0:T(8,128)(2,1)S(1)}, bf16[4,512,128]{2,1,0:T(8,128)(2,1)S(1)}, u32[]{:S(2)}, u32[]{:S(2)}) %collective-permute-start.12) | collective-permute-done | bytes 524320 | tf_op jit(solution)/shard_map/ppermute | solution.py:358
  55.6 1.8 %lay_out.1 = bf16[64,8,8,128]{3,2,1,0:T(8,128)(2,1)} custom-call(s32[8]{0:T(128)S(1)} %get-tuple-element.62.heads, bf16[4,512,128]{2,1,0:T(8,128)(2,1)S(1)} %get-tuple-element.49.refs_0_, bf16[4,512,128]{2,1,0:T(8,128)(2,1)S(1)} %collective-permute-done.12.refs_1_), custom_call_target="tpu_custom_call" | custom-call | tf_op jit(solution)/shard_map/lay_out/pallas_call | solution.py:334
  (15 shorter events, 0.3 us)
Async XLA Ops:
  0.7 0.9 %copy-start.1 = (bf16[128,4,128]{2,1,0:T(4,128)(2,1)S(1)}, bf16[128,4,128]{2,1,0:T(4,128)(2,1)}, u32[]{:S(2)}) copy-start(bf16[128,4,128]{2,1,0:T(4,128)(2,1)} %values.1) | copy-start | bytes 393220
  1.6 0.8 %copy-start.3 = (s32[128,4,16]{0,2,1:T(8,128)S(1)}, s32[128,4,16]{0,2,1:T(8,128)}, u32[]{:S(2)}) copy-start(s32[128,4,16]{0,2,1:T(8,128)} %param.13) | copy-start | bytes 98308
  2.4 0.7 %copy-start.4 = (f32[128,4]{0,1:T(4,128)S(1)}, f32[128,4]{0,1:T(4,128)}, u32[]{:S(2)}) copy-start(f32[128,4]{0,1:T(4,128)} %param.16) | copy-start | bytes 6148
  3.1 13.1 %copy-start.2 = (bf16[4,256,128]{2,1,0:T(8,128)(2,1)S(1)}, bf16[4,256,128]{2,1,0:T(8,128)(2,1)}, u32[]{:S(2)}) copy-start(bf16[4,256,128]{2,1,0:T(8,128)(2,1)} %refs_0_.5) | copy-start | bytes 786436
  3.9 1.9 %collective-permute-start = (bf16[304,128]{1,0:T(8,128)(2,1)S(1)}, bf16[304,128]{1,0:T(8,128)(2,1)S(1)}, u32[]{:S(2)}, u32[]{:S(2)}) collective-permute-start(bf16[304,128]{1,0:T(8,128)(2,1)S(1)} %get-tuple-element.29), channel_id=1, source_target_pairs={{0,2},{1,3},{2,0},{3,1},{4,6},{5,7},{6,4},{7,5},{8,10},{9,11},{10,... | collective-permute-start | bytes 233480 | tf_op jit(solution)/shard_map/ppermute | solution.py:358
  4.9 19.8 %copy-start.5 = (f32[64,128]{1,0:T(8,128)S(1)}, f32[64,128]{1,0:T(8,128)}, u32[]{:S(2)}) copy-start(f32[64,128]{1,0:T(8,128)} %constant.44.clone.refs_4_.refs_5_) | copy-start | bytes 98308
  4.9 19.8 %copy-start.6 = (f32[64,128]{1,0:T(8,128)S(1)}, f32[64,128]{1,0:T(8,128)}, u32[]{:S(2)}) copy-start(f32[64,128]{1,0:T(8,128)} %constant.45.clone.refs_5_.refs_6_) | copy-start | bytes 98308
  4.9 19.8 %copy-start.7 = (f32[64,128]{1,0:T(8,128)S(1)}, f32[64,128]{1,0:T(8,128)}, u32[]{:S(2)}) copy-start(f32[64,128]{1,0:T(8,128)} %constant.46.clone.refs_6_.refs_7_) | copy-start | bytes 98308
  4.9 19.8 %copy-start.8 = (f32[64,128]{1,0:T(8,128)S(1)}, f32[64,128]{1,0:T(8,128)}, u32[]{:S(2)}) copy-start(f32[64,128]{1,0:T(8,128)} %constant.47.clone.refs_7_.refs_8_) | copy-start | bytes 98308
  5.9 1.3 %copy-start = (bf16[64,8,10,128]{3,1,2,0:T(8,128)(2,1)S(1)}, bf16[64,8,10,128]{3,1,2,0:T(8,128)(2,1)}, u32[]{:S(2)}) copy-start(bf16[64,8,10,128]{3,1,2,0:T(8,128)(2,1)} %param.12) | copy-start | bytes 3932164
  9.1 15.6 %collective-permute-start.6 = (bf16[4,640,128]{2,1,0:T(8,128)(2,1)S(1)}, bf16[4,640,128]{2,1,0:T(8,128)(2,1)S(1)}, u32[]{:S(2)}, u32[]{:S(2)}) collective-permute-start(bf16[4,640,128]{2,1,0:T(8,128)(2,1)S(1)} %get-tuple-element.33), channel_id=1, source_target_pairs={{0,2},{1,3},{2,0},{3,1},{4,6},{5,7},{6,4},{7,5},{8,10},{9,11},{10,... | collective-permute-start | bytes 1966088 | tf_op jit(solution)/shard_map/ppermute | solution.py:358
  9.2 11.4 %collective-permute-start.1 = (bf16[592,128]{1,0:T(8,128)(2,1)S(1)}, bf16[592,128]{1,0:T(8,128)(2,1)S(1)}, u32[]{:S(2)}, u32[]{:S(2)}) collective-permute-start(bf16[592,128]{1,0:T(8,128)(2,1)S(1)} %pad_maximum_fusion.2.refs_1_), channel_id=1, source_target_pairs={{0,16},{1,17},{2,18},{3,19},{4,20},{5,21},{6,22},{7,23},{8,24},{9,... | collective-permute-start | bytes 454664 | tf_op jit(solution)/shard_map/ppermute | solution.py:358
  13.2 7.7 %collective-permute-start.2 = (bf16[592,128]{1,0:T(8,128)(2,1)S(1)}, bf16[592,128]{1,0:T(8,128)(2,1)S(1)}, u32[]{:S(2)}, u32[]{:S(2)}) collective-permute-start(bf16[592,128]{1,0:T(8,128)(2,1)S(1)} %pad_maximum_fusion.2.refs_1_), channel_id=1, source_target_pairs={{0,5},{1,4},{2,7},{3,6},{4,1},{5,0},{6,3},{7,2},{8,13},{9,12},{10,... | collective-permute-start | bytes 454664 | tf_op jit(solution)/shard_map/ppermute | solution.py:358
  15.7 7.3 %collective-permute-start.3 = (bf16[592,128]{1,0:T(8,128)(2,1)S(1)}, bf16[592,128]{1,0:T(8,128)(2,1)S(1)}, u32[]{:S(2)}, u32[]{:S(2)}) collective-permute-start(bf16[592,128]{1,0:T(8,128)(2,1)S(1)} %pad_maximum_fusion.2.refs_1_), channel_id=1, source_target_pairs={{0,4},{1,5},{2,6},{3,7},{4,0},{5,1},{6,2},{7,3},{8,12},{9,13},{10,... | collective-permute-start | bytes 454664 | tf_op jit(solution)/shard_map/ppermute | solution.py:358
  16.2 12.0 %collective-permute-start.7 = (bf16[1104,128]{1,0:T(8,128)(2,1)S(1)}, bf16[1104,128]{1,0:T(8,128)(2,1)S(1)}, u32[]{:S(2)}, u32[]{:S(2)}) collective-permute-start(bf16[1104,128]{1,0:T(8,128)(2,1)S(1)} %constant_dynamic-update-slice_fusion.7), channel_id=1, source_target_pairs={{0,1},{1,0},{2,3},{3,2},{4,5},{5,4},{6,7},{7,6},{8,9},{9,8},{10,11... | collective-permute-start | bytes 847880 | tf_op jit(solution)/shard_map/ppermute | solution.py:358
  23.0 9.1 %collective-permute-start.4 = (bf16[1184,128]{1,0:T(8,128)(2,1)S(1)}, bf16[1184,128]{1,0:T(8,128)(2,1)S(1)}, u32[]{:S(2)}, u32[]{:S(2)}) collective-permute-start(bf16[1184,128]{1,0:T(8,128)(2,1)S(1)} %get-tuple-element.51), channel_id=1, source_target_pairs={{0,8},{1,9},{2,10},{3,11},{4,12},{5,13},{6,14},{7,15},{8,0},{9,1},... | collective-permute-start | bytes 909320 | tf_op jit(solution)/shard_map/ppermute | solution.py:358
  28.2 9.3 %collective-permute-start.9 = (bf16[1024,128]{1,0:T(8,128)(2,1)S(1)}, bf16[1024,128]{1,0:T(8,128)(2,1)S(1)}, u32[]{:S(2)}, u32[]{:S(2)}) collective-permute-start(bf16[1024,128]{1,0:T(8,128)(2,1)S(1)} %bitcast.13), channel_id=1, source_target_pairs={{0,1},{1,0},{2,3},{3,2},{4,5},{5,4},{6,7},{7,6},{8,9},{9,8},{10,11... | collective-permute-start | bytes 786440 | tf_op jit(solution)/shard_map/ppermute | solution.py:358
  28.8 8.3 %collective-permute-start.8 = (bf16[592,128]{1,0:T(8,128)(2,1)S(1)}, bf16[592,128]{1,0:T(8,128)(2,1)S(1)}, u32[]{:S(2)}, u32[]{:S(2)}) collective-permute-start(bf16[592,128]{1,0:T(8,128)(2,1)S(1)} %collective-permute-done.2.refs_3_), channel_id=1, source_target_pairs={{0,16},{1,17},{2,18},{3,19},{4,20},{5,21},{6,22},{7,23},{8,24},{9,... | collective-permute-start | bytes 454664 | tf_op jit(solution)/shard_map/ppermute | solution.py:358
  32.2 12.6 %collective-permute-start.11 = (bf16[1776,128]{1,0:T(8,128)(2,1)S(1)}, bf16[1776,128]{1,0:T(8,128)(2,1)S(1)}, u32[]{:S(2)}, u32[]{:S(2)}) collective-permute-start(bf16[1776,128]{1,0:T(8,128)(2,1)S(1)} %constant_dynamic-update-slice_fusion.5), channel_id=1, source_target_pairs={{0,1},{1,0},{2,3},{3,2},{4,5},{5,4},{6,7},{7,6},{8,9},{9,8},{10,11... | collective-permute-start | bytes 1363976 | tf_op jit(solution)/shard_map/ppermute | solution.py:358
  32.3 12.5 %collective-permute-start.5 = (bf16[1776,128]{1,0:T(8,128)(2,1)S(1)}, bf16[1776,128]{1,0:T(8,128)(2,1)S(1)}, u32[]{:S(2)}, u32[]{:S(2)}) collective-permute-start(bf16[1776,128]{1,0:T(8,128)(2,1)S(1)} %constant_dynamic-update-slice_fusion.5), channel_id=1, source_target_pairs={{0,4},{1,5},{2,6},{3,7},{4,0},{5,1},{6,2},{7,3},{8,12},{9,13},{10,... | collective-permute-start | bytes 1363976 | tf_op jit(solution)/shard_map/ppermute | solution.py:358
  37.6 7.7 %collective-permute-start.10 = (bf16[1184,128]{1,0:T(8,128)(2,1)S(1)}, bf16[1184,128]{1,0:T(8,128)(2,1)S(1)}, u32[]{:S(2)}, u32[]{:S(2)}) collective-permute-start(bf16[1184,128]{1,0:T(8,128)(2,1)S(1)} %pad_maximum_fusion), channel_id=1, source_target_pairs={{0,8},{1,9},{2,10},{3,11},{4,12},{5,13},{6,14},{7,15},{8,0},{9,1},... | collective-permute-start | bytes 909320 | tf_op jit(solution)/shard_map/ppermute | solution.py:358
  53.6 2.0 %collective-permute-start.12 = (bf16[4,512,128]{2,1,0:T(8,128)(2,1)S(1)}, bf16[4,512,128]{2,1,0:T(8,128)(2,1)S(1)}, u32[]{:S(2)}, u32[]{:S(2)}) collective-permute-start(bf16[4,512,128]{2,1,0:T(8,128)(2,1)S(1)} %get-tuple-element.50), channel_id=1, source_target_pairs={{0,2},{1,3},{2,0},{3,1},{4,6},{5,7},{6,4},{7,5},{8,10},{9,11},{10,... | collective-permute-start | bytes 1572872 | tf_op jit(solution)/shard_map/ppermute | solution.py:358

commit v3 on v2

--- a/solution.py
+++ b/solution.py
@@ -32,13 +32,31 @@
     return pltpu.CompilerParams(vmem_limit_bytes=megabytes * 2**20)
 
 
-def pack_prefix(place, ids, codes, values, scales, half):
+def prepare(place, ids, codes, values, scales, qkv, prefix, half):
     rows, kv_local, groups = codes.shape
-    head_dim = values.shape[-1]
+    tokens, n_heads, slots, head_dim = qkv.shape
+    group = slots - 2
+    q_rows = tokens * group
     extent = half * (rows + groups)
-
-    def kernel(place, ids, codes, values, scales, keep, send):
-        core = place[0]
+    n_out = 2 * half
+    kv_at = extent + 16 + n_out * q_rows
+    size = kv_at + n_out * 2 * tokens
+    angles = angle_table(np.arange(2 * tokens) + prefix, head_dim)
+    cosine, sine = np.cos(angles).T, np.sin(angles).T
+    cosine = jnp.asarray(np.concatenate([cosine, cosine], axis=1).astype(np.float32))
+    sine = jnp.asarray(np.concatenate([-sine, sine], axis=1).astype(np.float32))
+    sources = (codes.transpose(1, 2, 0), values, scales.T, qkv.transpose(0, 2, 1, 3), cosine, sine)
+
+    def kernel(place, ids, *refs):
+        given, (keep, send), held = refs[:6], refs[6:8], refs[8:14]
+        codes, values, scales, qkv, cosine, sine = held
+        q_scratch, k_scratch, v_scratch, sems = refs[14:]
+        core, inner = place[0], place[1]
+        copies = [pltpu.make_async_copy(*pair, sems.at[i]) for i, pair in enumerate(zip(given, held))]
+        for copy in copies:
+            copy.start()
+        for copy in copies[:3]:
+            copy.wait()
         diagonal = lax.broadcasted_iota(jnp.int32, (rows, rows), 0) == lax.broadcasted_iota(jnp.int32, (rows, rows), 1)
 
         def put(target, head, k):
@@ -56,29 +74,13 @@
                     put(send, (1 - side) * half + k, k)
                     put(keep, side * half + k, k)
 
-        send[extent:, :] = jnp.full((16, head_dim), ids[0], jnp.int32).astype(f32).astype(bf16)
-
-    return pl.pallas_call(
-        kernel,
-        out_shape=(
-            jax.ShapeDtypeStruct((extent, head_dim), bf16),
-            jax.ShapeDtypeStruct((extent + 16, head_dim), bf16),
-        ),
-        in_specs=[whole(pltpu.SMEM), whole(pltpu.SMEM), whole(), whole(), whole()],
-        out_specs=(whole(), whole()),
-        compiler_params=params(),
-        name="pack_prefix",
-    )(place, ids, codes.transpose(1, 2, 0), values, scales.T)
-
-
-def rotate_stretch(heads, cosine, sine, qkv, half_heads):
-    tokens, n_heads, slots, head_dim = qkv.shape
-    group = slots - 2
-    q_rows = tokens * group
-    rows = q_rows + 2 * tokens
-
-    def kernel(heads, cosine, sine, qkv, keep, send, q_scratch, k_scratch, v_scratch):
-        cos, sin = cosine[...][:, None, :], sine[...][:, None, :]
+        number = jnp.full((16, head_dim), ids[0], jnp.int32).astype(f32).astype(bf16)
+        send[extent : extent + 16, :] = number
+        keep[extent : extent + 16, :] = number
+        for copy in copies[3:]:
+            copy.wait()
+        at = pl.ds(pl.multiple_of(inner * tokens, tokens), tokens)
+        cos, sin = cosine[at, :][:, None, :], sine[at, :][:, None, :]
 
         def turn(x):
             return x * cos + pltpu.roll(x, head_dim // 2, 2) * sin
@@ -92,28 +94,32 @@
         q_flat = q_scratch.reshape(q_rows * n_heads, head_dim)
         k_flat = k_scratch.reshape(tokens * n_heads, head_dim)
         v_flat = v_scratch.reshape(tokens * n_heads, head_dim)
-        for step in range(2 * half_heads):
-            target = send if step < half_heads else keep
-            at = step % half_heads
-            head = heads[step]
-            target[at, :q_rows, :] = q_flat[pl.ds(head, q_rows, stride=n_heads), :].astype(bf16)
-            target[at, q_rows : q_rows + tokens, :] = k_flat[pl.ds(head, tokens, stride=n_heads), :].astype(bf16)
-            target[at, q_rows + tokens :, :] = v_flat[pl.ds(head, tokens, stride=n_heads), :].astype(bf16)
-
-    shape = jax.ShapeDtypeStruct((half_heads, rows, head_dim), bf16)
+        for target, which in ((send, 1 - core), (keep, core)):
+            for j in range(n_out):
+                head = (inner if j < half else 1 - inner) * kv_local + which * half + j % half
+                first = extent + 16 + j * q_rows
+                target[first : first + q_rows, :] = q_flat[pl.ds(head, q_rows, stride=n_heads), :].astype(bf16)
+                first = kv_at + j * 2 * tokens
+                target[first : first + tokens, :] = k_flat[pl.ds(head, tokens, stride=n_heads), :].astype(bf16)
+                first += tokens
+                target[first : first + tokens, :] = v_flat[pl.ds(head, tokens, stride=n_heads), :].astype(bf16)
+
+    shape = jax.ShapeDtypeStruct((size, head_dim), bf16)
     return pl.pallas_call(
         kernel,
         out_shape=(shape, shape),
-        in_specs=[whole(pltpu.SMEM), whole(), whole(), whole()],
+        in_specs=[whole(pltpu.SMEM)] * 2 + [whole(pltpu.HBM)] * 6,
         out_specs=(whole(), whole()),
-        scratch_shapes=[
+        scratch_shapes=[pltpu.VMEM(x.shape, x.dtype) for x in sources]
+        + [
             pltpu.VMEM((tokens, group, n_heads, head_dim), f32),
             pltpu.VMEM((tokens, n_heads, head_dim), f32),
             pltpu.VMEM((tokens, n_heads, head_dim), f32),
+            pltpu.SemaphoreType.DMA((6,)),
         ],
         compiler_params=params(),
-        name="rotate_stretch",
-    )(heads, cosine, sine, qkv.transpose(0, 2, 1, 3))
+        name="prepare",
+    )(place, ids, *[pltpu.with_memory_space_constraint(x, pltpu.HBM) for x in sources])
 
 
 def attend(place, groups_of, tables, queries, stretch, state, sizes, final, megabytes=32):
@@ -122,7 +128,9 @@
     scale = head_dim**-0.5 * math.log2(math.e)
     gd = head_dim // groups
     half_dim = head_dim // 2
-    n_heads = queries[0].shape[0]
+    n_heads = 2 * half
+    q_at = half * (rows + groups) + 16
+    kv_at = q_at + n_heads * q_rows
     lengths = [sum(len(blocks) for _, blocks in pieces) * rows for _, _, pieces, _ in groups_of]
     extra = 2 * tokens if stretch is not None else 0
     chunk = 768
@@ -207,9 +215,10 @@
         def parts(work):
             return [(c, min(chunk, lengths[work[0]] - c)) for c in range(0, lengths[work[0]], chunk)]
 
-        def prepare(work):
+        def scaled_queries(work):
             g, k, e = work
-            scaled = requests[e][plan[g][0] + k, :q_rows, :].astype(f32) * scale
+            first = q_at + (plan[g][0] + k) * q_rows
+            scaled = requests[e][first : first + q_rows, :].astype(f32) * scale
             hi = scaled.astype(bf16)
             lo = (scaled - hi.astype(f32)).astype(bf16)
             return jnp.concatenate([hi, lo], axis=1)
@@ -229,8 +238,8 @@
             g, k, e = work
             head = plan[g][0] + k
             base = (e * n_heads + (head + half) % n_heads) * 2 * tokens + which * tokens
-            mine = q_rows + which * tokens
-            return jnp.concatenate([other[base : base + tokens, :], requests[e][head, mine : mine + tokens, :]], axis=0)
+            mine = kv_at + head * 2 * tokens + which * tokens
+            return jnp.concatenate([other[base : base + tokens, :], requests[e][mine : mine + tokens, :]], axis=0)
 
         def score_stretch(work, q, slot, top):
             key = stretch_rows(work, 0)
@@ -262,7 +271,7 @@
             work = works[t] if t < len(works) else None
             top = None
             if work is not None:
-                q = prepare(work)
+                q = scaled_queries(work)
             if current is not None:
                 done, m, part, mixed = current
             if stretch is not None:
@@ -281,7 +290,8 @@
             if current is not None:
                 if final:
                     head = plan[done[0]][0] + done[1]
-                    results[done[2]][head] = (mixed / jnp.sum(part, axis=1, keepdims=True)).astype(bf16)
+                    result = mixed / jnp.sum(part, axis=1, keepdims=True)
+                    results[done[2]][head] = result.reshape(tokens, group, head_dim).astype(bf16)
                 else:
                     for ref, value in zip(results, (m, part, mixed)):
                         ref[place_of(done)] = value
@@ -299,7 +309,7 @@
                 current = (work, m, part, mixed)
 
     if final:
-        out_shape = (jax.ShapeDtypeStruct((n_heads, q_rows, head_dim), bf16),) * 2
+        out_shape = (jax.ShapeDtypeStruct((n_heads, tokens, group, head_dim), bf16),) * 2
     else:
         out_shape = (jax.ShapeDtypeStruct((n_heads, 2 * q_rows, 128), f32),) * 3
     alias = {1 + n_plain + j: j for j in range(3)} if state is not None and not final else {}
@@ -320,25 +330,32 @@
     )(place, *operands)
 
 
-def lay_out(heads, own, received, tokens, group):
-    arrays = list(own) + list(received)
-    half, _, head_dim = arrays[0].shape
-    q_rows = tokens * group
-
-    def kernel(heads, *refs):
-        out = refs[-1]
-        for j, ref in enumerate(refs[:-1]):
-            for k in range(half):
-                out[:, pl.ds(heads[j * half + k], 1), :, :] = ref[k, :q_rows, :].reshape(tokens, 1, group, head_dim)
+def lay_out(place, heads_of, foreign, out):
+    n_out, tokens, group, head_dim = heads_of.shape
+    half = n_out // 2
+
+    def kernel(place, source, *refs):
+        target, sems = refs[-2:]
+        core, inner = place[0], place[1]
+        which = 1 - core if foreign else core
+        copies = []
+        for j in range(n_out):
+            head = (inner if j < half else 1 - inner) * n_out + which * half + j % half
+            copies.append(pltpu.make_async_copy(source.at[j], target.at[:, head], sems.at[j]))
+            copies[-1].start()
+        for copy in copies:
+            copy.wait()
 
     return pl.pallas_call(
         kernel,
-        out_shape=jax.ShapeDtypeStruct((tokens, half * len(arrays), group, head_dim), bf16),
-        in_specs=[whole(pltpu.SMEM)] + [whole()] * len(arrays),
-        out_specs=whole(),
+        out_shape=jax.ShapeDtypeStruct((tokens, 2 * n_out, group, head_dim), bf16),
+        in_specs=[whole(pltpu.SMEM), whole()] + ([] if out is None else [whole(pl.ANY)]),
+        out_specs=whole(pl.ANY),
+        scratch_shapes=[pltpu.SemaphoreType.DMA((n_out,))],
+        input_output_aliases={} if out is None else {2: 0},
         compiler_params=params(),
         name="lay_out",
-    )(heads, *arrays)
+    )(place, heads_of, *([] if out is None else [out]))
 
 
 def paired(qkv, key_codes, codebooks, value_codes, value_scales, block_ids, *, n_outer):
@@ -365,11 +382,11 @@
             ],
         )
 
-    keep, send = pack_prefix(place, block_ids, key_codes, value_codes, value_scales, half)
+    keep, send = prepare(place, block_ids, key_codes, value_codes, value_scales, qkv, prefix, half)
     mate = swap(send, 1)
-
-    own_id = jnp.full((8, head_dim), block_ids[0].astype(bf16))
-    pack = jnp.concatenate([keep, mate[:extent], own_id, mate[extent + 8 :]], axis=0)
+    queries = (keep, mate)
+
+    pack = jnp.concatenate([keep[:extent], mate[:extent], keep[extent : extent + 8], mate[extent : extent + 8]], axis=0)
     size = pack.shape[0]
 
     def blocks_of(base, count=1):
@@ -388,74 +405,54 @@
     diag = swap(pack, 2, 1)
     x_pack = swap(pack, 2)
     y_pack = swap(jnp.concatenate([pack, my_books], axis=0), 0, 1)
-    z_far[0], diag, x_pack = lax.optimization_barrier((z_far[0], diag, x_pack))
+    z_far[0], diag = lax.optimization_barrier((z_far[0], diag))
     diag_far = [along([diag], n_far // 2)]
     bits = n_far // 4
     while bits:
         z_far.append(along([pack] + z_far, bits))
         bits //= 2
 
-    mate, qkv = lax.optimization_barrier((mate, qkv))
-    own_first = jnp.stack([inner, 1 - inner]).astype(jnp.int32)
-
-    def order(which):
-        return (own_first[:, None] * kv_local + which * half + jnp.arange(half)[None, :]).reshape(-1).astype(jnp.int32)
-
-    cosine = np.cos(angle_table(np.arange(2 * tokens) + prefix, head_dim)).T
-    sine = np.sin(angle_table(np.arange(2 * tokens) + prefix, head_dim)).T
-    cosine = jnp.asarray(np.concatenate([cosine, cosine], axis=1))
-    sine = jnp.asarray(np.concatenate([-sine, sine], axis=1))
-    cosine = lax.dynamic_slice_in_dim(cosine, inner * tokens, tokens, 0)
-    sine = lax.dynamic_slice_in_dim(sine, inner * tokens, tokens, 0)
-    q_keep, q_send = rotate_stretch(
-        jnp.concatenate([order(1 - core), order(core)]), cosine, sine, qkv, 2 * half
-    )
-    q_mate = swap(q_send, 1)
-
-    q_rows = tokens * group
-
+    x_first, y_first = swap(z_far[0], 2), swap(z_far[0], 0, 1)
     positions = np.arange(rows)
     cos_tok, sin_tok = np.cos(angle_table(positions, head_dim)), np.sin(angle_table(positions, head_dim))
     starts = np.arange(128) * rows
     cos_blk, sin_blk = np.cos(angle_table(starts, head_dim)), np.sin(angle_table(starts, head_dim))
     tables = [jnp.asarray(t.astype(np.float32)) for t in (cos_tok, sin_tok, cos_blk, sin_blk)]
     sizes = (half, rows, groups, tokens, group, head_dim, codes)
-    queries = (q_keep, q_mate)
     call = functools.partial(attend, place, tables=tables, queries=queries, sizes=sizes)
     own_book = (codebooks, None)
 
     def pieces(*arrays):
         return [(a, blocks_of(0, a.shape[0] // size)) for a in arrays]
 
-    state = call([(0, own_book, pieces(pack, x_pack, z_far[0]), False)], stretch=None, state=None, final=False)
-    kv_own = jnp.concatenate([q_keep[:, q_rows:], q_mate[:, q_rows:]], axis=0).reshape(-1, head_dim)
-    kv_own, y_pack, *state = lax.optimization_barrier((kv_own, y_pack, *state))
+    own_kv = 2 * half * 2 * tokens
+    kv_own = jnp.concatenate([keep[-own_kv:], mate[-own_kv:]], axis=0)
+    kv_own, y_pack = lax.optimization_barrier((kv_own, y_pack))
     kv_pair = swap(kv_own, 0, 1)
+    state = call([(0, own_book, pieces(pack, x_pack, z_far[0], x_first), False)], stretch=None, state=None, final=False)
     other_book, y_near = (y_pack, size), [(y_pack, blocks_of(0))]
-    z_all = jnp.concatenate(z_far, axis=0)
-    y_far = swap(z_all, 0, 1)
-    x_far = swap(z_all, 2)
-    diag_far[0], kv_pair = lax.optimization_barrier((diag_far[0], kv_pair))
+    *z_rest, y_first = lax.optimization_barrier((*z_far[1:], y_first))
+    z_rest = jnp.concatenate(z_rest, axis=0) if len(z_rest) > 1 else z_rest[0]
+    y_rest = swap(z_rest, 0, 1)
+    x_rest = swap(z_rest, 2)
+    diag_far[0], kv_pair, *state = lax.optimization_barrier((diag_far[0], kv_pair, *state))
     bits = n_far // 4
     while bits:
         diag_far.append(along([diag] + diag_far, bits))
         bits //= 2
     state = call(
-        [(0, own_book, pieces(*z_far[1:]), True), (half, other_book, y_near + pieces(diag, diag_far[0]), False)],
+        [
+            (0, own_book, pieces(*z_far[1:]), True),
+            (half, other_book, y_near + pieces(diag, diag_far[0], y_first), False),
+        ],
         stretch=kv_pair, state=state, final=False,
     )
     out, out_send = call(
-        [(0, own_book, pieces(x_far), True), (half, other_book, pieces(*diag_far[1:], y_far), True)],
+        [(0, own_book, pieces(x_rest), True), (half, other_book, pieces(*diag_far[1:], y_rest), True)],
         stretch=None, state=state, final=True,
     )
     out_mate = swap(out_send, 1)
-    return lay_out(
-        jnp.concatenate([order(core), order(1 - core)]),
-        [out],
-        [out_mate],
-        tokens,
-        group,
-    )
+    return lay_out(place, out_mate, True, lay_out(place, out, False, None))
 
 
 def rotate(tensor, position):
@@ -569,7 +566,7 @@
         fits = (
             n_inner == 2
             and n_outer % 4 == 0
-            and 1 < far
+            and 4 <= far
             and far & (far - 1) == 0
             and n_outer <= 128
             and key_codes.shape[1] % 2 == 0

time: 57.7 us -> 56 us (0.971)
  starting transfers between devices: 13.7 us -> 17.7 us
  local copies, waits for them, and re-layouts: 4.87 us -> 1.06 us
  waiting for transfers between devices: 15.1 us -> 11.3 us
  Pallas kernels: 22.5 us -> 24.6 us
    ppermute x13 -> x14, starting transfers between devices: 13.7 us -> 17.7 us  [swap(): lax.ppermute(x, axes, [(2 * o + i, 2 * (o ^ outer_bits) + (i ^ inner_bits...]
    ppermute x13 -> x14, waiting for transfers between devices: 15.1 us -> 11.3 us  [swap(): lax.ppermute(x, axes, [(2 * o + i, 2 * (o ^ outer_bits) + (i ^ inner_bits...]
    unnamed x23 -> x14, local copies, waits for them, and re-layouts: 3.75 us -> 0.09 us
    pallas_call x3, Pallas kernels: 4.46 us -> 5.91 us  [the longest x1 3.18 us: prepare(): pl.pallas_call(kernel, out_shape=(shape, shape), in_specs=[whole(pltpu.SM...]
    dynamic_slice x1, local copies, waits for them, and re-layouts: 0.01 us -> 0.91 us  [paired(): lax.dynamic_slice_in_dim(codebooks, core * half, half, 0)]
    dynamic_slice x1 -> x0, local copies, waits for them, and re-layouts: 0.82 us -> none  [paired(): sine = lax.dynamic_slice_in_dim(sine, inner * tokens, tokens, 0)]
    pallas_call x3, Pallas kernels: 18 us -> 18.7 us  [attend(): pl.pallas_call(kernel, out_shape=out_shape, in_specs=[whole(pltpu.SMEM)]...]
  transfers between devices with their start and end apart: 13 -> 14, of which waited for: 9 -> 5; matrix products, arithmetic and copies ran while one was open for 3% -> 2% of each run, Pallas kernels for 17% -> 24%
where the time goes in v3:
time: 56 us; the launch traced here: 55.8 us
  Pallas kernels  24.6 us (44%)
  starting transfers between devices  17.7 us (32%)
  waiting for transfers between devices  11.3 us (20%)
  local copies, waits for them, and re-layouts  1.06 us (2%)
  between operations  0.98 us (2%)
    pallas_call x3, Pallas kernels, attend(): pl.pallas_call(kernel, out_shape=out_shape, in_specs=[whole(pltpu.SMEM)]...  18.7 us
    ppermute x14, starting transfers between devices, swap(): lax.ppermute(x, axes, [(2 * o + i, 2 * (o ^ outer_bits) + (i ^ inner_bits...  17.7 us
    ppermute x14, waiting for transfers between devices, swap(): lax.ppermute(x, axes, [(2 * o + i, 2 * (o ^ outer_bits) + (i ^ inner_bits...  11.3 us
    pallas_call x1, Pallas kernels, prepare(): pl.pallas_call(kernel, out_shape=(shape, shape), in_specs=[whole(pltpu.SM...  3.18 us
    pallas_call x2, Pallas kernels, lay_out(): pl.pallas_call(kernel, out_shape=jax.ShapeDtypeStruct((tokens, 2 * n_out,...  2.73 us
  transfers between devices with their start and end apart: 14, of which 5 were waited for; matrix products, arithmetic and copies ran while one was open for 2% of the time, Pallas kernels for 24%

profile of v3, /device:TPU:0, one launch (start us, length us, event | category | flops | bytes accessed | tf_op | source)
XLA Modules:
  0.0 55.8 jit_solution(4596766164371003546)
XLA Ops:
  0.7 0.1 pad_add_fusion.place
  0.7 0.0 copy-start
  0.7 0.0 copy-start.1
  0.7 0.0 copy-start.2
  0.7 0.0 copy-start.3
  0.7 0.0 copy-start.4
  0.8 3.2 %prepare.1 = (bf16[2864,128]{1,0:T(8,128)(2,1)S(1)}, bf16[2864,128]{1,0:T(8,128)(2,1)S(1)}) custom-call(s32[2]{0:T(128)S(1)} %pad_add_fusion.place, s32[1]{0:T(128)S(6)} %copy.29.ids, s32[4,16,128]{2,1,0:T(8,128)} %bitcast.8, bf16[128,4,128]{2,1,0:T(4,128)(2,1)} %refs_1_.1, f32[4,128]{1,0:T(4,128)} %bitcast.9, bf16[64,10,8,128]{3,2,1,0:T(8,128)(2,1)} %bitcast.6, ...), custom_call_target="tpu_custom_call" | custom-call | tf_op jit(solution)/shard_map/prepare/pallas_call | solution.py:108
  3.9 0.5 collective-permute-start
  4.5 0.9 %constant_dynamic-slice_fusion = bf16[2,256,128]{2,1,0:T(8,128)(2,1)S(1)} fusion(bf16[4,256,128]{2,1,0:T(8,128)(2,1)} %refs_0_.5, s32[]{:T(128)S(6)} %select_n.11), kind=kLoop, calls=%fused_computation.14 | loop fusion | bytes 262148 | tf_op jit(solution)/shard_map/dynamic_slice | solution.py:403
  5.4 0.9 %collective-permute-done.refs_10_.refs_11_ = bf16[2864,128]{1,0:T(8,128)(2,1)S(1)} collective-permute-done((bf16[2864,128]{1,0:T(8,128)(2,1)S(1)}, bf16[2864,128]{1,0:T(8,128)(2,1)S(1)}, u32[]{:S(2)}, u32[]{:S(2)}) %collective-permute-start) | collective-permute-done | bytes 733216 | tf_op jit(solution)/shard_map/ppermute | solution.py:375
  6.4 4.0 %collective-permute-start.1 = (bf16[592,128]{1,0:T(8,128)(2,1)S(1)}, bf16[592,128]{1,0:T(8,128)(2,1)S(1)}, u32[]{:S(2)}, u32[]{:S(2)}) collective-permute-start(bf16[592,128]{1,0:T(8,128)(2,1)S(1)} %pad_maximum_fusion.2.refs_1_), channel_id=1, source_target_pairs={{0,16},{1,17},{2,18},{3,19},{4,20},{5,21},{6,22},{7,23},{8,24},{9,... | collective-permute-start | bytes 454664 | tf_op jit(solution)/shard_map/ppermute | solution.py:375
  10.4 2.4 %collective-permute-start.2 = (bf16[592,128]{1,0:T(8,128)(2,1)S(1)}, bf16[592,128]{1,0:T(8,128)(2,1)S(1)}, u32[]{:S(2)}, u32[]{:S(2)}) collective-permute-start(bf16[592,128]{1,0:T(8,128)(2,1)S(1)} %pad_maximum_fusion.2.refs_1_), channel_id=1, source_target_pairs={{0,5},{1,4},{2,7},{3,6},{4,1},{5,0},{6,3},{7,2},{8,13},{9,12},{10,... | collective-permute-start | bytes 454664 | tf_op jit(solution)/shard_map/ppermute | solution.py:375
  12.9 0.6 %collective-permute-start.6 = (bf16[1104,128]{1,0:T(8,128)(2,1)S(1)}, bf16[1104,128]{1,0:T(8,128)(2,1)S(1)}, u32[]{:S(2)}, u32[]{:S(2)}) collective-permute-start(bf16[1104,128]{1,0:T(8,128)(2,1)S(1)} %constant_dynamic-update-slice_fusion.5), channel_id=1, source_target_pairs={{0,1},{1,0},{2,3},{3,2},{4,5},{5,4},{6,7},{7,6},{8,9},{9,8},{10,11... | collective-permute-start | bytes 847880 | tf_op jit(solution)/shard_map/ppermute | solution.py:375
  13.5 0.6 %collective-permute-start.9 = (bf16[592,128]{1,0:T(8,128)(2,1)S(1)}, bf16[592,128]{1,0:T(8,128)(2,1)S(1)}, u32[]{:S(2)}, u32[]{:S(2)}) collective-permute-start(bf16[592,128]{1,0:T(8,128)(2,1)S(1)} %pad_maximum_fusion.2.refs_1_), channel_id=1, source_target_pairs={{0,4},{1,5},{2,6},{3,7},{4,0},{5,1},{6,2},{7,3},{8,12},{9,13},{10,... | collective-permute-start | bytes 454664 | tf_op jit(solution)/shard_map/ppermute | solution.py:375
  14.1 3.8 %collective-permute-done.1.refs_3_ = bf16[592,128]{1,0:T(8,128)(2,1)S(1)} collective-permute-done((bf16[592,128]{1,0:T(8,128)(2,1)S(1)}, bf16[592,128]{1,0:T(8,128)(2,1)S(1)}, u32[]{:S(2)}, u32[]{:S(2)}) %collective-permute-start.1) | collective-permute-done | bytes 151584 | tf_op jit(solution)/shard_map/ppermute | solution.py:375
  17.9 0.0 collective-permute-done.2.refs_3_
  17.9 1.8 %collective-permute-start.10 = (bf16[592,128]{1,0:T(8,128)(2,1)S(1)}, bf16[592,128]{1,0:T(8,128)(2,1)S(1)}, u32[]{:S(2)}, u32[]{:S(2)}) collective-permute-start(bf16[592,128]{1,0:T(8,128)(2,1)S(1)} %collective-permute-done.1.refs_3_), channel_id=1, source_target_pairs={{0,4},{1,5},{2,6},{3,7},{4,0},{5,1},{6,2},{7,3},{8,12},{9,13},{10,... | collective-permute-start | bytes 454664 | tf_op jit(solution)/shard_map/ppermute | solution.py:375
  19.7 1.6 %collective-permute-start.3 = (bf16[1184,128]{1,0:T(8,128)(2,1)S(1)}, bf16[1184,128]{1,0:T(8,128)(2,1)S(1)}, u32[]{:S(2)}, u32[]{:S(2)}) collective-permute-start(bf16[1184,128]{1,0:T(8,128)(2,1)S(1)} %constant_dynamic-update-slice_fusion), channel_id=1, source_target_pairs={{0,8},{1,9},{2,10},{3,11},{4,12},{5,13},{6,14},{7,15},{8,0},{9,1},... | collective-permute-start | bytes 909320 | tf_op jit(solution)/shard_map/ppermute | solution.py:375
  21.3 1.7 %collective-permute-done.6.refs_2_ = bf16[1104,128]{1,0:T(8,128)(2,1)S(1)} collective-permute-done((bf16[1104,128]{1,0:T(8,128)(2,1)S(1)}, bf16[1104,128]{1,0:T(8,128)(2,1)S(1)}, u32[]{:S(2)}, u32[]{:S(2)}) %collective-permute-start.6) | collective-permute-done | bytes 282656 | tf_op jit(solution)/shard_map/ppermute | solution.py:375
  23.1 1.5 %collective-permute-start.8 = (bf16[1024,128]{1,0:T(8,128)(2,1)S(1)}, bf16[1024,128]{1,0:T(8,128)(2,1)S(1)}, u32[]{:S(2)}, u32[]{:S(2)}) collective-permute-start(bf16[1024,128]{1,0:T(8,128)(2,1)S(1)} %pad_maximum_fusion.1), channel_id=1, source_target_pairs={{0,1},{1,0},{2,3},{3,2},{4,5},{5,4},{6,7},{7,6},{8,9},{9,8},{10,11... | collective-permute-start | bytes 786440 | tf_op jit(solution)/shard_map/ppermute | solution.py:375
  24.6 0.5 collective-permute-start.4
  25.1 0.0 collective-permute-done.9.refs_2_
  25.1 0.6 %collective-permute-start.7 = (bf16[592,128]{1,0:T(8,128)(2,1)S(1)}, bf16[592,128]{1,0:T(8,128)(2,1)S(1)}, u32[]{:S(2)}, u32[]{:S(2)}) collective-permute-start(bf16[592,128]{1,0:T(8,128)(2,1)S(1)} %collective-permute-done.2.refs_3_), channel_id=1, source_target_pairs={{0,16},{1,17},{2,18},{3,19},{4,20},{5,21},{6,22},{7,23},{8,24},{9,... | collective-permute-start | bytes 454664 | tf_op jit(solution)/shard_map/ppermute | solution.py:375
  25.7 0.0 collective-permute-done.10.refs_4_
  25.7 0.0 copy-done
  25.7 0.0 copy-done.1
  25.7 0.0 copy-done.2
  25.7 0.0 copy-done.3
  25.7 0.0 copy-done.4
  25.7 4.4 %attend.3 = (f32[4,1024,128]{2,1,0:T(8,128)S(1)}, f32[4,1024,128]{2,1,0:T(8,128)S(1)}, f32[4,1024,128]{2,1,0:T(8,128)S(1)}) custom-call(s32[2]{0:T(128)S(1)} %pad_add_fusion.place, bf16[4,256,128]{2,1,0:T(8,128)(2,1)S(1)} %copy-done, bf16[592,128]{1,0:T(8,128)(2,1)S(1)} %pad_maximum_fusion.2.refs_1_, bf16[592,128]{1,0:T(8,128)(2,1)S(1)} %collective-permute-done.9.refs_2_, ...), custom_call_target="tpu_custom_call" | custom-call | flops 2147483648 | bytes 4194304 | tf_op jit(solution)/shard_map/attend/pallas_call | solution.py:318
  30.2 4.3 %collective-permute-done.4.refs_5_ = bf16[592,128]{1,0:T(8,128)(2,1)S(1)} collective-permute-done((bf16[592,128]{1,0:T(8,128)(2,1)S(1)}, bf16[592,128]{1,0:T(8,128)(2,1)S(1)}, u32[]{:S(2)}, u32[]{:S(2)}) %collective-permute-start.4) | collective-permute-done | bytes 151584 | tf_op jit(solution)/shard_map/ppermute | solution.py:375
  34.5 0.0 collective-permute-done.3.refs_1_
  34.5 1.5 %collective-permute-start.12 = (bf16[1184,128]{1,0:T(8,128)(2,1)S(1)}, bf16[1184,128]{1,0:T(8,128)(2,1)S(1)}, u32[]{:S(2)}, u32[]{:S(2)}) collective-permute-start(bf16[1184,128]{1,0:T(8,128)(2,1)S(1)} %collective-permute-done.3.refs_1_), channel_id=1, source_target_pairs={{0,1},{1,0},{2,3},{3,2},{4,5},{5,4},{6,7},{7,6},{8,9},{9,8},{10,11... | collective-permute-start | bytes 909320 | tf_op jit(solution)/shard_map/ppermute | solution.py:375
  36.1 0.3 collective-permute-start.5
  36.3 0.0 collective-permute-done.7.refs_4_
  36.3 0.0 collective-permute-done.8.refs_12_
  36.3 1.6 %collective-permute-start.11 = (bf16[1184,128]{1,0:T(8,128)(2,1)S(1)}, bf16[1184,128]{1,0:T(8,128)(2,1)S(1)}, u32[]{:S(2)}, u32[]{:S(2)}) collective-permute-start(bf16[1184,128]{1,0:T(8,128)(2,1)S(1)} %pad_maximum_fusion), channel_id=1, source_target_pairs={{0,8},{1,9},{2,10},{3,11},{4,12},{5,13},{6,14},{7,15},{8,0},{9,1},... | collective-permute-start | bytes 909320 | tf_op jit(solution)/shard_map/ppermute | solution.py:375
  38.0 7.5 %attend.4 = (f32[4,1024,128]{2,1,0:T(8,128)S(1)}, f32[4,1024,128]{2,1,0:T(8,128)S(1)}, f32[4,1024,128]{2,1,0:T(8,128)S(1)}) custom-call(s32[2]{0:T(128)S(1)} %pad_add_fusion.place, bf16[4,256,128]{2,1,0:T(8,128)(2,1)S(1)} %copy-done, ...), custom_call_target="tpu_custom_call", output_to_operand_aliasing={{0}: (14, {}), {1}: (15, {}), {2}: (16, {})} | custom-call | flops 3758096384 | bytes 4194304 | tf_op jit(solution)/shard_map/attend/pallas_call | solution.py:318
  45.5 0.0 collective-permute-done.12.refs_4_
  45.5 0.0 collective-permute-done.5.refs_1_
  45.5 0.0 collective-permute-done.11.refs_3_
  45.5 6.8 %attend.5 = (bf16[4,64,8,128]{3,2,1,0:T(8,128)(2,1)S(1)}, bf16[4,64,8,128]{3,2,1,0:T(8,128)(2,1)S(1)}) custom-call(s32[2]{0:T(128)S(1)} %pad_add_fusion.place, bf16[4,256,128]{2,1,0:T(8,128)(2,1)S(1)} %copy-done, bf16[1184,128]{1,0:T(8,128)(2,1)S(1)} %collective-permute-done.5.refs_1_, bf16[1104,128]{1,0:T(8,128)(2,1)S(1)} %collective-permute-done.6.refs_2_, ...), custom_call_target="tpu_custom_call" | custom-call | flops 3221225472 | bytes 4194304 | tf_op jit(solution)/shard_map/attend/pallas_call | solution.py:318
  52.3 0.1 collective-permute-start.13
  52.4 1.4 %lay_out.2.refs_0_ = bf16[64,8,8,128]{3,2,1,0:T(8,128)(2,1)} custom-call(s32[2]{0:T(128)S(1)} %pad_add_fusion.place, bf16[4,64,8,128]{3,2,1,0:T(8,128)(2,1)S(1)} %get-tuple-element.46.source), custom_call_target="tpu_custom_call" | custom-call | tf_op jit(solution)/shard_map/lay_out/pallas_call | solution.py:349
  53.8 0.5 collective-permute-done.13.source
  54.3 1.4 %lay_out.3 = bf16[64,8,8,128]{3,2,1,0:T(8,128)(2,1)} custom-call(s32[2]{0:T(128)S(1)} %pad_add_fusion.place, bf16[4,64,8,128]{3,2,1,0:T(8,128)(2,1)S(1)} %collective-permute-done.13.source, bf16[64,8,8,128]{3,2,1,0:T(8,128)(2,1)} %lay_out.2.refs_0_), custom_call_target="tpu_custom_call", output_to_operand_aliasing={{}: (2, {})} | custom-call | tf_op jit(solution)/shard_map/lay_out/pallas_call | solution.py:349
  (11 shorter events, 0.2 us)
Async XLA Ops:
  0.7 25.0 %copy-start = (bf16[4,256,128]{2,1,0:T(8,128)(2,1)S(1)}, bf16[4,256,128]{2,1,0:T(8,128)(2,1)}, u32[]{:S(2)}) copy-start(bf16[4,256,128]{2,1,0:T(8,128)(2,1)} %refs_0_.5) | copy-start | bytes 786436
  0.7 25.0 %copy-start.1 = (f32[64,128]{1,0:T(8,128)S(1)}, f32[64,128]{1,0:T(8,128)}, u32[]{:S(2)}) copy-start(f32[64,128]{1,0:T(8,128)} %constant.38.clone.refs_5_.refs_6_) | copy-start | bytes 98308
  0.7 25.0 %copy-start.2 = (f32[64,128]{1,0:T(8,128)S(1)}, f32[64,128]{1,0:T(8,128)}, u32[]{:S(2)}) copy-start(f32[64,128]{1,0:T(8,128)} %constant.39.clone.refs_6_.refs_7_) | copy-start | bytes 98308
  0.7 25.0 %copy-start.3 = (f32[64,128]{1,0:T(8,128)S(1)}, f32[64,128]{1,0:T(8,128)}, u32[]{:S(2)}) copy-start(f32[64,128]{1,0:T(8,128)} %constant.40.clone.refs_7_.refs_8_) | copy-start | bytes 98308
  0.7 25.0 %copy-start.4 = (f32[64,128]{1,0:T(8,128)S(1)}, f32[64,128]{1,0:T(8,128)}, u32[]{:S(2)}) copy-start(f32[64,128]{1,0:T(8,128)} %constant.41.clone.refs_8_.refs_9_) | copy-start | bytes 98308
  3.9 2.4 %collective-permute-start = (bf16[2864,128]{1,0:T(8,128)(2,1)S(1)}, bf16[2864,128]{1,0:T(8,128)(2,1)S(1)}, u32[]{:S(2)}, u32[]{:S(2)}) collective-permute-start(bf16[2864,128]{1,0:T(8,128)(2,1)S(1)} %get-tuple-element.27), channel_id=1, source_target_pairs={{0,2},{1,3},{2,0},{3,1},{4,6},{5,7},{6,4},{7,5},{8,10},{9,11},{10,... | collective-permute-start | bytes 2199560 | tf_op jit(solution)/shard_map/ppermute | solution.py:375
  6.4 11.5 %collective-permute-start.1 = (bf16[592,128]{1,0:T(8,128)(2,1)S(1)}, bf16[592,128]{1,0:T(8,128)(2,1)S(1)}, u32[]{:S(2)}, u32[]{:S(2)}) collective-permute-start(bf16[592,128]{1,0:T(8,128)(2,1)S(1)} %pad_maximum_fusion.2.refs_1_), channel_id=1, source_target_pairs={{0,16},{1,17},{2,18},{3,19},{4,20},{5,21},{6,22},{7,23},{8,24},{9,... | collective-permute-start | bytes 454664 | tf_op jit(solution)/shard_map/ppermute | solution.py:375
  10.4 7.5 %collective-permute-start.2 = (bf16[592,128]{1,0:T(8,128)(2,1)S(1)}, bf16[592,128]{1,0:T(8,128)(2,1)S(1)}, u32[]{:S(2)}, u32[]{:S(2)}) collective-permute-start(bf16[592,128]{1,0:T(8,128)(2,1)S(1)} %pad_maximum_fusion.2.refs_1_), channel_id=1, source_target_pairs={{0,5},{1,4},{2,7},{3,6},{4,1},{5,0},{6,3},{7,2},{8,13},{9,12},{10,... | collective-permute-start | bytes 454664 | tf_op jit(solution)/shard_map/ppermute | solution.py:375
  12.9 10.2 %collective-permute-start.6 = (bf16[1104,128]{1,0:T(8,128)(2,1)S(1)}, bf16[1104,128]{1,0:T(8,128)(2,1)S(1)}, u32[]{:S(2)}, u32[]{:S(2)}) collective-permute-start(bf16[1104,128]{1,0:T(8,128)(2,1)S(1)} %constant_dynamic-update-slice_fusion.5), channel_id=1, source_target_pairs={{0,1},{1,0},{2,3},{3,2},{4,5},{5,4},{6,7},{7,6},{8,9},{9,8},{10,11... | collective-permute-start | bytes 847880 | tf_op jit(solution)/shard_map/ppermute | solution.py:375
  13.5 11.6 %collective-permute-start.9 = (bf16[592,128]{1,0:T(8,128)(2,1)S(1)}, bf16[592,128]{1,0:T(8,128)(2,1)S(1)}, u32[]{:S(2)}, u32[]{:S(2)}) collective-permute-start(bf16[592,128]{1,0:T(8,128)(2,1)S(1)} %pad_maximum_fusion.2.refs_1_), channel_id=1, source_target_pairs={{0,4},{1,5},{2,6},{3,7},{4,0},{5,1},{6,2},{7,3},{8,12},{9,13},{10,... | collective-permute-start | bytes 454664 | tf_op jit(solution)/shard_map/ppermute | solution.py:375
  17.9 7.8 %collective-permute-start.10 = (bf16[592,128]{1,0:T(8,128)(2,1)S(1)}, bf16[592,128]{1,0:T(8,128)(2,1)S(1)}, u32[]{:S(2)}, u32[]{:S(2)}) collective-permute-start(bf16[592,128]{1,0:T(8,128)(2,1)S(1)} %collective-permute-done.1.refs_3_), channel_id=1, source_target_pairs={{0,4},{1,5},{2,6},{3,7},{4,0},{5,1},{6,2},{7,3},{8,12},{9,13},{10,... | collective-permute-start | bytes 454664 | tf_op jit(solution)/shard_map/ppermute | solution.py:375
  19.7 14.9 %collective-permute-start.3 = (bf16[1184,128]{1,0:T(8,128)(2,1)S(1)}, bf16[1184,128]{1,0:T(8,128)(2,1)S(1)}, u32[]{:S(2)}, u32[]{:S(2)}) collective-permute-start(bf16[1184,128]{1,0:T(8,128)(2,1)S(1)} %constant_dynamic-update-slice_fusion), channel_id=1, source_target_pairs={{0,8},{1,9},{2,10},{3,11},{4,12},{5,13},{6,14},{7,15},{8,0},{9,1},... | collective-permute-start | bytes 909320 | tf_op jit(solution)/shard_map/ppermute | solution.py:375
  23.1 13.3 %collective-permute-start.8 = (bf16[1024,128]{1,0:T(8,128)(2,1)S(1)}, bf16[1024,128]{1,0:T(8,128)(2,1)S(1)}, u32[]{:S(2)}, u32[]{:S(2)}) collective-permute-start(bf16[1024,128]{1,0:T(8,128)(2,1)S(1)} %pad_maximum_fusion.1), channel_id=1, source_target_pairs={{0,1},{1,0},{2,3},{3,2},{4,5},{5,4},{6,7},{7,6},{8,9},{9,8},{10,11... | collective-permute-start | bytes 786440 | tf_op jit(solution)/shard_map/ppermute | solution.py:375
  24.6 10.0 %collective-permute-start.4 = (bf16[592,128]{1,0:T(8,128)(2,1)S(1)}, bf16[592,128]{1,0:T(8,128)(2,1)S(1)}, u32[]{:S(2)}, u32[]{:S(2)}) collective-permute-start(bf16[592,128]{1,0:T(8,128)(2,1)S(1)} %collective-permute-done.1.refs_3_), channel_id=1, source_target_pairs={{0,1},{1,0},{2,3},{3,2},{4,5},{5,4},{6,7},{7,6},{8,9},{9,8},{10,11... | collective-permute-start | bytes 454664 | tf_op jit(solution)/shard_map/ppermute | solution.py:375
  25.1 11.2 %collective-permute-start.7 = (bf16[592,128]{1,0:T(8,128)(2,1)S(1)}, bf16[592,128]{1,0:T(8,128)(2,1)S(1)}, u32[]{:S(2)}, u32[]{:S(2)}) collective-permute-start(bf16[592,128]{1,0:T(8,128)(2,1)S(1)} %collective-permute-done.2.refs_3_), channel_id=1, source_target_pairs={{0,16},{1,17},{2,18},{3,19},{4,20},{5,21},{6,22},{7,23},{8,24},{9,... | collective-permute-start | bytes 454664 | tf_op jit(solution)/shard_map/ppermute | solution.py:375
  34.5 11.0 %collective-permute-start.12 = (bf16[1184,128]{1,0:T(8,128)(2,1)S(1)}, bf16[1184,128]{1,0:T(8,128)(2,1)S(1)}, u32[]{:S(2)}, u32[]{:S(2)}) collective-permute-start(bf16[1184,128]{1,0:T(8,128)(2,1)S(1)} %collective-permute-done.3.refs_1_), channel_id=1, source_target_pairs={{0,1},{1,0},{2,3},{3,2},{4,5},{5,4},{6,7},{7,6},{8,9},{9,8},{10,11... | collective-permute-start | bytes 909320 | tf_op jit(solution)/shard_map/ppermute | solution.py:375
  36.1 9.5 %collective-permute-start.5 = (bf16[1184,128]{1,0:T(8,128)(2,1)S(1)}, bf16[1184,128]{1,0:T(8,128)(2,1)S(1)}, u32[]{:S(2)}, u32[]{:S(2)}) collective-permute-start(bf16[1184,128]{1,0:T(8,128)(2,1)S(1)} %collective-permute-done.3.refs_1_), channel_id=1, source_target_pairs={{0,4},{1,5},{2,6},{3,7},{4,0},{5,1},{6,2},{7,3},{8,12},{9,13},{10,... | collective-permute-start | bytes 909320 | tf_op jit(solution)/shard_map/ppermute | solution.py:375
  36.3 9.2 %collective-permute-start.11 = (bf16[1184,128]{1,0:T(8,128)(2,1)S(1)}, bf16[1184,128]{1,0:T(8,128)(2,1)S(1)}, u32[]{:S(2)}, u32[]{:S(2)}) collective-permute-start(bf16[1184,128]{1,0:T(8,128)(2,1)S(1)} %pad_maximum_fusion), channel_id=1, source_target_pairs={{0,8},{1,9},{2,10},{3,11},{4,12},{5,13},{6,14},{7,15},{8,0},{9,1},... | collective-permute-start | bytes 909320 | tf_op jit(solution)/shard_map/ppermute | solution.py:375
  52.3 2.0 %collective-permute-start.13 = (bf16[4,64,8,128]{3,2,1,0:T(8,128)(2,1)S(1)}, bf16[4,64,8,128]{3,2,1,0:T(8,128)(2,1)S(1)}, u32[]{:S(2)}, u32[]{:S(2)}) collective-permute-start(bf16[4,64,8,128]{3,2,1,0:T(8,128)(2,1)S(1)} %get-tuple-element.45), channel_id=1, source_target_pairs={{0,2},{1,3},{2,0},{3,1},{4,6},{5,7},{6,4},{7,5},{8,10},{9,11},{10,... | collective-permute-start | bytes 1572872 | tf_op jit(solution)/shard_map/ppermute | solution.py:375

commit v4 on v3

--- a/solution.py
+++ b/solution.py
@@ -133,7 +133,7 @@
     kv_at = q_at + n_heads * q_rows
     lengths = [sum(len(blocks) for _, blocks in pieces) * rows for _, _, pieces, _ in groups_of]
     extra = 2 * tokens if stretch is not None else 0
-    chunk = 768
+    chunk = 512
 
     operands, where = [], {}
 
@@ -149,7 +149,7 @@
     ]
     table_at = [ref_of(t) for t in tables]
     query_at = [ref_of(q) for q in queries]
-    stretch_at = ref_of(stretch) if stretch is not None else None
+    stretch_at = ref_of(stretch[0]) if stretch is not None else None
     n_plain = len(operands)
     if state is not None:
         operands += list(state)
@@ -168,57 +168,63 @@
         requests = [given[i] for i in query_at]
         other = given[stretch_at] if stretch is not None else None
 
-        def decode(group_index):
+        def load_books(group_index):
             first, book_at, book_row, pieces = plan[group_index]
-            kt, vv, book = kts[group_index], vvs[group_index], given[book_at]
+            book = given[book_at]
             for k in range(half):
                 if book_row is None:
                     entries = book[core * half + k]
                 else:
                     entries = book[book_row + k * codes : book_row + (k + 1) * codes, :]
-                tab[k] = entries.astype(f32).T
-            index = 0
-            for at, blocks in pieces:
-                ref = given[at]
-                for value_row, code_row, id_row in blocks:
-                    base = id_row - id_row % 16
-                    block = ref[base : base + 16, :].astype(f32)
-                    block = block[id_row % 16 : id_row % 16 + 8].astype(jnp.int32)
-                    block = jnp.broadcast_to(block[None], (half_dim // 8, 8, head_dim)).reshape(half_dim, head_dim)
-                    cb = jnp.take_along_axis(cos_blk[...], block, axis=1, mode="promise_in_bounds")
-                    sb = jnp.take_along_axis(sin_blk[...], block, axis=1, mode="promise_in_bounds")
-                    ct, st = cos_tok[...], sin_tok[...]
-                    cos = cb * ct - sb * st
-                    sin = sb * ct + cb * st
-                    span = slice(index * rows, (index + 1) * rows)
-                    for k in range(half):
-                        code = ref[code_row + k * groups : code_row + (k + 1) * groups, :].astype(f32).astype(jnp.int32)
-                        code = jnp.broadcast_to(code[:, None, :], (groups, gd, rows)).reshape(head_dim, rows)
-                        low = code & 127
-                        key = jnp.take_along_axis(tab[k, :, :128], low, axis=1, mode="promise_in_bounds")
-                        for part in range(1, codes // 128):
-                            entries = tab[k, :, part * 128 : (part + 1) * 128]
-                            more = jnp.take_along_axis(entries, low, axis=1, mode="promise_in_bounds")
-                            key = jnp.where(code >= part * 128, more, key)
-                        a, b = key[:half_dim], key[half_dim:]
-                        key = jnp.concatenate([a * cos - b * sin, b * cos + a * sin], axis=0).astype(bf16)
-                        kt[k, :head_dim, span] = key
-                        kt[k, head_dim:, span] = key
-                        vv[k, span, :] = ref[value_row + k * rows : value_row + (k + 1) * rows, :]
-                    index += 1
+                tab[group_index * half + k] = entries.astype(f32).T
+
+        def decode(group_index, index, at, value_row, code_row, id_row):
+            kt, vv, ref = kts[group_index], vvs[group_index], given[at]
+            base = id_row - id_row % 16
+            block = ref[base : base + 16, :].astype(f32)
+            block = block[id_row % 16 : id_row % 16 + 8].astype(jnp.int32)
+            block = jnp.broadcast_to(block[None], (half_dim // 8, 8, head_dim)).reshape(half_dim, head_dim)
+            cb = jnp.take_along_axis(cos_blk[...], block, axis=1, mode="promise_in_bounds")
+            sb = jnp.take_along_axis(sin_blk[...], block, axis=1, mode="promise_in_bounds")
+            ct, st = cos_tok[...], sin_tok[...]
+            cos = cb * ct - sb * st
+            sin = sb * ct + cb * st
+            span = slice(index * rows, (index + 1) * rows)
+            for k in range(half):
+                table = group_index * half + k
+                code = ref[code_row + k * groups : code_row + (k + 1) * groups, :].astype(f32).astype(jnp.int32)
+                code = jnp.broadcast_to(code[:, None, :], (groups, gd, rows)).reshape(head_dim, rows)
+                low = code & 127
+                key = jnp.take_along_axis(tab[table, :, :128], low, axis=1, mode="promise_in_bounds")
+                for part in range(1, codes // 128):
+                    entries = tab[table, :, part * 128 : (part + 1) * 128]
+                    more = jnp.take_along_axis(entries, low, axis=1, mode="promise_in_bounds")
+                    key = jnp.where(code >= part * 128, more, key)
+                a, b = key[:half_dim], key[half_dim:]
+                key = jnp.concatenate([a * cos - b * sin, b * cos + a * sin], axis=0).astype(bf16)
+                kt[k, :head_dim, span] = key
+                kt[k, head_dim:, span] = key
+                vv[k, span, :] = ref[value_row + k * rows : value_row + (k + 1) * rows, :]
+
+        def blocks_in(group_index):
+            every = [(at, *block) for at, blocks in plan[group_index][3] for block in blocks]
+            return [functools.partial(decode, group_index, i, *block) for i, block in enumerate(every)]
 
         for group_index in range(len(plan)):
-            decode(group_index)
-
-        works = [(g, k, e) for g in range(len(plan)) for k in range(half) for e in range(2)]
+            load_books(group_index)
+        for task in blocks_in(0):
+            task()
+        later = blocks_in(1) if len(plan) > 1 else []
+
+        works = [(g, k) for g in range(len(plan)) for k in range(half)]
 
         def parts(work):
             return [(c, min(chunk, lengths[work[0]] - c)) for c in range(0, lengths[work[0]], chunk)]
 
         def scaled_queries(work):
-            g, k, e = work
+            g, k = work
             first = q_at + (plan[g][0] + k) * q_rows
-            scaled = requests[e][first : first + q_rows, :].astype(f32) * scale
+            scaled = jnp.concatenate([ref[first : first + q_rows, :] for ref in requests], axis=0).astype(f32) * scale
             hi = scaled.astype(bf16)
             lo = (scaled - hi.astype(f32)).astype(bf16)
             return jnp.concatenate([hi, lo], axis=1)
@@ -234,23 +240,28 @@
             slot[:, c : c + width] = score
             return fold(top, score)
 
-        def stretch_rows(work, which):
-            g, k, e = work
+        def stretch_rows(work, e, which):
+            g, k = work
             head = plan[g][0] + k
-            base = (e * n_heads + (head + half) % n_heads) * 2 * tokens + which * tokens
+            base = stretch[1] + (e * n_heads + (head + half) % n_heads) * 2 * tokens + which * tokens
             mine = kv_at + head * 2 * tokens + which * tokens
             return jnp.concatenate([other[base : base + tokens, :], requests[e][mine : mine + tokens, :]], axis=0)
 
         def score_stretch(work, q, slot, top):
-            key = stretch_rows(work, 0)
-            key = jnp.concatenate([key, key], axis=1)
-            score = lax.dot_general(q, key, (((1,), (1,)), ((), ())), preferred_element_type=f32)
-            column = lax.broadcasted_iota(jnp.int32, score.shape, 1)
-            row = lax.broadcasted_iota(jnp.int32, score.shape, 0) // group
-            allowed = (column - tokens <= row) & (column >= tokens * (1 - inner))
-            score = jnp.where(allowed, score, -jnp.inf)
-            slot[:, lengths[work[0]] : lengths[work[0]] + extra] = score
-            return fold(top, score)
+            for e in range(2):
+                key = stretch_rows(work, e, 0)
+                key = jnp.concatenate([key, key], axis=1)
+                score = lax.dot_general(
+                    q[e * q_rows : (e + 1) * q_rows], key, (((1,), (1,)), ((), ())), preferred_element_type=f32
+                )
+                column = lax.broadcasted_iota(jnp.int32, score.shape, 1)
+                row = lax.broadcasted_iota(jnp.int32, score.shape, 0) // group
+                allowed = (column - tokens <= row) & (column >= tokens * (1 - inner))
+                tops.append(jnp.where(allowed, score, -jnp.inf))
+                slot[e * q_rows : (e + 1) * q_rows, lengths[work[0]] : lengths[work[0]] + extra] = tops[-1]
+            return fold(top, jnp.concatenate(tops[-2:], axis=0))
+
+        tops = []
 
         def weigh(slot, m, part, mixed, c, width, value):
             weights = []
@@ -259,11 +270,14 @@
                 part = part + weight
                 weights.append(weight.astype(bf16))
             weight = jnp.concatenate(weights, axis=1) if len(weights) > 1 else weights[0]
+            if isinstance(value, list):
+                new = [jnp.dot(weight[i * q_rows : (i + 1) * q_rows], v, preferred_element_type=f32) for i, v in enumerate(value)]
+                return part, mixed + jnp.concatenate(new, axis=0)
             return part, mixed + jnp.dot(weight, value, preferred_element_type=f32)
 
         def place_of(work):
-            g, k, e = work
-            return plan[g][0] + k, slice(e * q_rows, (e + 1) * q_rows), slice(None)
+            g, k = work
+            return plan[g][0] + k
 
         current = None
         for t in range(len(works) + 1):
@@ -278,10 +292,14 @@
                 if work is not None:
                     top = score_stretch(work, q, slot, top)
                 if current is not None:
-                    part, mixed = weigh(old, m, part, mixed, lengths[done[0]], extra, stretch_rows(done, 1))
+                    part, mixed = weigh(old, m, part, mixed, lengths[done[0]], extra, [stretch_rows(done, e, 1) for e in range(2)])
             ahead = parts(work) if work is not None else []
             behind = parts(done) if current is not None else []
+            first_steps = half * len(parts(works[0]))
             for i in range(max(len(ahead), len(behind))):
+                for _ in range(-(-len(blocks_in(1)) // first_steps) if later else 0):
+                    if later:
+                        later.pop(0)()
                 if i < len(ahead):
                     top = score_part(work, q, slot, top, *ahead[i])
                 if i < len(behind):
@@ -291,15 +309,17 @@
                 if final:
                     head = plan[done[0]][0] + done[1]
                     result = mixed / jnp.sum(part, axis=1, keepdims=True)
-                    results[done[2]][head] = result.reshape(tokens, group, head_dim).astype(bf16)
+                    for e in range(2):
+                        result_e = result[e * q_rows : (e + 1) * q_rows].reshape(tokens, group, head_dim)
+                        results[e][head] = result_e.astype(bf16)
                 else:
                     for ref, value in zip(results, (m, part, mixed)):
                         ref[place_of(done)] = value
             if work is not None:
-                m = jnp.broadcast_to(jnp.max(top, axis=1, keepdims=True), (q_rows, 128))
+                m = jnp.broadcast_to(jnp.max(top, axis=1, keepdims=True), (2 * q_rows, 128))
                 if not groups_of[work[0]][3]:
-                    part = jnp.zeros((q_rows, 128), f32)
-                    mixed = jnp.zeros((q_rows, head_dim), f32)
+                    part = jnp.zeros((2 * q_rows, 128), f32)
+                    mixed = jnp.zeros((2 * q_rows, head_dim), f32)
                 else:
                     past = before[0][place_of(work)]
                     m = jnp.maximum(past, m)
@@ -314,7 +334,7 @@
         out_shape = (jax.ShapeDtypeStruct((n_heads, 2 * q_rows, 128), f32),) * 3
     alias = {1 + n_plain + j: j for j in range(3)} if state is not None and not final else {}
     pairs = 2 * half * q_rows * (sum(lengths) + extra * len(plan))
-    slot = pltpu.VMEM((q_rows, max(lengths) + extra), f32)
+    slot = pltpu.VMEM((2 * q_rows, max(lengths) + extra), f32)
     return pl.pallas_call(
         kernel,
         out_shape=out_shape,
@@ -322,7 +342,7 @@
         out_specs=(whole(),) * len(out_shape),
         scratch_shapes=[pltpu.VMEM((half, 2 * head_dim, n), bf16) for n in lengths]
         + [pltpu.VMEM((half, n, head_dim), bf16) for n in lengths]
-        + [pltpu.VMEM((half, head_dim, codes), f32), slot, slot],
+        + [pltpu.VMEM((len(lengths) * half, head_dim, codes), f32), slot, slot],
         input_output_aliases=alias,
         compiler_params=params(megabytes),
         cost_estimate=pl.CostEstimate(flops=8 * pairs * head_dim, bytes_accessed=4 * 2**20, transcendentals=pairs),
@@ -397,22 +417,19 @@
             out.append((b + extent, b + extent + half * rows, b + 2 * extent + 8))
         return out
 
+    my_books = lax.dynamic_slice_in_dim(codebooks, core * half, half, 0).reshape(half * codes, head_dim)
+    own_kv = 2 * half * 2 * tokens
+    stretch = jnp.concatenate([keep[-own_kv:], mate[-own_kv:]], axis=0)
+
     def along(parts, bits):
         return swap(jnp.concatenate(parts, axis=0) if len(parts) > 1 else parts[0], 4 * bits)
 
-    my_books = lax.dynamic_slice_in_dim(codebooks, core * half, half, 0).reshape(half * codes, head_dim)
-    z_far = [along([pack], n_far // 2)]
+    steps = [n_far >> (i + 1) for i in range(n_far.bit_length() - 1)]
+    z_one = [along([pack], bits) for bits in steps]
+    x_pack = swap(pack, 2)
+    y_pack = swap(jnp.concatenate([pack, my_books, stretch], axis=0), 0, 1)
     diag = swap(pack, 2, 1)
-    x_pack = swap(pack, 2)
-    y_pack = swap(jnp.concatenate([pack, my_books], axis=0), 0, 1)
-    z_far[0], diag = lax.optimization_barrier((z_far[0], diag))
-    diag_far = [along([diag], n_far // 2)]
-    bits = n_far // 4
-    while bits:
-        z_far.append(along([pack] + z_far, bits))
-        bits //= 2
-
-    x_first, y_first = swap(z_far[0], 2), swap(z_far[0], 0, 1)
+
     positions = np.arange(rows)
     cos_tok, sin_tok = np.cos(angle_table(positions, head_dim)), np.sin(angle_table(positions, head_dim))
     starts = np.arange(128) * rows
@@ -425,27 +442,32 @@
     def pieces(*arrays):
         return [(a, blocks_of(0, a.shape[0] // size)) for a in arrays]
 
-    own_kv = 2 * half * 2 * tokens
-    kv_own = jnp.concatenate([keep[-own_kv:], mate[-own_kv:]], axis=0)
-    kv_own, y_pack = lax.optimization_barrier((kv_own, y_pack))
-    kv_pair = swap(kv_own, 0, 1)
-    state = call([(0, own_book, pieces(pack, x_pack, z_far[0], x_first), False)], stretch=None, state=None, final=False)
-    other_book, y_near = (y_pack, size), [(y_pack, blocks_of(0))]
-    *z_rest, y_first = lax.optimization_barrier((*z_far[1:], y_first))
-    z_rest = jnp.concatenate(z_rest, axis=0) if len(z_rest) > 1 else z_rest[0]
-    y_rest = swap(z_rest, 0, 1)
-    x_rest = swap(z_rest, 2)
-    diag_far[0], kv_pair, *state = lax.optimization_barrier((diag_far[0], kv_pair, *state))
-    bits = n_far // 4
-    while bits:
+    other_book, other_stretch = (y_pack, size), (y_pack, size + half * codes)
+
+    state = call([(0, own_book, pieces(pack, x_pack, z_one[-1]), False)], stretch=None, state=None, final=False)
+    *z_one, diag, first, second, third = lax.optimization_barrier((*z_one, diag, *state))
+    state = (first, second, third)
+    z_two, reached = [], [z_one[0]]
+    for i, bits in enumerate(steps[1:]):
+        z_two.append(along(reached, bits))
+        reached = reached + [z_one[i + 1], z_two[-1]]
+    diag_far = [along([diag], steps[0])]
+    near = jnp.concatenate(z_one, axis=0)
+    x_near, y_near = swap(near, 2), swap(near, 0, 1)
+    state = call(
+        [(0, own_book, pieces(*z_one[:-1]), True), (half, other_book, [(y_pack, blocks_of(0))] + pieces(diag), False)],
+        stretch=other_stretch, state=state, final=False,
+    )
+
+    z_rest = jnp.concatenate(z_two, axis=0) if len(z_two) > 1 else z_two[0]
+    x_rest, y_rest = swap(z_rest, 2), swap(z_rest, 0, 1)
+    diag_far[0], first, second, third = lax.optimization_barrier((diag_far[0], *state))
+    state = (first, second, third)
+    for bits in steps[1:]:
         diag_far.append(along([diag] + diag_far, bits))
-        bits //= 2
     state = call(
-        [
-            (0, own_book, pieces(*z_far[1:]), True),
-            (half, other_book, y_near + pieces(diag, diag_far[0], y_first), False),
-        ],
-        stretch=kv_pair, state=state, final=False,
+        [(0, own_book, pieces(z_rest, x_near), True), (half, other_book, pieces(diag_far[0], y_near), True)],
+        stretch=None, state=state, final=False,
     )
     out, out_send = call(
         [(0, own_book, pieces(x_rest), True), (half, other_book, pieces(*diag_far[1:], y_rest), True)],

time: 56 us -> 52.3 us (0.934)
  waiting for transfers between devices: 11.3 us -> 4.3 us
  Pallas kernels: 24.6 us -> 26.8 us
  starting transfers between devices: 17.7 us -> 18.9 us
    ppermute x14, waiting for transfers between devices: 11.3 us -> 4.3 us  [swap(): lax.ppermute(x, axes, [(2 * o + i, 2 * (o ^ outer_bits) + (i ^ inner_bits...]
    pallas_call x3 -> x4, Pallas kernels: 18.7 us -> 20.9 us  [attend(): pl.pallas_call(kernel, out_shape=out_shape, in_specs=[whole(pltpu.SMEM)]...]
    ppermute x14, starting transfers between devices: 17.7 us -> 18.9 us  [swap(): lax.ppermute(x, axes, [(2 * o + i, 2 * (o ^ outer_bits) + (i ^ inner_bits...]
  transfers between devices with their start and end apart: 14 -> 14, of which waited for: 5 -> 4; matrix products, arithmetic and copies ran while one was open for 2% -> 2% of each run, Pallas kernels for 24% -> 33%
where the time goes in v4:
time: 52.3 us; the launch traced here: 52.2 us
  Pallas kernels  26.8 us (51%)
  starting transfers between devices  18.9 us (36%)
  waiting for transfers between devices  4.3 us (8%)
  local copies, waits for them, and re-layouts  1.07 us (2%)
  between operations  1.04 us (2%)
    pallas_call x4, Pallas kernels, attend(): pl.pallas_call(kernel, out_shape=out_shape, in_specs=[whole(pltpu.SMEM)]...  20.9 us
    ppermute x14, starting transfers between devices, swap(): lax.ppermute(x, axes, [(2 * o + i, 2 * (o ^ outer_bits) + (i ^ inner_bits...  18.9 us
    ppermute x14, waiting for transfers between devices, swap(): lax.ppermute(x, axes, [(2 * o + i, 2 * (o ^ outer_bits) + (i ^ inner_bits...  4.3 us
    pallas_call x1, Pallas kernels, prepare(): pl.pallas_call(kernel, out_shape=(shape, shape), in_specs=[whole(pltpu.SM...  3.18 us
    pallas_call x2, Pallas kernels, lay_out(): pl.pallas_call(kernel, out_shape=jax.ShapeDtypeStruct((tokens, 2 * n_out,...  2.73 us
  transfers between devices with their start and end apart: 14, of which 4 were waited for; matrix products, arithmetic and copies ran while one was open for 2% of the time, Pallas kernels for 33%

profile of v4, /device:TPU:0, one launch (start us, length us, event | category | flops | bytes accessed | tf_op | source)
XLA Modules:
  0.0 52.2 jit_solution(16663663798148065286)
XLA Ops:
  0.0 0.0 copy-start.1
  0.0 0.0 copy-start.2
  0.0 0.0 copy-start.3
  0.0 0.0 copy-start.4
  0.0 0.0 copy-start
  0.7 0.1 pad_add_fusion.place
  0.8 3.2 %prepare.1 = (bf16[2864,128]{1,0:T(8,128)(2,1)S(1)}, bf16[2864,128]{1,0:T(8,128)(2,1)S(1)}) custom-call(s32[2]{0:T(128)S(1)} %pad_add_fusion.place, s32[1]{0:T(128)S(6)} %copy.34.ids, s32[4,16,128]{2,1,0:T(8,128)} %bitcast.8, bf16[128,4,128]{2,1,0:T(4,128)(2,1)} %refs_1_.1, f32[4,128]{1,0:T(4,128)} %bitcast.9, bf16[64,10,8,128]{3,2,1,0:T(8,128)(2,1)} %bitcast.6, ...), custom_call_target="tpu_custom_call" | custom-call | tf_op jit(solution)/shard_map/prepare/pallas_call | solution.py:108
  4.0 0.5 %collective-permute-start = (bf16[2864,128]{1,0:T(8,128)(2,1)S(1)}, bf16[2864,128]{1,0:T(8,128)(2,1)S(1)}, u32[]{:S(2)}, u32[]{:S(2)}) collective-permute-start(bf16[2864,128]{1,0:T(8,128)(2,1)S(1)} %get-tuple-element.29), channel_id=1, source_target_pairs={{0,2},{1,3},{2,0},{3,1},{4,6},{5,7},{6,4},{7,5},{8,10},{9,11},{10,... | collective-permute-start | bytes 2199560 | tf_op jit(solution)/shard_map/ppermute | solution.py:395
  4.5 0.9 %constant_dynamic-slice_fusion = bf16[2,256,128]{2,1,0:T(8,128)(2,1)S(1)} fusion(bf16[4,256,128]{2,1,0:T(8,128)(2,1)} %refs_0_.7, s32[]{:T(128)S(6)} %select_n.11), kind=kLoop, calls=%fused_computation.12 | loop fusion | bytes 262148 | tf_op jit(solution)/shard_map/dynamic_slice | solution.py:420
  5.4 0.9 %collective-permute-done.refs_9_.refs_11_.refs_10_ = bf16[2864,128]{1,0:T(8,128)(2,1)S(1)} collective-permute-done((bf16[2864,128]{1,0:T(8,128)(2,1)S(1)}, bf16[2864,128]{1,0:T(8,128)(2,1)S(1)}, u32[]{:S(2)}, u32[]{:S(2)}) %collective-permute-start) | collective-permute-done | bytes 733216 | tf_op jit(solution)/shard_map/ppermute | solution.py:395
  6.5 3.0 %collective-permute-start.7 = (bf16[2128,128]{1,0:T(8,128)(2,1)S(1)}, bf16[2128,128]{1,0:T(8,128)(2,1)S(1)}, u32[]{:S(2)}, u32[]{:S(2)}) collective-permute-start(bf16[2128,128]{1,0:T(8,128)(2,1)S(1)} %slice_dynamic-update-slice_fusion), channel_id=1, source_target_pairs={{0,1},{1,0},{2,3},{3,2},{4,5},{5,4},{6,7},{7,6},{8,9},{9,8},{10,11... | collective-permute-start | bytes 1634312 | tf_op jit(solution)/shard_map/ppermute | solution.py:395
  9.4 1.6 %collective-permute-start.2 = (bf16[592,128]{1,0:T(8,128)(2,1)S(1)}, bf16[592,128]{1,0:T(8,128)(2,1)S(1)}, u32[]{:S(2)}, u32[]{:S(2)}) collective-permute-start(bf16[592,128]{1,0:T(8,128)(2,1)S(1)} %pad_maximum_fusion.1.refs_1_), channel_id=1, source_target_pairs={{0,8},{1,9},{2,10},{3,11},{4,12},{5,13},{6,14},{7,15},{8,0},{9,1},... | collective-permute-start | bytes 454664 | tf_op jit(solution)/shard_map/ppermute | solution.py:395
  11.1 1.5 %collective-permute-start.4 = (bf16[592,128]{1,0:T(8,128)(2,1)S(1)}, bf16[592,128]{1,0:T(8,128)(2,1)S(1)}, u32[]{:S(2)}, u32[]{:S(2)}) collective-permute-start(bf16[592,128]{1,0:T(8,128)(2,1)S(1)} %pad_maximum_fusion.1.refs_1_), channel_id=1, source_target_pairs={{0,4},{1,5},{2,6},{3,7},{4,0},{5,1},{6,2},{7,3},{8,12},{9,13},{10,... | collective-permute-start | bytes 454664 | tf_op jit(solution)/shard_map/ppermute | solution.py:395
  12.6 2.6 %collective-permute-start.1 = (bf16[592,128]{1,0:T(8,128)(2,1)S(1)}, bf16[592,128]{1,0:T(8,128)(2,1)S(1)}, u32[]{:S(2)}, u32[]{:S(2)}) collective-permute-start(bf16[592,128]{1,0:T(8,128)(2,1)S(1)} %pad_maximum_fusion.1.refs_1_), channel_id=1, source_target_pairs={{0,16},{1,17},{2,18},{3,19},{4,20},{5,21},{6,22},{7,23},{8,24},{9,... | collective-permute-start | bytes 454664 | tf_op jit(solution)/shard_map/ppermute | solution.py:395
  15.2 0.5 collective-permute-start.3
  15.6 0.0 collective-permute-done.2.refs_3_
  15.6 0.9 %collective-permute-done.4.refs_2_ = bf16[592,128]{1,0:T(8,128)(2,1)S(1)} collective-permute-done((bf16[592,128]{1,0:T(8,128)(2,1)S(1)}, bf16[592,128]{1,0:T(8,128)(2,1)S(1)}, u32[]{:S(2)}, u32[]{:S(2)}) %collective-permute-start.4) | collective-permute-done | bytes 151584 | tf_op jit(solution)/shard_map/ppermute | solution.py:395
  16.5 0.0 copy-done.1
  16.5 0.0 copy-done.2
  16.5 0.0 copy-done.3
  16.5 0.0 copy-done.4
  16.5 0.0 copy-done
  16.5 3.3 %attend.4 = (f32[4,1024,128]{2,1,0:T(8,128)S(1)}, f32[4,1024,128]{2,1,0:T(8,128)S(1)}, f32[4,1024,128]{2,1,0:T(8,128)S(1)}) custom-call(s32[2]{0:T(128)S(1)} %pad_add_fusion.place, bf16[4,256,128]{2,1,0:T(8,128)(2,1)S(1)} %copy-done, bf16[592,128]{1,0:T(8,128)(2,1)S(1)} %pad_maximum_fusion.1.refs_1_, bf16[592,128]{1,0:T(8,128)(2,1)S(1)} %collective-permute-done.4.refs_2_, ...), custom_call_target="tpu_custom_call" | custom-call | flops 1610612736 | bytes 4194304 | tf_op jit(solution)/shard_map/attend/pallas_call | solution.py:338
  19.9 2.0 %collective-permute-done.1.refs_1_ = bf16[592,128]{1,0:T(8,128)(2,1)S(1)} collective-permute-done((bf16[592,128]{1,0:T(8,128)(2,1)S(1)}, bf16[592,128]{1,0:T(8,128)(2,1)S(1)}, u32[]{:S(2)}, u32[]{:S(2)}) %collective-permute-start.1) | collective-permute-done | bytes 151584 | tf_op jit(solution)/shard_map/ppermute | solution.py:395
  21.9 0.0 collective-permute-done.3.refs_3_
  21.9 0.7 %collective-permute-start.11 = (bf16[1184,128]{1,0:T(8,128)(2,1)S(1)}, bf16[1184,128]{1,0:T(8,128)(2,1)S(1)}, u32[]{:S(2)}, u32[]{:S(2)}) collective-permute-start(bf16[1184,128]{1,0:T(8,128)(2,1)S(1)} %constant_dynamic-update-slice_fusion.5), channel_id=1, source_target_pairs={{0,4},{1,5},{2,6},{3,7},{4,0},{5,1},{6,2},{7,3},{8,12},{9,13},{10,... | collective-permute-start | bytes 909320 | tf_op jit(solution)/shard_map/ppermute | solution.py:395
  22.6 0.5 collective-permute-start.12
  23.1 0.3 collective-permute-start.5
  23.4 3.3 %collective-permute-start.8 = (bf16[592,128]{1,0:T(8,128)(2,1)S(1)}, bf16[592,128]{1,0:T(8,128)(2,1)S(1)}, u32[]{:S(2)}, u32[]{:S(2)}) collective-permute-start(bf16[592,128]{1,0:T(8,128)(2,1)S(1)} %collective-permute-done.3.refs_3_), channel_id=1, source_target_pairs={{0,16},{1,17},{2,18},{3,19},{4,20},{5,21},{6,22},{7,23},{8,24},{9,... | collective-permute-start | bytes 454664 | tf_op jit(solution)/shard_map/ppermute | solution.py:395
  26.6 0.0 collective-permute-done.7.refs_2_.refs_3_
  26.6 5.1 %attend.5 = (f32[4,1024,128]{2,1,0:T(8,128)S(1)}, f32[4,1024,128]{2,1,0:T(8,128)S(1)}, f32[4,1024,128]{2,1,0:T(8,128)S(1)}) custom-call(s32[2]{0:T(128)S(1)} %pad_add_fusion.place, bf16[4,256,128]{2,1,0:T(8,128)(2,1)S(1)} %copy-done, ...), custom_call_target="tpu_custom_call", output_to_operand_aliasing={{0}: (11, {}), {1}: (12, {}), {2}: (13, {})} | custom-call | flops 2147483648 | bytes 4194304 | tf_op jit(solution)/shard_map/attend/pallas_call | solution.py:338
  31.7 0.0 collective-permute-done.8.refs_4_
  31.7 1.5 %collective-permute-start.9 = (bf16[1184,128]{1,0:T(8,128)(2,1)S(1)}, bf16[1184,128]{1,0:T(8,128)(2,1)S(1)}, u32[]{:S(2)}, u32[]{:S(2)}) collective-permute-start(bf16[1184,128]{1,0:T(8,128)(2,1)S(1)} %pad_maximum_fusion), channel_id=1, source_target_pairs={{0,8},{1,9},{2,10},{3,11},{4,12},{5,13},{6,14},{7,15},{8,0},{9,1},... | collective-permute-start | bytes 909320 | tf_op jit(solution)/shard_map/ppermute | solution.py:395
  33.2 0.0 collective-permute-done.5.refs_1_
  33.3 1.5 %collective-permute-start.10 = (bf16[592,128]{1,0:T(8,128)(2,1)S(1)}, bf16[592,128]{1,0:T(8,128)(2,1)S(1)}, u32[]{:S(2)}, u32[]{:S(2)}) collective-permute-start(bf16[592,128]{1,0:T(8,128)(2,1)S(1)} %collective-permute-done.5.refs_1_), channel_id=1, source_target_pairs={{0,1},{1,0},{2,3},{3,2},{4,5},{5,4},{6,7},{7,6},{8,9},{9,8},{10,11... | collective-permute-start | bytes 454664 | tf_op jit(solution)/shard_map/ppermute | solution.py:395
  34.8 1.4 %collective-permute-start.6 = (bf16[592,128]{1,0:T(8,128)(2,1)S(1)}, bf16[592,128]{1,0:T(8,128)(2,1)S(1)}, u32[]{:S(2)}, u32[]{:S(2)}) collective-permute-start(bf16[592,128]{1,0:T(8,128)(2,1)S(1)} %collective-permute-done.5.refs_1_), channel_id=1, source_target_pairs={{0,4},{1,5},{2,6},{3,7},{4,0},{5,1},{6,2},{7,3},{8,12},{9,13},{10,... | collective-permute-start | bytes 454664 | tf_op jit(solution)/shard_map/ppermute | solution.py:395
  36.1 0.0 collective-permute-done.11.refs_2_
  36.1 0.0 collective-permute-done.12.refs_5_
  36.1 7.5 %attend.6 = (f32[4,1024,128]{2,1,0:T(8,128)S(1)}, f32[4,1024,128]{2,1,0:T(8,128)S(1)}, f32[4,1024,128]{2,1,0:T(8,128)S(1)}) custom-call(s32[2]{0:T(128)S(1)} %pad_add_fusion.place, bf16[4,256,128]{2,1,0:T(8,128)(2,1)S(1)} %copy-done, ...), custom_call_target="tpu_custom_call", output_to_operand_aliasing={{0}: (13, {}), {1}: (14, {}), {2}: (15, {})} | custom-call | flops 3221225472 | bytes 4194304 | tf_op jit(solution)/shard_map/attend/pallas_call | solution.py:338
  43.6 0.0 collective-permute-done.10.refs_4_
  43.6 0.0 collective-permute-done.6.refs_1_
  43.6 0.0 collective-permute-done.9.refs_3_
  43.6 5.0 %attend.7 = (bf16[4,64,8,128]{3,2,1,0:T(8,128)(2,1)S(1)}, bf16[4,64,8,128]{3,2,1,0:T(8,128)(2,1)S(1)}) custom-call(s32[2]{0:T(128)S(1)} %pad_add_fusion.place, bf16[4,256,128]{2,1,0:T(8,128)(2,1)S(1)} %copy-done, bf16[592,128]{1,0:T(8,128)(2,1)S(1)} %collective-permute-done.6.refs_1_, bf16[2128,128]{1,0:T(8,128)(2,1)S(1)} %collective-permute-done.7.refs_2_.refs_3_, ...), custom_call_target="tpu_custom_call" | custom-call | flops 2147483648 | bytes 4194304 | tf_op jit(solution)/shard_map/attend/pallas_call | solution.py:338
  48.7 0.1 collective-permute-start.13
  48.7 1.4 %lay_out.2.refs_0_ = bf16[64,8,8,128]{3,2,1,0:T(8,128)(2,1)} custom-call(s32[2]{0:T(128)S(1)} %pad_add_fusion.place, bf16[4,64,8,128]{3,2,1,0:T(8,128)(2,1)S(1)} %get-tuple-element.50.source), custom_call_target="tpu_custom_call" | custom-call | tf_op jit(solution)/shard_map/lay_out/pallas_call | solution.py:369
  50.1 0.5 %collective-permute-done.13.source = bf16[4,64,8,128]{3,2,1,0:T(8,128)(2,1)S(1)} collective-permute-done((bf16[4,64,8,128]{3,2,1,0:T(8,128)(2,1)S(1)}, bf16[4,64,8,128]{3,2,1,0:T(8,128)(2,1)S(1)}, u32[]{:S(2)}, u32[]{:S(2)}) %collective-permute-start.13) | collective-permute-done | bytes 524320 | tf_op jit(solution)/shard_map/ppermute | solution.py:395
  50.6 1.4 %lay_out.3 = bf16[64,8,8,128]{3,2,1,0:T(8,128)(2,1)} custom-call(s32[2]{0:T(128)S(1)} %pad_add_fusion.place, bf16[4,64,8,128]{3,2,1,0:T(8,128)(2,1)S(1)} %collective-permute-done.13.source, bf16[64,8,8,128]{3,2,1,0:T(8,128)(2,1)} %lay_out.2.refs_0_), custom_call_target="tpu_custom_call", output_to_operand_aliasing={{}: (2, {})} | custom-call | tf_op jit(solution)/shard_map/lay_out/pallas_call | solution.py:369
  (11 shorter events, 0.2 us)
Async XLA Ops:
  0.0 16.5 %copy-start.1 = (f32[64,128]{1,0:T(8,128)S(1)}, f32[64,128]{1,0:T(8,128)}, u32[]{:S(2)}) copy-start(f32[64,128]{1,0:T(8,128)} %constant.38.clone.refs_4_.refs_6_.refs_5_) | copy-start | bytes 98308
  0.0 16.5 %copy-start.2 = (f32[64,128]{1,0:T(8,128)S(1)}, f32[64,128]{1,0:T(8,128)}, u32[]{:S(2)}) copy-start(f32[64,128]{1,0:T(8,128)} %constant.39.clone.refs_5_.refs_7_.refs_6_) | copy-start | bytes 98308
  0.0 16.5 %copy-start.3 = (f32[64,128]{1,0:T(8,128)S(1)}, f32[64,128]{1,0:T(8,128)}, u32[]{:S(2)}) copy-start(f32[64,128]{1,0:T(8,128)} %constant.40.clone.refs_6_.refs_8_.refs_7_) | copy-start | bytes 98308
  0.0 16.5 %copy-start.4 = (f32[64,128]{1,0:T(8,128)S(1)}, f32[64,128]{1,0:T(8,128)}, u32[]{:S(2)}) copy-start(f32[64,128]{1,0:T(8,128)} %constant.41.clone.refs_7_.refs_9_.refs_8_) | copy-start | bytes 98308
  0.0 16.5 %copy-start = (bf16[4,256,128]{2,1,0:T(8,128)(2,1)S(1)}, bf16[4,256,128]{2,1,0:T(8,128)(2,1)}, u32[]{:S(2)}) copy-start(bf16[4,256,128]{2,1,0:T(8,128)(2,1)} %refs_0_.7) | copy-start | bytes 786436
  4.0 2.4 %collective-permute-start = (bf16[2864,128]{1,0:T(8,128)(2,1)S(1)}, bf16[2864,128]{1,0:T(8,128)(2,1)S(1)}, u32[]{:S(2)}, u32[]{:S(2)}) collective-permute-start(bf16[2864,128]{1,0:T(8,128)(2,1)S(1)} %get-tuple-element.29), channel_id=1, source_target_pairs={{0,2},{1,3},{2,0},{3,1},{4,6},{5,7},{6,4},{7,5},{8,10},{9,11},{10,... | collective-permute-start | bytes 2199560 | tf_op jit(solution)/shard_map/ppermute | solution.py:395
  6.5 20.2 %collective-permute-start.7 = (bf16[2128,128]{1,0:T(8,128)(2,1)S(1)}, bf16[2128,128]{1,0:T(8,128)(2,1)S(1)}, u32[]{:S(2)}, u32[]{:S(2)}) collective-permute-start(bf16[2128,128]{1,0:T(8,128)(2,1)S(1)} %slice_dynamic-update-slice_fusion), channel_id=1, source_target_pairs={{0,1},{1,0},{2,3},{3,2},{4,5},{5,4},{6,7},{7,6},{8,9},{9,8},{10,11... | collective-permute-start | bytes 1634312 | tf_op jit(solution)/shard_map/ppermute | solution.py:395
  9.4 6.2 %collective-permute-start.2 = (bf16[592,128]{1,0:T(8,128)(2,1)S(1)}, bf16[592,128]{1,0:T(8,128)(2,1)S(1)}, u32[]{:S(2)}, u32[]{:S(2)}) collective-permute-start(bf16[592,128]{1,0:T(8,128)(2,1)S(1)} %pad_maximum_fusion.1.refs_1_), channel_id=1, source_target_pairs={{0,8},{1,9},{2,10},{3,11},{4,12},{5,13},{6,14},{7,15},{8,0},{9,1},... | collective-permute-start | bytes 454664 | tf_op jit(solution)/shard_map/ppermute | solution.py:395
  11.1 5.4 %collective-permute-start.4 = (bf16[592,128]{1,0:T(8,128)(2,1)S(1)}, bf16[592,128]{1,0:T(8,128)(2,1)S(1)}, u32[]{:S(2)}, u32[]{:S(2)}) collective-permute-start(bf16[592,128]{1,0:T(8,128)(2,1)S(1)} %pad_maximum_fusion.1.refs_1_), channel_id=1, source_target_pairs={{0,4},{1,5},{2,6},{3,7},{4,0},{5,1},{6,2},{7,3},{8,12},{9,13},{10,... | collective-permute-start | bytes 454664 | tf_op jit(solution)/shard_map/ppermute | solution.py:395
  12.6 9.3 %collective-permute-start.1 = (bf16[592,128]{1,0:T(8,128)(2,1)S(1)}, bf16[592,128]{1,0:T(8,128)(2,1)S(1)}, u32[]{:S(2)}, u32[]{:S(2)}) collective-permute-start(bf16[592,128]{1,0:T(8,128)(2,1)S(1)} %pad_maximum_fusion.1.refs_1_), channel_id=1, source_target_pairs={{0,16},{1,17},{2,18},{3,19},{4,20},{5,21},{6,22},{7,23},{8,24},{9,... | collective-permute-start | bytes 454664 | tf_op jit(solution)/shard_map/ppermute | solution.py:395
  15.2 6.7 %collective-permute-start.3 = (bf16[592,128]{1,0:T(8,128)(2,1)S(1)}, bf16[592,128]{1,0:T(8,128)(2,1)S(1)}, u32[]{:S(2)}, u32[]{:S(2)}) collective-permute-start(bf16[592,128]{1,0:T(8,128)(2,1)S(1)} %pad_maximum_fusion.1.refs_1_), channel_id=1, source_target_pairs={{0,5},{1,4},{2,7},{3,6},{4,1},{5,0},{6,3},{7,2},{8,13},{9,12},{10,... | collective-permute-start | bytes 454664 | tf_op jit(solution)/shard_map/ppermute | solution.py:395
  21.9 14.2 %collective-permute-start.11 = (bf16[1184,128]{1,0:T(8,128)(2,1)S(1)}, bf16[1184,128]{1,0:T(8,128)(2,1)S(1)}, u32[]{:S(2)}, u32[]{:S(2)}) collective-permute-start(bf16[1184,128]{1,0:T(8,128)(2,1)S(1)} %constant_dynamic-update-slice_fusion.5), channel_id=1, source_target_pairs={{0,4},{1,5},{2,6},{3,7},{4,0},{5,1},{6,2},{7,3},{8,12},{9,13},{10,... | collective-permute-start | bytes 909320 | tf_op jit(solution)/shard_map/ppermute | solution.py:395
  22.6 13.5 %collective-permute-start.12 = (bf16[1184,128]{1,0:T(8,128)(2,1)S(1)}, bf16[1184,128]{1,0:T(8,128)(2,1)S(1)}, u32[]{:S(2)}, u32[]{:S(2)}) collective-permute-start(bf16[1184,128]{1,0:T(8,128)(2,1)S(1)} %constant_dynamic-update-slice_fusion.5), channel_id=1, source_target_pairs={{0,1},{1,0},{2,3},{3,2},{4,5},{5,4},{6,7},{7,6},{8,9},{9,8},{10,11... | collective-permute-start | bytes 909320 | tf_op jit(solution)/shard_map/ppermute | solution.py:395
  23.1 10.1 %collective-permute-start.5 = (bf16[592,128]{1,0:T(8,128)(2,1)S(1)}, bf16[592,128]{1,0:T(8,128)(2,1)S(1)}, u32[]{:S(2)}, u32[]{:S(2)}) collective-permute-start(bf16[592,128]{1,0:T(8,128)(2,1)S(1)} %collective-permute-done.1.refs_1_), channel_id=1, source_target_pairs={{0,8},{1,9},{2,10},{3,11},{4,12},{5,13},{6,14},{7,15},{8,0},{9,1},... | collective-permute-start | bytes 454664 | tf_op jit(solution)/shard_map/ppermute | solution.py:395
  23.4 8.3 %collective-permute-start.8 = (bf16[592,128]{1,0:T(8,128)(2,1)S(1)}, bf16[592,128]{1,0:T(8,128)(2,1)S(1)}, u32[]{:S(2)}, u32[]{:S(2)}) collective-permute-start(bf16[592,128]{1,0:T(8,128)(2,1)S(1)} %collective-permute-done.3.refs_3_), channel_id=1, source_target_pairs={{0,16},{1,17},{2,18},{3,19},{4,20},{5,21},{6,22},{7,23},{8,24},{9,... | collective-permute-start | bytes 454664 | tf_op jit(solution)/shard_map/ppermute | solution.py:395
  31.7 11.9 %collective-permute-start.9 = (bf16[1184,128]{1,0:T(8,128)(2,1)S(1)}, bf16[1184,128]{1,0:T(8,128)(2,1)S(1)}, u32[]{:S(2)}, u32[]{:S(2)}) collective-permute-start(bf16[1184,128]{1,0:T(8,128)(2,1)S(1)} %pad_maximum_fusion), channel_id=1, source_target_pairs={{0,8},{1,9},{2,10},{3,11},{4,12},{5,13},{6,14},{7,15},{8,0},{9,1},... | collective-permute-start | bytes 909320 | tf_op jit(solution)/shard_map/ppermute | solution.py:395
  33.3 10.3 %collective-permute-start.10 = (bf16[592,128]{1,0:T(8,128)(2,1)S(1)}, bf16[592,128]{1,0:T(8,128)(2,1)S(1)}, u32[]{:S(2)}, u32[]{:S(2)}) collective-permute-start(bf16[592,128]{1,0:T(8,128)(2,1)S(1)} %collective-permute-done.5.refs_1_), channel_id=1, source_target_pairs={{0,1},{1,0},{2,3},{3,2},{4,5},{5,4},{6,7},{7,6},{8,9},{9,8},{10,11... | collective-permute-start | bytes 454664 | tf_op jit(solution)/shard_map/ppermute | solution.py:395
  34.8 8.8 %collective-permute-start.6 = (bf16[592,128]{1,0:T(8,128)(2,1)S(1)}, bf16[592,128]{1,0:T(8,128)(2,1)S(1)}, u32[]{:S(2)}, u32[]{:S(2)}) collective-permute-start(bf16[592,128]{1,0:T(8,128)(2,1)S(1)} %collective-permute-done.5.refs_1_), channel_id=1, source_target_pairs={{0,4},{1,5},{2,6},{3,7},{4,0},{5,1},{6,2},{7,3},{8,12},{9,13},{10,... | collective-permute-start | bytes 454664 | tf_op jit(solution)/shard_map/ppermute | solution.py:395
  48.7 2.0 %collective-permute-start.13 = (bf16[4,64,8,128]{3,2,1,0:T(8,128)(2,1)S(1)}, bf16[4,64,8,128]{3,2,1,0:T(8,128)(2,1)S(1)}, u32[]{:S(2)}, u32[]{:S(2)}) collective-permute-start(bf16[4,64,8,128]{3,2,1,0:T(8,128)(2,1)S(1)} %get-tuple-element.49), channel_id=1, source_target_pairs={{0,2},{1,3},{2,0},{3,1},{4,6},{5,7},{6,4},{7,5},{8,10},{9,11},{10,... | collective-permute-start | bytes 1572872 | tf_op jit(solution)/shard_map/ppermute | solution.py:395

commit v5 on v4

--- a/solution.py
+++ b/solution.py
@@ -133,7 +133,7 @@
     kv_at = q_at + n_heads * q_rows
     lengths = [sum(len(blocks) for _, blocks in pieces) * rows for _, _, pieces, _ in groups_of]
     extra = 2 * tokens if stretch is not None else 0
-    chunk = 512
+    chunk = 256
 
     operands, where = [], {}
 
@@ -289,9 +289,9 @@
             if current is not None:
                 done, m, part, mixed = current
             if stretch is not None:
-                if work is not None:
+                if work is not None and work[0] in stretch[2]:
                     top = score_stretch(work, q, slot, top)
-                if current is not None:
+                if current is not None and done[0] in stretch[2]:
                     part, mixed = weigh(old, m, part, mixed, lengths[done[0]], extra, [stretch_rows(done, e, 1) for e in range(2)])
             ahead = parts(work) if work is not None else []
             behind = parts(done) if current is not None else []
@@ -333,7 +333,7 @@
     else:
         out_shape = (jax.ShapeDtypeStruct((n_heads, 2 * q_rows, 128), f32),) * 3
     alias = {1 + n_plain + j: j for j in range(3)} if state is not None and not final else {}
-    pairs = 2 * half * q_rows * (sum(lengths) + extra * len(plan))
+    pairs = 2 * half * q_rows * (sum(lengths) + (extra * len(stretch[2]) if stretch is not None else 0))
     slot = pltpu.VMEM((2 * q_rows, max(lengths) + extra), f32)
     return pl.pallas_call(
         kernel,
@@ -455,8 +455,11 @@
     near = jnp.concatenate(z_one, axis=0)
     x_near, y_near = swap(near, 2), swap(near, 0, 1)
     state = call(
-        [(0, own_book, pieces(*z_one[:-1]), True), (half, other_book, [(y_pack, blocks_of(0))] + pieces(diag), False)],
-        stretch=other_stretch, state=state, final=False,
+        [
+            (0, own_book, pieces(*z_one[:-1]), True),
+            (half, other_book, [(y_pack, blocks_of(0))] + pieces(diag), False),
+        ],
+        stretch=(*other_stretch, (1,)), state=state, final=False,
     )
 
     z_rest = jnp.concatenate(z_two, axis=0) if len(z_two) > 1 else z_two[0]
@@ -466,8 +469,11 @@
     for bits in steps[1:]:
         diag_far.append(along([diag] + diag_far, bits))
     state = call(
-        [(0, own_book, pieces(z_rest, x_near), True), (half, other_book, pieces(diag_far[0], y_near), True)],
-        stretch=None, state=state, final=False,
+        [
+            (0, own_book, pieces(z_rest, x_near), True),
+            (half, other_book, pieces(diag_far[0], y_near), True),
+        ],
+        stretch=(*other_stretch, (0,)), state=state, final=False,
     )
     out, out_send = call(
         [(0, own_book, pieces(x_rest), True), (half, other_book, pieces(*diag_far[1:], y_rest), True)],

time: 52.3 us -> 50.8 us (0.971)
  starting transfers between devices: 18.9 us -> 17.3 us
  Pallas kernels: 26.8 us -> 26 us
  waiting for transfers between devices: 4.3 us -> 5.09 us
    ppermute x14, starting transfers between devices: 18.9 us -> 17.3 us  [swap(): lax.ppermute(x, axes, [(2 * o + i, 2 * (o ^ outer_bits) + (i ^ inner_bits...]
    ppermute x14, waiting for transfers between devices: 4.3 us -> 5.09 us  [swap(): lax.ppermute(x, axes, [(2 * o + i, 2 * (o ^ outer_bits) + (i ^ inner_bits...]
    pallas_call x4, Pallas kernels: 20.9 us -> 20.1 us  [attend(): pl.pallas_call(kernel, out_shape=out_shape, in_specs=[whole(pltpu.SMEM)]...]
  transfers between devices with their start and end apart: 14 -> 14, of which waited for: 4 -> 5; matrix products, arithmetic and copies ran while one was open for 2% -> 2% of each run, Pallas kernels for 33% -> 33%
where the time goes in v5:
time: 50.8 us; the launch traced here: 50.6 us
  Pallas kernels  26 us (51%)
  starting transfers between devices  17.3 us (34%)
  waiting for transfers between devices  5.09 us (10%)
  local copies, waits for them, and re-layouts  1.07 us (2%)
  between operations  1.04 us (2%)
    pallas_call x4, Pallas kernels, attend(): pl.pallas_call(kernel, out_shape=out_shape, in_specs=[whole(pltpu.SMEM)]...  20.1 us
    ppermute x14, starting transfers between devices, swap(): lax.ppermute(x, axes, [(2 * o + i, 2 * (o ^ outer_bits) + (i ^ inner_bits...  17.3 us
    ppermute x14, waiting for transfers between devices, swap(): lax.ppermute(x, axes, [(2 * o + i, 2 * (o ^ outer_bits) + (i ^ inner_bits...  5.09 us
    pallas_call x1, Pallas kernels, prepare(): pl.pallas_call(kernel, out_shape=(shape, shape), in_specs=[whole(pltpu.SM...  3.18 us
    pallas_call x2, Pallas kernels, lay_out(): pl.pallas_call(kernel, out_shape=jax.ShapeDtypeStruct((tokens, 2 * n_out,...  2.73 us
  transfers between devices with their start and end apart: 14, of which 5 were waited for; matrix products, arithmetic and copies ran while one was open for 2% of the time, Pallas kernels for 33%

profile of v5, /device:TPU:0, one launch (start us, length us, event | category | flops | bytes accessed | tf_op | source)
XLA Modules:
  0.0 50.6 jit_solution(14643247480151219720)
XLA Ops:
  0.0 0.0 copy-start.1
  0.0 0.0 copy-start.2
  0.0 0.0 copy-start.3
  0.0 0.0 copy-start.4
  0.0 0.0 copy-start
  0.7 0.1 pad_add_fusion.place
  0.8 3.2 %prepare.1 = (bf16[2864,128]{1,0:T(8,128)(2,1)S(1)}, bf16[2864,128]{1,0:T(8,128)(2,1)S(1)}) custom-call(s32[2]{0:T(128)S(1)} %pad_add_fusion.place, s32[1]{0:T(128)S(6)} %copy.34.ids, s32[4,16,128]{2,1,0:T(8,128)} %bitcast.8, bf16[128,4,128]{2,1,0:T(4,128)(2,1)} %refs_1_.1, f32[4,128]{1,0:T(4,128)} %bitcast.9, bf16[64,10,8,128]{3,2,1,0:T(8,128)(2,1)} %bitcast.6, ...), custom_call_target="tpu_custom_call" | custom-call | tf_op jit(solution)/shard_map/prepare/pallas_call | solution.py:108
  4.0 0.5 %collective-permute-start = (bf16[2864,128]{1,0:T(8,128)(2,1)S(1)}, bf16[2864,128]{1,0:T(8,128)(2,1)S(1)}, u32[]{:S(2)}, u32[]{:S(2)}) collective-permute-start(bf16[2864,128]{1,0:T(8,128)(2,1)S(1)} %get-tuple-element.29), channel_id=1, source_target_pairs={{0,2},{1,3},{2,0},{3,1},{4,6},{5,7},{6,4},{7,5},{8,10},{9,11},{10,... | collective-permute-start | bytes 2199560 | tf_op jit(solution)/shard_map/ppermute | solution.py:395
  4.5 0.9 %constant_dynamic-slice_fusion = bf16[2,256,128]{2,1,0:T(8,128)(2,1)S(1)} fusion(bf16[4,256,128]{2,1,0:T(8,128)(2,1)} %refs_0_.7, s32[]{:T(128)S(6)} %select_n.11), kind=kLoop, calls=%fused_computation.12 | loop fusion | bytes 262148 | tf_op jit(solution)/shard_map/dynamic_slice | solution.py:420
  5.4 0.9 %collective-permute-done.refs_9_.refs_11_.refs_10_ = bf16[2864,128]{1,0:T(8,128)(2,1)S(1)} collective-permute-done((bf16[2864,128]{1,0:T(8,128)(2,1)S(1)}, bf16[2864,128]{1,0:T(8,128)(2,1)S(1)}, u32[]{:S(2)}, u32[]{:S(2)}) %collective-permute-start) | collective-permute-done | bytes 733216 | tf_op jit(solution)/shard_map/ppermute | solution.py:395
  6.5 3.0 %collective-permute-start.7 = (bf16[2128,128]{1,0:T(8,128)(2,1)S(1)}, bf16[2128,128]{1,0:T(8,128)(2,1)S(1)}, u32[]{:S(2)}, u32[]{:S(2)}) collective-permute-start(bf16[2128,128]{1,0:T(8,128)(2,1)S(1)} %slice_dynamic-update-slice_fusion), channel_id=1, source_target_pairs={{0,1},{1,0},{2,3},{3,2},{4,5},{5,4},{6,7},{7,6},{8,9},{9,8},{10,11... | collective-permute-start | bytes 1634312 | tf_op jit(solution)/shard_map/ppermute | solution.py:395
  9.4 1.6 %collective-permute-start.2 = (bf16[592,128]{1,0:T(8,128)(2,1)S(1)}, bf16[592,128]{1,0:T(8,128)(2,1)S(1)}, u32[]{:S(2)}, u32[]{:S(2)}) collective-permute-start(bf16[592,128]{1,0:T(8,128)(2,1)S(1)} %pad_maximum_fusion.1.refs_1_), channel_id=1, source_target_pairs={{0,8},{1,9},{2,10},{3,11},{4,12},{5,13},{6,14},{7,15},{8,0},{9,1},... | collective-permute-start | bytes 454664 | tf_op jit(solution)/shard_map/ppermute | solution.py:395
  11.1 1.5 %collective-permute-start.4 = (bf16[592,128]{1,0:T(8,128)(2,1)S(1)}, bf16[592,128]{1,0:T(8,128)(2,1)S(1)}, u32[]{:S(2)}, u32[]{:S(2)}) collective-permute-start(bf16[592,128]{1,0:T(8,128)(2,1)S(1)} %pad_maximum_fusion.1.refs_1_), channel_id=1, source_target_pairs={{0,4},{1,5},{2,6},{3,7},{4,0},{5,1},{6,2},{7,3},{8,12},{9,13},{10,... | collective-permute-start | bytes 454664 | tf_op jit(solution)/shard_map/ppermute | solution.py:395
  12.6 2.6 %collective-permute-start.1 = (bf16[592,128]{1,0:T(8,128)(2,1)S(1)}, bf16[592,128]{1,0:T(8,128)(2,1)S(1)}, u32[]{:S(2)}, u32[]{:S(2)}) collective-permute-start(bf16[592,128]{1,0:T(8,128)(2,1)S(1)} %pad_maximum_fusion.1.refs_1_), channel_id=1, source_target_pairs={{0,16},{1,17},{2,18},{3,19},{4,20},{5,21},{6,22},{7,23},{8,24},{9,... | collective-permute-start | bytes 454664 | tf_op jit(solution)/shard_map/ppermute | solution.py:395
  15.2 0.5 collective-permute-start.3
  15.6 0.0 collective-permute-done.2.refs_3_
  15.6 0.9 %collective-permute-done.4.refs_2_ = bf16[592,128]{1,0:T(8,128)(2,1)S(1)} collective-permute-done((bf16[592,128]{1,0:T(8,128)(2,1)S(1)}, bf16[592,128]{1,0:T(8,128)(2,1)S(1)}, u32[]{:S(2)}, u32[]{:S(2)}) %collective-permute-start.4) | collective-permute-done | bytes 151584 | tf_op jit(solution)/shard_map/ppermute | solution.py:395
  16.5 0.0 copy-done.1
  16.5 0.0 copy-done.2
  16.5 0.0 copy-done.3
  16.5 0.0 copy-done.4
  16.5 0.0 copy-done
  16.5 3.3 %attend.4 = (f32[4,1024,128]{2,1,0:T(8,128)S(1)}, f32[4,1024,128]{2,1,0:T(8,128)S(1)}, f32[4,1024,128]{2,1,0:T(8,128)S(1)}) custom-call(s32[2]{0:T(128)S(1)} %pad_add_fusion.place, bf16[4,256,128]{2,1,0:T(8,128)(2,1)S(1)} %copy-done, bf16[592,128]{1,0:T(8,128)(2,1)S(1)} %pad_maximum_fusion.1.refs_1_, bf16[592,128]{1,0:T(8,128)(2,1)S(1)} %collective-permute-done.4.refs_2_, ...), custom_call_target="tpu_custom_call" | custom-call | flops 1610612736 | bytes 4194304 | tf_op jit(solution)/shard_map/attend/pallas_call | solution.py:338
  19.9 2.0 %collective-permute-done.1.refs_1_ = bf16[592,128]{1,0:T(8,128)(2,1)S(1)} collective-permute-done((bf16[592,128]{1,0:T(8,128)(2,1)S(1)}, bf16[592,128]{1,0:T(8,128)(2,1)S(1)}, u32[]{:S(2)}, u32[]{:S(2)}) %collective-permute-start.1) | collective-permute-done | bytes 151584 | tf_op jit(solution)/shard_map/ppermute | solution.py:395
  21.9 0.0 collective-permute-done.3.refs_3_
  21.9 0.0 collective-permute-start.5
  21.9 0.8 %collective-permute-start.11 = (bf16[1184,128]{1,0:T(8,128)(2,1)S(1)}, bf16[1184,128]{1,0:T(8,128)(2,1)S(1)}, u32[]{:S(2)}, u32[]{:S(2)}) collective-permute-start(bf16[1184,128]{1,0:T(8,128)(2,1)S(1)} %constant_dynamic-update-slice_fusion.5), channel_id=1, source_target_pairs={{0,4},{1,5},{2,6},{3,7},{4,0},{5,1},{6,2},{7,3},{8,12},{9,13},{10,... | collective-permute-start | bytes 909320 | tf_op jit(solution)/shard_map/ppermute | solution.py:395
  22.8 0.6 %collective-permute-start.12 = (bf16[1184,128]{1,0:T(8,128)(2,1)S(1)}, bf16[1184,128]{1,0:T(8,128)(2,1)S(1)}, u32[]{:S(2)}, u32[]{:S(2)}) collective-permute-start(bf16[1184,128]{1,0:T(8,128)(2,1)S(1)} %constant_dynamic-update-slice_fusion.5), channel_id=1, source_target_pairs={{0,1},{1,0},{2,3},{3,2},{4,5},{5,4},{6,7},{7,6},{8,9},{9,8},{10,11... | collective-permute-start | bytes 909320 | tf_op jit(solution)/shard_map/ppermute | solution.py:395
  23.4 3.3 %collective-permute-start.8 = (bf16[592,128]{1,0:T(8,128)(2,1)S(1)}, bf16[592,128]{1,0:T(8,128)(2,1)S(1)}, u32[]{:S(2)}, u32[]{:S(2)}) collective-permute-start(bf16[592,128]{1,0:T(8,128)(2,1)S(1)} %collective-permute-done.3.refs_3_), channel_id=1, source_target_pairs={{0,16},{1,17},{2,18},{3,19},{4,20},{5,21},{6,22},{7,23},{8,24},{9,... | collective-permute-start | bytes 454664 | tf_op jit(solution)/shard_map/ppermute | solution.py:395
  26.7 0.8 %collective-permute-done.5.refs_1_ = bf16[592,128]{1,0:T(8,128)(2,1)S(1)} collective-permute-done((bf16[592,128]{1,0:T(8,128)(2,1)S(1)}, bf16[592,128]{1,0:T(8,128)(2,1)S(1)}, u32[]{:S(2)}, u32[]{:S(2)}) %collective-permute-start.5) | collective-permute-done | bytes 151584 | tf_op jit(solution)/shard_map/ppermute | solution.py:395
  27.5 0.7 %collective-permute-start.10 = (bf16[592,128]{1,0:T(8,128)(2,1)S(1)}, bf16[592,128]{1,0:T(8,128)(2,1)S(1)}, u32[]{:S(2)}, u32[]{:S(2)}) collective-permute-start(bf16[592,128]{1,0:T(8,128)(2,1)S(1)} %collective-permute-done.5.refs_1_), channel_id=1, source_target_pairs={{0,1},{1,0},{2,3},{3,2},{4,5},{5,4},{6,7},{7,6},{8,9},{9,8},{10,11... | collective-permute-start | bytes 454664 | tf_op jit(solution)/shard_map/ppermute | solution.py:395
  28.2 0.0 collective-permute-done.7.refs_2_.refs_3_
  28.2 0.9 %collective-permute-start.6 = (bf16[592,128]{1,0:T(8,128)(2,1)S(1)}, bf16[592,128]{1,0:T(8,128)(2,1)S(1)}, u32[]{:S(2)}, u32[]{:S(2)}) collective-permute-start(bf16[592,128]{1,0:T(8,128)(2,1)S(1)} %collective-permute-done.5.refs_1_), channel_id=1, source_target_pairs={{0,4},{1,5},{2,6},{3,7},{4,0},{5,1},{6,2},{7,3},{8,12},{9,13},{10,... | collective-permute-start | bytes 454664 | tf_op jit(solution)/shard_map/ppermute | solution.py:395
  29.1 4.7 %attend.5 = (f32[4,1024,128]{2,1,0:T(8,128)S(1)}, f32[4,1024,128]{2,1,0:T(8,128)S(1)}, f32[4,1024,128]{2,1,0:T(8,128)S(1)}) custom-call(s32[2]{0:T(128)S(1)} %pad_add_fusion.place, bf16[4,256,128]{2,1,0:T(8,128)(2,1)S(1)} %copy-done, ...), custom_call_target="tpu_custom_call", output_to_operand_aliasing={{0}: (11, {}), {1}: (12, {}), {2}: (13, {})} | custom-call | flops 1879048192 | bytes 4194304 | tf_op jit(solution)/shard_map/attend/pallas_call | solution.py:338
  33.8 0.0 collective-permute-done.8.refs_4_
  33.8 1.1 %collective-permute-start.9 = (bf16[1184,128]{1,0:T(8,128)(2,1)S(1)}, bf16[1184,128]{1,0:T(8,128)(2,1)S(1)}, u32[]{:S(2)}, u32[]{:S(2)}) collective-permute-start(bf16[1184,128]{1,0:T(8,128)(2,1)S(1)} %pad_maximum_fusion), channel_id=1, source_target_pairs={{0,8},{1,9},{2,10},{3,11},{4,12},{5,13},{6,14},{7,15},{8,0},{9,1},... | collective-permute-start | bytes 909320 | tf_op jit(solution)/shard_map/ppermute | solution.py:395
  35.0 0.0 collective-permute-done.11.refs_2_
  35.0 0.0 collective-permute-done.12.refs_5_
  35.0 7.4 %attend.6 = (f32[4,1024,128]{2,1,0:T(8,128)S(1)}, f32[4,1024,128]{2,1,0:T(8,128)S(1)}, f32[4,1024,128]{2,1,0:T(8,128)S(1)}) custom-call(s32[2]{0:T(128)S(1)} %pad_add_fusion.place, bf16[4,256,128]{2,1,0:T(8,128)(2,1)S(1)} %copy-done, ...), custom_call_target="tpu_custom_call", output_to_operand_aliasing={{0}: (13, {}), {1}: (14, {}), {2}: (15, {})} | custom-call | flops 3489660928 | bytes 4194304 | tf_op jit(solution)/shard_map/attend/pallas_call | solution.py:338
  42.4 0.0 collective-permute-done.10.refs_4_
  42.4 0.0 collective-permute-done.6.refs_1_
  42.4 0.0 collective-permute-done.9.refs_3_
  42.4 4.7 %attend.7 = (bf16[4,64,8,128]{3,2,1,0:T(8,128)(2,1)S(1)}, bf16[4,64,8,128]{3,2,1,0:T(8,128)(2,1)S(1)}) custom-call(s32[2]{0:T(128)S(1)} %pad_add_fusion.place, bf16[4,256,128]{2,1,0:T(8,128)(2,1)S(1)} %copy-done, bf16[592,128]{1,0:T(8,128)(2,1)S(1)} %collective-permute-done.6.refs_1_, bf16[2128,128]{1,0:T(8,128)(2,1)S(1)} %collective-permute-done.7.refs_2_.refs_3_, ...), custom_call_target="tpu_custom_call" | custom-call | flops 2147483648 | bytes 4194304 | tf_op jit(solution)/shard_map/attend/pallas_call | solution.py:338
  47.1 0.1 collective-permute-start.13
  47.2 1.4 %lay_out.2.refs_0_ = bf16[64,8,8,128]{3,2,1,0:T(8,128)(2,1)} custom-call(s32[2]{0:T(128)S(1)} %pad_add_fusion.place, bf16[4,64,8,128]{3,2,1,0:T(8,128)(2,1)S(1)} %get-tuple-element.50.source), custom_call_target="tpu_custom_call" | custom-call | tf_op jit(solution)/shard_map/lay_out/pallas_call | solution.py:369
  48.6 0.5 %collective-permute-done.13.source = bf16[4,64,8,128]{3,2,1,0:T(8,128)(2,1)S(1)} collective-permute-done((bf16[4,64,8,128]{3,2,1,0:T(8,128)(2,1)S(1)}, bf16[4,64,8,128]{3,2,1,0:T(8,128)(2,1)S(1)}, u32[]{:S(2)}, u32[]{:S(2)}) %collective-permute-start.13) | collective-permute-done | bytes 524320 | tf_op jit(solution)/shard_map/ppermute | solution.py:395
  49.1 1.4 %lay_out.3 = bf16[64,8,8,128]{3,2,1,0:T(8,128)(2,1)} custom-call(s32[2]{0:T(128)S(1)} %pad_add_fusion.place, bf16[4,64,8,128]{3,2,1,0:T(8,128)(2,1)S(1)} %collective-permute-done.13.source, bf16[64,8,8,128]{3,2,1,0:T(8,128)(2,1)} %lay_out.2.refs_0_), custom_call_target="tpu_custom_call", output_to_operand_aliasing={{}: (2, {})} | custom-call | tf_op jit(solution)/shard_map/lay_out/pallas_call | solution.py:369
  (11 shorter events, 0.2 us)
Async XLA Ops:
  0.0 16.5 %copy-start.1 = (f32[64,128]{1,0:T(8,128)S(1)}, f32[64,128]{1,0:T(8,128)}, u32[]{:S(2)}) copy-start(f32[64,128]{1,0:T(8,128)} %constant.38.clone.refs_4_.refs_6_.refs_5_) | copy-start | bytes 98308
  0.0 16.5 %copy-start.2 = (f32[64,128]{1,0:T(8,128)S(1)}, f32[64,128]{1,0:T(8,128)}, u32[]{:S(2)}) copy-start(f32[64,128]{1,0:T(8,128)} %constant.39.clone.refs_5_.refs_7_.refs_6_) | copy-start | bytes 98308
  0.0 16.5 %copy-start.3 = (f32[64,128]{1,0:T(8,128)S(1)}, f32[64,128]{1,0:T(8,128)}, u32[]{:S(2)}) copy-start(f32[64,128]{1,0:T(8,128)} %constant.40.clone.refs_6_.refs_8_.refs_7_) | copy-start | bytes 98308
  0.0 16.5 %copy-start.4 = (f32[64,128]{1,0:T(8,128)S(1)}, f32[64,128]{1,0:T(8,128)}, u32[]{:S(2)}) copy-start(f32[64,128]{1,0:T(8,128)} %constant.41.clone.refs_7_.refs_9_.refs_8_) | copy-start | bytes 98308
  0.0 16.5 %copy-start = (bf16[4,256,128]{2,1,0:T(8,128)(2,1)S(1)}, bf16[4,256,128]{2,1,0:T(8,128)(2,1)}, u32[]{:S(2)}) copy-start(bf16[4,256,128]{2,1,0:T(8,128)(2,1)} %refs_0_.7) | copy-start | bytes 786436
  4.0 2.4 %collective-permute-start = (bf16[2864,128]{1,0:T(8,128)(2,1)S(1)}, bf16[2864,128]{1,0:T(8,128)(2,1)S(1)}, u32[]{:S(2)}, u32[]{:S(2)}) collective-permute-start(bf16[2864,128]{1,0:T(8,128)(2,1)S(1)} %get-tuple-element.29), channel_id=1, source_target_pairs={{0,2},{1,3},{2,0},{3,1},{4,6},{5,7},{6,4},{7,5},{8,10},{9,11},{10,... | collective-permute-start | bytes 2199560 | tf_op jit(solution)/shard_map/ppermute | solution.py:395
  6.5 21.7 %collective-permute-start.7 = (bf16[2128,128]{1,0:T(8,128)(2,1)S(1)}, bf16[2128,128]{1,0:T(8,128)(2,1)S(1)}, u32[]{:S(2)}, u32[]{:S(2)}) collective-permute-start(bf16[2128,128]{1,0:T(8,128)(2,1)S(1)} %slice_dynamic-update-slice_fusion), channel_id=1, source_target_pairs={{0,1},{1,0},{2,3},{3,2},{4,5},{5,4},{6,7},{7,6},{8,9},{9,8},{10,11... | collective-permute-start | bytes 1634312 | tf_op jit(solution)/shard_map/ppermute | solution.py:395
  9.4 6.2 %collective-permute-start.2 = (bf16[592,128]{1,0:T(8,128)(2,1)S(1)}, bf16[592,128]{1,0:T(8,128)(2,1)S(1)}, u32[]{:S(2)}, u32[]{:S(2)}) collective-permute-start(bf16[592,128]{1,0:T(8,128)(2,1)S(1)} %pad_maximum_fusion.1.refs_1_), channel_id=1, source_target_pairs={{0,8},{1,9},{2,10},{3,11},{4,12},{5,13},{6,14},{7,15},{8,0},{9,1},... | collective-permute-start | bytes 454664 | tf_op jit(solution)/shard_map/ppermute | solution.py:395
  11.1 5.4 %collective-permute-start.4 = (bf16[592,128]{1,0:T(8,128)(2,1)S(1)}, bf16[592,128]{1,0:T(8,128)(2,1)S(1)}, u32[]{:S(2)}, u32[]{:S(2)}) collective-permute-start(bf16[592,128]{1,0:T(8,128)(2,1)S(1)} %pad_maximum_fusion.1.refs_1_), channel_id=1, source_target_pairs={{0,4},{1,5},{2,6},{3,7},{4,0},{5,1},{6,2},{7,3},{8,12},{9,13},{10,... | collective-permute-start | bytes 454664 | tf_op jit(solution)/shard_map/ppermute | solution.py:395
  12.6 9.3 %collective-permute-start.1 = (bf16[592,128]{1,0:T(8,128)(2,1)S(1)}, bf16[592,128]{1,0:T(8,128)(2,1)S(1)}, u32[]{:S(2)}, u32[]{:S(2)}) collective-permute-start(bf16[592,128]{1,0:T(8,128)(2,1)S(1)} %pad_maximum_fusion.1.refs_1_), channel_id=1, source_target_pairs={{0,16},{1,17},{2,18},{3,19},{4,20},{5,21},{6,22},{7,23},{8,24},{9,... | collective-permute-start | bytes 454664 | tf_op jit(solution)/shard_map/ppermute | solution.py:395
  15.2 6.7 %collective-permute-start.3 = (bf16[592,128]{1,0:T(8,128)(2,1)S(1)}, bf16[592,128]{1,0:T(8,128)(2,1)S(1)}, u32[]{:S(2)}, u32[]{:S(2)}) collective-permute-start(bf16[592,128]{1,0:T(8,128)(2,1)S(1)} %pad_maximum_fusion.1.refs_1_), channel_id=1, source_target_pairs={{0,5},{1,4},{2,7},{3,6},{4,1},{5,0},{6,3},{7,2},{8,13},{9,12},{10,... | collective-permute-start | bytes 454664 | tf_op jit(solution)/shard_map/ppermute | solution.py:395
  21.9 5.6 %collective-permute-start.5 = (bf16[592,128]{1,0:T(8,128)(2,1)S(1)}, bf16[592,128]{1,0:T(8,128)(2,1)S(1)}, u32[]{:S(2)}, u32[]{:S(2)}) collective-permute-start(bf16[592,128]{1,0:T(8,128)(2,1)S(1)} %collective-permute-done.1.refs_1_), channel_id=1, source_target_pairs={{0,8},{1,9},{2,10},{3,11},{4,12},{5,13},{6,14},{7,15},{8,0},{9,1},... | collective-permute-start | bytes 454664 | tf_op jit(solution)/shard_map/ppermute | solution.py:395
  21.9 13.0 %collective-permute-start.11 = (bf16[1184,128]{1,0:T(8,128)(2,1)S(1)}, bf16[1184,128]{1,0:T(8,128)(2,1)S(1)}, u32[]{:S(2)}, u32[]{:S(2)}) collective-permute-start(bf16[1184,128]{1,0:T(8,128)(2,1)S(1)} %constant_dynamic-update-slice_fusion.5), channel_id=1, source_target_pairs={{0,4},{1,5},{2,6},{3,7},{4,0},{5,1},{6,2},{7,3},{8,12},{9,13},{10,... | collective-permute-start | bytes 909320 | tf_op jit(solution)/shard_map/ppermute | solution.py:395
  22.8 12.2 %collective-permute-start.12 = (bf16[1184,128]{1,0:T(8,128)(2,1)S(1)}, bf16[1184,128]{1,0:T(8,128)(2,1)S(1)}, u32[]{:S(2)}, u32[]{:S(2)}) collective-permute-start(bf16[1184,128]{1,0:T(8,128)(2,1)S(1)} %constant_dynamic-update-slice_fusion.5), channel_id=1, source_target_pairs={{0,1},{1,0},{2,3},{3,2},{4,5},{5,4},{6,7},{7,6},{8,9},{9,8},{10,11... | collective-permute-start | bytes 909320 | tf_op jit(solution)/shard_map/ppermute | solution.py:395
  23.4 10.4 %collective-permute-start.8 = (bf16[592,128]{1,0:T(8,128)(2,1)S(1)}, bf16[592,128]{1,0:T(8,128)(2,1)S(1)}, u32[]{:S(2)}, u32[]{:S(2)}) collective-permute-start(bf16[592,128]{1,0:T(8,128)(2,1)S(1)} %collective-permute-done.3.refs_3_), channel_id=1, source_target_pairs={{0,16},{1,17},{2,18},{3,19},{4,20},{5,21},{6,22},{7,23},{8,24},{9,... | collective-permute-start | bytes 454664 | tf_op jit(solution)/shard_map/ppermute | solution.py:395
  27.5 14.9 %collective-permute-start.10 = (bf16[592,128]{1,0:T(8,128)(2,1)S(1)}, bf16[592,128]{1,0:T(8,128)(2,1)S(1)}, u32[]{:S(2)}, u32[]{:S(2)}) collective-permute-start(bf16[592,128]{1,0:T(8,128)(2,1)S(1)} %collective-permute-done.5.refs_1_), channel_id=1, source_target_pairs={{0,1},{1,0},{2,3},{3,2},{4,5},{5,4},{6,7},{7,6},{8,9},{9,8},{10,11... | collective-permute-start | bytes 454664 | tf_op jit(solution)/shard_map/ppermute | solution.py:395
  28.2 14.2 %collective-permute-start.6 = (bf16[592,128]{1,0:T(8,128)(2,1)S(1)}, bf16[592,128]{1,0:T(8,128)(2,1)S(1)}, u32[]{:S(2)}, u32[]{:S(2)}) collective-permute-start(bf16[592,128]{1,0:T(8,128)(2,1)S(1)} %collective-permute-done.5.refs_1_), channel_id=1, source_target_pairs={{0,4},{1,5},{2,6},{3,7},{4,0},{5,1},{6,2},{7,3},{8,12},{9,13},{10,... | collective-permute-start | bytes 454664 | tf_op jit(solution)/shard_map/ppermute | solution.py:395
  33.8 8.6 %collective-permute-start.9 = (bf16[1184,128]{1,0:T(8,128)(2,1)S(1)}, bf16[1184,128]{1,0:T(8,128)(2,1)S(1)}, u32[]{:S(2)}, u32[]{:S(2)}) collective-permute-start(bf16[1184,128]{1,0:T(8,128)(2,1)S(1)} %pad_maximum_fusion), channel_id=1, source_target_pairs={{0,8},{1,9},{2,10},{3,11},{4,12},{5,13},{6,14},{7,15},{8,0},{9,1},... | collective-permute-start | bytes 909320 | tf_op jit(solution)/shard_map/ppermute | solution.py:395
  47.1 2.0 %collective-permute-start.13 = (bf16[4,64,8,128]{3,2,1,0:T(8,128)(2,1)S(1)}, bf16[4,64,8,128]{3,2,1,0:T(8,128)(2,1)S(1)}, u32[]{:S(2)}, u32[]{:S(2)}) collective-permute-start(bf16[4,64,8,128]{3,2,1,0:T(8,128)(2,1)S(1)} %get-tuple-element.49), channel_id=1, source_target_pairs={{0,2},{1,3},{2,0},{3,1},{4,6},{5,7},{6,4},{7,5},{8,10},{9,11},{10,... | collective-permute-start | bytes 1572872 | tf_op jit(solution)/shard_map/ppermute | solution.py:395

commit v6 on v5

--- a/solution.py
+++ b/solution.py
@@ -88,12 +88,12 @@
         spread = (tokens, 1, n_heads, head_dim)
         for slot in range(group):
             x = turn(qkv[:, slot, :, :].astype(f32))
-            q_scratch[:, slot : slot + 1, :, :] = x.reshape(spread)
-        k_scratch[...] = turn(qkv[:, group, :, :].astype(f32))
-        v_scratch[...] = qkv[:, group + 1, :, :].astype(f32)
-        q_flat = q_scratch.reshape(q_rows * n_heads, head_dim)
-        k_flat = k_scratch.reshape(tokens * n_heads, head_dim)
-        v_flat = v_scratch.reshape(tokens * n_heads, head_dim)
+            q_scratch[:tokens, slot : slot + 1, :, :] = x.reshape(spread)
+        k_scratch[:tokens] = turn(qkv[:, group, :, :].astype(f32))
+        v_scratch[:tokens] = qkv[:, group + 1, :, :].astype(f32)
+        q_flat = q_scratch.reshape((tokens + 1) * group * n_heads, head_dim)
+        k_flat = k_scratch.reshape((tokens + 1) * n_heads, head_dim)
+        v_flat = v_scratch.reshape((tokens + 1) * n_heads, head_dim)
         for target, which in ((send, 1 - core), (keep, core)):
             for j in range(n_out):
                 head = (inner if j < half else 1 - inner) * kv_local + which * half + j % half
@@ -112,9 +112,9 @@
         out_specs=(whole(), whole()),
         scratch_shapes=[pltpu.VMEM(x.shape, x.dtype) for x in sources]
         + [
-            pltpu.VMEM((tokens, group, n_heads, head_dim), f32),
-            pltpu.VMEM((tokens, n_heads, head_dim), f32),
-            pltpu.VMEM((tokens, n_heads, head_dim), f32),
+            pltpu.VMEM((tokens + 1, group, n_heads, head_dim), f32),
+            pltpu.VMEM((tokens + 1, n_heads, head_dim), f32),
+            pltpu.VMEM((tokens + 1, n_heads, head_dim), f32),
             pltpu.SemaphoreType.DMA((6,)),
         ],
         compiler_params=params(),

time: 50.8 us -> 50.8 us (level)
  no operation moved by 1% of the time
where the time goes in v6:
time: 50.8 us; the launch traced here: 50.6 us
  Pallas kernels  26 us (51%)
  starting transfers between devices  17.3 us (34%)
  waiting for transfers between devices  5.09 us (10%)
  local copies, waits for them, and re-layouts  1.07 us (2%)
  between operations  1.04 us (2%)
    pallas_call x4, Pallas kernels, attend(): pl.pallas_call(kernel, out_shape=out_shape, in_specs=[whole(pltpu.SMEM)]...  20.1 us
    ppermute x14, starting transfers between devices, swap(): lax.ppermute(x, axes, [(2 * o + i, 2 * (o ^ outer_bits) + (i ^ inner_bits...  17.3 us
    ppermute x14, waiting for transfers between devices, swap(): lax.ppermute(x, axes, [(2 * o + i, 2 * (o ^ outer_bits) + (i ^ inner_bits...  5.09 us
    pallas_call x1, Pallas kernels, prepare(): pl.pallas_call(kernel, out_shape=(shape, shape), in_specs=[whole(pltpu.SM...  3.17 us
    pallas_call x2, Pallas kernels, lay_out(): pl.pallas_call(kernel, out_shape=jax.ShapeDtypeStruct((tokens, 2 * n_out,...  2.73 us
  transfers between devices with their start and end apart: 14, of which 5 were waited for; matrix products, arithmetic and copies ran while one was open for 2% of the time, Pallas kernels for 33%

profile of v6, /device:TPU:0, one launch (start us, length us, event | category | flops | bytes accessed | tf_op | source)
XLA Modules:
  0.0 50.6 jit_solution(10388181373029113578)
XLA Ops:
  0.0 0.0 copy-start.1
  0.0 0.0 copy-start.2
  0.0 0.0 copy-start.3
  0.0 0.0 copy-start.4
  0.0 0.0 copy-start
  0.7 0.1 pad_add_fusion.place
  0.8 3.2 %prepare.1 = (bf16[2864,128]{1,0:T(8,128)(2,1)S(1)}, bf16[2864,128]{1,0:T(8,128)(2,1)S(1)}) custom-call(s32[2]{0:T(128)S(1)} %pad_add_fusion.place, s32[1]{0:T(128)S(6)} %copy.34.ids, s32[4,16,128]{2,1,0:T(8,128)} %bitcast.8, bf16[128,4,128]{2,1,0:T(4,128)(2,1)} %refs_1_.1, f32[4,128]{1,0:T(4,128)} %bitcast.9, bf16[64,10,8,128]{3,2,1,0:T(8,128)(2,1)} %bitcast.6, ...), custom_call_target="tpu_custom_call" | custom-call | tf_op jit(solution)/shard_map/prepare/pallas_call | solution.py:108
  4.0 0.5 %collective-permute-start = (bf16[2864,128]{1,0:T(8,128)(2,1)S(1)}, bf16[2864,128]{1,0:T(8,128)(2,1)S(1)}, u32[]{:S(2)}, u32[]{:S(2)}) collective-permute-start(bf16[2864,128]{1,0:T(8,128)(2,1)S(1)} %get-tuple-element.29), channel_id=1, source_target_pairs={{0,2},{1,3},{2,0},{3,1},{4,6},{5,7},{6,4},{7,5},{8,10},{9,11},{10,... | collective-permute-start | bytes 2199560 | tf_op jit(solution)/shard_map/ppermute | solution.py:395
  4.5 0.9 %constant_dynamic-slice_fusion = bf16[2,256,128]{2,1,0:T(8,128)(2,1)S(1)} fusion(bf16[4,256,128]{2,1,0:T(8,128)(2,1)} %refs_0_.7, s32[]{:T(128)S(6)} %select_n.11), kind=kLoop, calls=%fused_computation.12 | loop fusion | bytes 262148 | tf_op jit(solution)/shard_map/dynamic_slice | solution.py:420
  5.4 0.9 %collective-permute-done.refs_9_.refs_11_.refs_10_ = bf16[2864,128]{1,0:T(8,128)(2,1)S(1)} collective-permute-done((bf16[2864,128]{1,0:T(8,128)(2,1)S(1)}, bf16[2864,128]{1,0:T(8,128)(2,1)S(1)}, u32[]{:S(2)}, u32[]{:S(2)}) %collective-permute-start) | collective-permute-done | bytes 733216 | tf_op jit(solution)/shard_map/ppermute | solution.py:395
  6.5 3.0 %collective-permute-start.7 = (bf16[2128,128]{1,0:T(8,128)(2,1)S(1)}, bf16[2128,128]{1,0:T(8,128)(2,1)S(1)}, u32[]{:S(2)}, u32[]{:S(2)}) collective-permute-start(bf16[2128,128]{1,0:T(8,128)(2,1)S(1)} %slice_dynamic-update-slice_fusion), channel_id=1, source_target_pairs={{0,1},{1,0},{2,3},{3,2},{4,5},{5,4},{6,7},{7,6},{8,9},{9,8},{10,11... | collective-permute-start | bytes 1634312 | tf_op jit(solution)/shard_map/ppermute | solution.py:395
  9.4 1.6 %collective-permute-start.2 = (bf16[592,128]{1,0:T(8,128)(2,1)S(1)}, bf16[592,128]{1,0:T(8,128)(2,1)S(1)}, u32[]{:S(2)}, u32[]{:S(2)}) collective-permute-start(bf16[592,128]{1,0:T(8,128)(2,1)S(1)} %pad_maximum_fusion.1.refs_1_), channel_id=1, source_target_pairs={{0,8},{1,9},{2,10},{3,11},{4,12},{5,13},{6,14},{7,15},{8,0},{9,1},... | collective-permute-start | bytes 454664 | tf_op jit(solution)/shard_map/ppermute | solution.py:395
  11.1 1.5 %collective-permute-start.4 = (bf16[592,128]{1,0:T(8,128)(2,1)S(1)}, bf16[592,128]{1,0:T(8,128)(2,1)S(1)}, u32[]{:S(2)}, u32[]{:S(2)}) collective-permute-start(bf16[592,128]{1,0:T(8,128)(2,1)S(1)} %pad_maximum_fusion.1.refs_1_), channel_id=1, source_target_pairs={{0,4},{1,5},{2,6},{3,7},{4,0},{5,1},{6,2},{7,3},{8,12},{9,13},{10,... | collective-permute-start | bytes 454664 | tf_op jit(solution)/shard_map/ppermute | solution.py:395
  12.6 2.6 %collective-permute-start.1 = (bf16[592,128]{1,0:T(8,128)(2,1)S(1)}, bf16[592,128]{1,0:T(8,128)(2,1)S(1)}, u32[]{:S(2)}, u32[]{:S(2)}) collective-permute-start(bf16[592,128]{1,0:T(8,128)(2,1)S(1)} %pad_maximum_fusion.1.refs_1_), channel_id=1, source_target_pairs={{0,16},{1,17},{2,18},{3,19},{4,20},{5,21},{6,22},{7,23},{8,24},{9,... | collective-permute-start | bytes 454664 | tf_op jit(solution)/shard_map/ppermute | solution.py:395
  15.2 0.5 collective-permute-start.3
  15.6 0.0 collective-permute-done.2.refs_3_
  15.6 0.9 %collective-permute-done.4.refs_2_ = bf16[592,128]{1,0:T(8,128)(2,1)S(1)} collective-permute-done((bf16[592,128]{1,0:T(8,128)(2,1)S(1)}, bf16[592,128]{1,0:T(8,128)(2,1)S(1)}, u32[]{:S(2)}, u32[]{:S(2)}) %collective-permute-start.4) | collective-permute-done | bytes 151584 | tf_op jit(solution)/shard_map/ppermute | solution.py:395
  16.5 0.0 copy-done.1
  16.5 0.0 copy-done.2
  16.5 0.0 copy-done.3
  16.5 0.0 copy-done.4
  16.5 0.0 copy-done
  16.5 3.3 %attend.4 = (f32[4,1024,128]{2,1,0:T(8,128)S(1)}, f32[4,1024,128]{2,1,0:T(8,128)S(1)}, f32[4,1024,128]{2,1,0:T(8,128)S(1)}) custom-call(s32[2]{0:T(128)S(1)} %pad_add_fusion.place, bf16[4,256,128]{2,1,0:T(8,128)(2,1)S(1)} %copy-done, bf16[592,128]{1,0:T(8,128)(2,1)S(1)} %pad_maximum_fusion.1.refs_1_, bf16[592,128]{1,0:T(8,128)(2,1)S(1)} %collective-permute-done.4.refs_2_, ...), custom_call_target="tpu_custom_call" | custom-call | flops 1610612736 | bytes 4194304 | tf_op jit(solution)/shard_map/attend/pallas_call | solution.py:338
  19.9 2.0 %collective-permute-done.1.refs_1_ = bf16[592,128]{1,0:T(8,128)(2,1)S(1)} collective-permute-done((bf16[592,128]{1,0:T(8,128)(2,1)S(1)}, bf16[592,128]{1,0:T(8,128)(2,1)S(1)}, u32[]{:S(2)}, u32[]{:S(2)}) %collective-permute-start.1) | collective-permute-done | bytes 151584 | tf_op jit(solution)/shard_map/ppermute | solution.py:395
  21.9 0.0 collective-permute-done.3.refs_3_
  21.9 0.0 collective-permute-start.5
  21.9 0.8 %collective-permute-start.11 = (bf16[1184,128]{1,0:T(8,128)(2,1)S(1)}, bf16[1184,128]{1,0:T(8,128)(2,1)S(1)}, u32[]{:S(2)}, u32[]{:S(2)}) collective-permute-start(bf16[1184,128]{1,0:T(8,128)(2,1)S(1)} %constant_dynamic-update-slice_fusion.5), channel_id=1, source_target_pairs={{0,4},{1,5},{2,6},{3,7},{4,0},{5,1},{6,2},{7,3},{8,12},{9,13},{10,... | collective-permute-start | bytes 909320 | tf_op jit(solution)/shard_map/ppermute | solution.py:395
  22.7 0.6 %collective-permute-start.12 = (bf16[1184,128]{1,0:T(8,128)(2,1)S(1)}, bf16[1184,128]{1,0:T(8,128)(2,1)S(1)}, u32[]{:S(2)}, u32[]{:S(2)}) collective-permute-start(bf16[1184,128]{1,0:T(8,128)(2,1)S(1)} %constant_dynamic-update-slice_fusion.5), channel_id=1, source_target_pairs={{0,1},{1,0},{2,3},{3,2},{4,5},{5,4},{6,7},{7,6},{8,9},{9,8},{10,11... | collective-permute-start | bytes 909320 | tf_op jit(solution)/shard_map/ppermute | solution.py:395
  23.4 3.3 %collective-permute-start.8 = (bf16[592,128]{1,0:T(8,128)(2,1)S(1)}, bf16[592,128]{1,0:T(8,128)(2,1)S(1)}, u32[]{:S(2)}, u32[]{:S(2)}) collective-permute-start(bf16[592,128]{1,0:T(8,128)(2,1)S(1)} %collective-permute-done.3.refs_3_), channel_id=1, source_target_pairs={{0,16},{1,17},{2,18},{3,19},{4,20},{5,21},{6,22},{7,23},{8,24},{9,... | collective-permute-start | bytes 454664 | tf_op jit(solution)/shard_map/ppermute | solution.py:395
  26.7 0.8 %collective-permute-done.5.refs_1_ = bf16[592,128]{1,0:T(8,128)(2,1)S(1)} collective-permute-done((bf16[592,128]{1,0:T(8,128)(2,1)S(1)}, bf16[592,128]{1,0:T(8,128)(2,1)S(1)}, u32[]{:S(2)}, u32[]{:S(2)}) %collective-permute-start.5) | collective-permute-done | bytes 151584 | tf_op jit(solution)/shard_map/ppermute | solution.py:395
  27.5 0.8 %collective-permute-start.10 = (bf16[592,128]{1,0:T(8,128)(2,1)S(1)}, bf16[592,128]{1,0:T(8,128)(2,1)S(1)}, u32[]{:S(2)}, u32[]{:S(2)}) collective-permute-start(bf16[592,128]{1,0:T(8,128)(2,1)S(1)} %collective-permute-done.5.refs_1_), channel_id=1, source_target_pairs={{0,1},{1,0},{2,3},{3,2},{4,5},{5,4},{6,7},{7,6},{8,9},{9,8},{10,11... | collective-permute-start | bytes 454664 | tf_op jit(solution)/shard_map/ppermute | solution.py:395
  28.2 0.0 collective-permute-done.7.refs_2_.refs_3_
  28.2 0.9 %collective-permute-start.6 = (bf16[592,128]{1,0:T(8,128)(2,1)S(1)}, bf16[592,128]{1,0:T(8,128)(2,1)S(1)}, u32[]{:S(2)}, u32[]{:S(2)}) collective-permute-start(bf16[592,128]{1,0:T(8,128)(2,1)S(1)} %collective-permute-done.5.refs_1_), channel_id=1, source_target_pairs={{0,4},{1,5},{2,6},{3,7},{4,0},{5,1},{6,2},{7,3},{8,12},{9,13},{10,... | collective-permute-start | bytes 454664 | tf_op jit(solution)/shard_map/ppermute | solution.py:395
  29.1 4.7 %attend.5 = (f32[4,1024,128]{2,1,0:T(8,128)S(1)}, f32[4,1024,128]{2,1,0:T(8,128)S(1)}, f32[4,1024,128]{2,1,0:T(8,128)S(1)}) custom-call(s32[2]{0:T(128)S(1)} %pad_add_fusion.place, bf16[4,256,128]{2,1,0:T(8,128)(2,1)S(1)} %copy-done, ...), custom_call_target="tpu_custom_call", output_to_operand_aliasing={{0}: (11, {}), {1}: (12, {}), {2}: (13, {})} | custom-call | flops 1879048192 | bytes 4194304 | tf_op jit(solution)/shard_map/attend/pallas_call | solution.py:338
  33.8 0.0 collective-permute-done.8.refs_4_
  33.8 1.1 %collective-permute-start.9 = (bf16[1184,128]{1,0:T(8,128)(2,1)S(1)}, bf16[1184,128]{1,0:T(8,128)(2,1)S(1)}, u32[]{:S(2)}, u32[]{:S(2)}) collective-permute-start(bf16[1184,128]{1,0:T(8,128)(2,1)S(1)} %pad_maximum_fusion), channel_id=1, source_target_pairs={{0,8},{1,9},{2,10},{3,11},{4,12},{5,13},{6,14},{7,15},{8,0},{9,1},... | collective-permute-start | bytes 909320 | tf_op jit(solution)/shard_map/ppermute | solution.py:395
  35.0 0.0 collective-permute-done.11.refs_2_
  35.0 0.0 collective-permute-done.12.refs_5_
  35.0 7.4 %attend.6 = (f32[4,1024,128]{2,1,0:T(8,128)S(1)}, f32[4,1024,128]{2,1,0:T(8,128)S(1)}, f32[4,1024,128]{2,1,0:T(8,128)S(1)}) custom-call(s32[2]{0:T(128)S(1)} %pad_add_fusion.place, bf16[4,256,128]{2,1,0:T(8,128)(2,1)S(1)} %copy-done, ...), custom_call_target="tpu_custom_call", output_to_operand_aliasing={{0}: (13, {}), {1}: (14, {}), {2}: (15, {})} | custom-call | flops 3489660928 | bytes 4194304 | tf_op jit(solution)/shard_map/attend/pallas_call | solution.py:338
  42.4 0.0 collective-permute-done.10.refs_4_
  42.4 0.0 collective-permute-done.6.refs_1_
  42.4 0.0 collective-permute-done.9.refs_3_
  42.4 4.7 %attend.7 = (bf16[4,64,8,128]{3,2,1,0:T(8,128)(2,1)S(1)}, bf16[4,64,8,128]{3,2,1,0:T(8,128)(2,1)S(1)}) custom-call(s32[2]{0:T(128)S(1)} %pad_add_fusion.place, bf16[4,256,128]{2,1,0:T(8,128)(2,1)S(1)} %copy-done, bf16[592,128]{1,0:T(8,128)(2,1)S(1)} %collective-permute-done.6.refs_1_, bf16[2128,128]{1,0:T(8,128)(2,1)S(1)} %collective-permute-done.7.refs_2_.refs_3_, ...), custom_call_target="tpu_custom_call" | custom-call | flops 2147483648 | bytes 4194304 | tf_op jit(solution)/shard_map/attend/pallas_call | solution.py:338
  47.1 0.1 collective-permute-start.13
  47.2 1.4 %lay_out.2.refs_0_ = bf16[64,8,8,128]{3,2,1,0:T(8,128)(2,1)} custom-call(s32[2]{0:T(128)S(1)} %pad_add_fusion.place, bf16[4,64,8,128]{3,2,1,0:T(8,128)(2,1)S(1)} %get-tuple-element.50.source), custom_call_target="tpu_custom_call" | custom-call | tf_op jit(solution)/shard_map/lay_out/pallas_call | solution.py:369
  48.6 0.5 %collective-permute-done.13.source = bf16[4,64,8,128]{3,2,1,0:T(8,128)(2,1)S(1)} collective-permute-done((bf16[4,64,8,128]{3,2,1,0:T(8,128)(2,1)S(1)}, bf16[4,64,8,128]{3,2,1,0:T(8,128)(2,1)S(1)}, u32[]{:S(2)}, u32[]{:S(2)}) %collective-permute-start.13) | collective-permute-done | bytes 524320 | tf_op jit(solution)/shard_map/ppermute | solution.py:395
  49.1 1.4 %lay_out.3 = bf16[64,8,8,128]{3,2,1,0:T(8,128)(2,1)} custom-call(s32[2]{0:T(128)S(1)} %pad_add_fusion.place, bf16[4,64,8,128]{3,2,1,0:T(8,128)(2,1)S(1)} %collective-permute-done.13.source, bf16[64,8,8,128]{3,2,1,0:T(8,128)(2,1)} %lay_out.2.refs_0_), custom_call_target="tpu_custom_call", output_to_operand_aliasing={{}: (2, {})} | custom-call | tf_op jit(solution)/shard_map/lay_out/pallas_call | solution.py:369
  (11 shorter events, 0.2 us)
Async XLA Ops:
  0.0 16.5 %copy-start.1 = (f32[64,128]{1,0:T(8,128)S(1)}, f32[64,128]{1,0:T(8,128)}, u32[]{:S(2)}) copy-start(f32[64,128]{1,0:T(8,128)} %constant.38.clone.refs_4_.refs_6_.refs_5_) | copy-start | bytes 98308
  0.0 16.5 %copy-start.2 = (f32[64,128]{1,0:T(8,128)S(1)}, f32[64,128]{1,0:T(8,128)}, u32[]{:S(2)}) copy-start(f32[64,128]{1,0:T(8,128)} %constant.39.clone.refs_5_.refs_7_.refs_6_) | copy-start | bytes 98308
  0.0 16.5 %copy-start.3 = (f32[64,128]{1,0:T(8,128)S(1)}, f32[64,128]{1,0:T(8,128)}, u32[]{:S(2)}) copy-start(f32[64,128]{1,0:T(8,128)} %constant.40.clone.refs_6_.refs_8_.refs_7_) | copy-start | bytes 98308
  0.0 16.5 %copy-start.4 = (f32[64,128]{1,0:T(8,128)S(1)}, f32[64,128]{1,0:T(8,128)}, u32[]{:S(2)}) copy-start(f32[64,128]{1,0:T(8,128)} %constant.41.clone.refs_7_.refs_9_.refs_8_) | copy-start | bytes 98308
  0.0 16.5 %copy-start = (bf16[4,256,128]{2,1,0:T(8,128)(2,1)S(1)}, bf16[4,256,128]{2,1,0:T(8,128)(2,1)}, u32[]{:S(2)}) copy-start(bf16[4,256,128]{2,1,0:T(8,128)(2,1)} %refs_0_.7) | copy-start | bytes 786436
  4.0 2.4 %collective-permute-start = (bf16[2864,128]{1,0:T(8,128)(2,1)S(1)}, bf16[2864,128]{1,0:T(8,128)(2,1)S(1)}, u32[]{:S(2)}, u32[]{:S(2)}) collective-permute-start(bf16[2864,128]{1,0:T(8,128)(2,1)S(1)} %get-tuple-element.29), channel_id=1, source_target_pairs={{0,2},{1,3},{2,0},{3,1},{4,6},{5,7},{6,4},{7,5},{8,10},{9,11},{10,... | collective-permute-start | bytes 2199560 | tf_op jit(solution)/shard_map/ppermute | solution.py:395
  6.5 21.7 %collective-permute-start.7 = (bf16[2128,128]{1,0:T(8,128)(2,1)S(1)}, bf16[2128,128]{1,0:T(8,128)(2,1)S(1)}, u32[]{:S(2)}, u32[]{:S(2)}) collective-permute-start(bf16[2128,128]{1,0:T(8,128)(2,1)S(1)} %slice_dynamic-update-slice_fusion), channel_id=1, source_target_pairs={{0,1},{1,0},{2,3},{3,2},{4,5},{5,4},{6,7},{7,6},{8,9},{9,8},{10,11... | collective-permute-start | bytes 1634312 | tf_op jit(solution)/shard_map/ppermute | solution.py:395
  9.4 6.2 %collective-permute-start.2 = (bf16[592,128]{1,0:T(8,128)(2,1)S(1)}, bf16[592,128]{1,0:T(8,128)(2,1)S(1)}, u32[]{:S(2)}, u32[]{:S(2)}) collective-permute-start(bf16[592,128]{1,0:T(8,128)(2,1)S(1)} %pad_maximum_fusion.1.refs_1_), channel_id=1, source_target_pairs={{0,8},{1,9},{2,10},{3,11},{4,12},{5,13},{6,14},{7,15},{8,0},{9,1},... | collective-permute-start | bytes 454664 | tf_op jit(solution)/shard_map/ppermute | solution.py:395
  11.1 5.4 %collective-permute-start.4 = (bf16[592,128]{1,0:T(8,128)(2,1)S(1)}, bf16[592,128]{1,0:T(8,128)(2,1)S(1)}, u32[]{:S(2)}, u32[]{:S(2)}) collective-permute-start(bf16[592,128]{1,0:T(8,128)(2,1)S(1)} %pad_maximum_fusion.1.refs_1_), channel_id=1, source_target_pairs={{0,4},{1,5},{2,6},{3,7},{4,0},{5,1},{6,2},{7,3},{8,12},{9,13},{10,... | collective-permute-start | bytes 454664 | tf_op jit(solution)/shard_map/ppermute | solution.py:395
  12.6 9.3 %collective-permute-start.1 = (bf16[592,128]{1,0:T(8,128)(2,1)S(1)}, bf16[592,128]{1,0:T(8,128)(2,1)S(1)}, u32[]{:S(2)}, u32[]{:S(2)}) collective-permute-start(bf16[592,128]{1,0:T(8,128)(2,1)S(1)} %pad_maximum_fusion.1.refs_1_), channel_id=1, source_target_pairs={{0,16},{1,17},{2,18},{3,19},{4,20},{5,21},{6,22},{7,23},{8,24},{9,... | collective-permute-start | bytes 454664 | tf_op jit(solution)/shard_map/ppermute | solution.py:395
  15.2 6.7 %collective-permute-start.3 = (bf16[592,128]{1,0:T(8,128)(2,1)S(1)}, bf16[592,128]{1,0:T(8,128)(2,1)S(1)}, u32[]{:S(2)}, u32[]{:S(2)}) collective-permute-start(bf16[592,128]{1,0:T(8,128)(2,1)S(1)} %pad_maximum_fusion.1.refs_1_), channel_id=1, source_target_pairs={{0,5},{1,4},{2,7},{3,6},{4,1},{5,0},{6,3},{7,2},{8,13},{9,12},{10,... | collective-permute-start | bytes 454664 | tf_op jit(solution)/shard_map/ppermute | solution.py:395
  21.9 5.6 %collective-permute-start.5 = (bf16[592,128]{1,0:T(8,128)(2,1)S(1)}, bf16[592,128]{1,0:T(8,128)(2,1)S(1)}, u32[]{:S(2)}, u32[]{:S(2)}) collective-permute-start(bf16[592,128]{1,0:T(8,128)(2,1)S(1)} %collective-permute-done.1.refs_1_), channel_id=1, source_target_pairs={{0,8},{1,9},{2,10},{3,11},{4,12},{5,13},{6,14},{7,15},{8,0},{9,1},... | collective-permute-start | bytes 454664 | tf_op jit(solution)/shard_map/ppermute | solution.py:395
  21.9 13.1 %collective-permute-start.11 = (bf16[1184,128]{1,0:T(8,128)(2,1)S(1)}, bf16[1184,128]{1,0:T(8,128)(2,1)S(1)}, u32[]{:S(2)}, u32[]{:S(2)}) collective-permute-start(bf16[1184,128]{1,0:T(8,128)(2,1)S(1)} %constant_dynamic-update-slice_fusion.5), channel_id=1, source_target_pairs={{0,4},{1,5},{2,6},{3,7},{4,0},{5,1},{6,2},{7,3},{8,12},{9,13},{10,... | collective-permute-start | bytes 909320 | tf_op jit(solution)/shard_map/ppermute | solution.py:395
  22.7 12.2 %collective-permute-start.12 = (bf16[1184,128]{1,0:T(8,128)(2,1)S(1)}, bf16[1184,128]{1,0:T(8,128)(2,1)S(1)}, u32[]{:S(2)}, u32[]{:S(2)}) collective-permute-start(bf16[1184,128]{1,0:T(8,128)(2,1)S(1)} %constant_dynamic-update-slice_fusion.5), channel_id=1, source_target_pairs={{0,1},{1,0},{2,3},{3,2},{4,5},{5,4},{6,7},{7,6},{8,9},{9,8},{10,11... | collective-permute-start | bytes 909320 | tf_op jit(solution)/shard_map/ppermute | solution.py:395
  23.4 10.4 %collective-permute-start.8 = (bf16[592,128]{1,0:T(8,128)(2,1)S(1)}, bf16[592,128]{1,0:T(8,128)(2,1)S(1)}, u32[]{:S(2)}, u32[]{:S(2)}) collective-permute-start(bf16[592,128]{1,0:T(8,128)(2,1)S(1)} %collective-permute-done.3.refs_3_), channel_id=1, source_target_pairs={{0,16},{1,17},{2,18},{3,19},{4,20},{5,21},{6,22},{7,23},{8,24},{9,... | collective-permute-start | bytes 454664 | tf_op jit(solution)/shard_map/ppermute | solution.py:395
  27.5 14.9 %collective-permute-start.10 = (bf16[592,128]{1,0:T(8,128)(2,1)S(1)}, bf16[592,128]{1,0:T(8,128)(2,1)S(1)}, u32[]{:S(2)}, u32[]{:S(2)}) collective-permute-start(bf16[592,128]{1,0:T(8,128)(2,1)S(1)} %collective-permute-done.5.refs_1_), channel_id=1, source_target_pairs={{0,1},{1,0},{2,3},{3,2},{4,5},{5,4},{6,7},{7,6},{8,9},{9,8},{10,11... | collective-permute-start | bytes 454664 | tf_op jit(solution)/shard_map/ppermute | solution.py:395
  28.2 14.2 %collective-permute-start.6 = (bf16[592,128]{1,0:T(8,128)(2,1)S(1)}, bf16[592,128]{1,0:T(8,128)(2,1)S(1)}, u32[]{:S(2)}, u32[]{:S(2)}) collective-permute-start(bf16[592,128]{1,0:T(8,128)(2,1)S(1)} %collective-permute-done.5.refs_1_), channel_id=1, source_target_pairs={{0,4},{1,5},{2,6},{3,7},{4,0},{5,1},{6,2},{7,3},{8,12},{9,13},{10,... | collective-permute-start | bytes 454664 | tf_op jit(solution)/shard_map/ppermute | solution.py:395
  33.8 8.6 %collective-permute-start.9 = (bf16[1184,128]{1,0:T(8,128)(2,1)S(1)}, bf16[1184,128]{1,0:T(8,128)(2,1)S(1)}, u32[]{:S(2)}, u32[]{:S(2)}) collective-permute-start(bf16[1184,128]{1,0:T(8,128)(2,1)S(1)} %pad_maximum_fusion), channel_id=1, source_target_pairs={{0,8},{1,9},{2,10},{3,11},{4,12},{5,13},{6,14},{7,15},{8,0},{9,1},... | collective-permute-start | bytes 909320 | tf_op jit(solution)/shard_map/ppermute | solution.py:395
  47.1 2.0 %collective-permute-start.13 = (bf16[4,64,8,128]{3,2,1,0:T(8,128)(2,1)S(1)}, bf16[4,64,8,128]{3,2,1,0:T(8,128)(2,1)S(1)}, u32[]{:S(2)}, u32[]{:S(2)}) collective-permute-start(bf16[4,64,8,128]{3,2,1,0:T(8,128)(2,1)S(1)} %get-tuple-element.49), channel_id=1, source_target_pairs={{0,2},{1,3},{2,0},{3,1},{4,6},{5,7},{6,4},{7,5},{8,10},{9,11},{10,... | collective-permute-start | bytes 1572872 | tf_op jit(solution)/shard_map/ppermute | solution.py:395

commit v7 on v6

--- a/solution.py
+++ b/solution.py
@@ -133,7 +133,7 @@
     kv_at = q_at + n_heads * q_rows
     lengths = [sum(len(blocks) for _, blocks in pieces) * rows for _, _, pieces, _ in groups_of]
     extra = 2 * tokens if stretch is not None else 0
-    chunk = 256
+    chunk = 512
 
     operands, where = [], {}
 
@@ -216,15 +216,15 @@
             task()
         later = blocks_in(1) if len(plan) > 1 else []
 
-        works = [(g, k) for g in range(len(plan)) for k in range(half)]
+        works = [(g, k, e) for g in range(len(plan)) for k in range(half) for e in range(2)]
 
         def parts(work):
             return [(c, min(chunk, lengths[work[0]] - c)) for c in range(0, lengths[work[0]], chunk)]
 
         def scaled_queries(work):
-            g, k = work
+            g, k, e = work
             first = q_at + (plan[g][0] + k) * q_rows
-            scaled = jnp.concatenate([ref[first : first + q_rows, :] for ref in requests], axis=0).astype(f32) * scale
+            scaled = requests[e][first : first + q_rows, :].astype(f32) * scale
             hi = scaled.astype(bf16)
             lo = (scaled - hi.astype(f32)).astype(bf16)
             return jnp.concatenate([hi, lo], axis=1)
@@ -240,28 +240,23 @@
             slot[:, c : c + width] = score
             return fold(top, score)
 
-        def stretch_rows(work, e, which):
-            g, k = work
+        def stretch_rows(work, which):
+            g, k, e = work
             head = plan[g][0] + k
             base = stretch[1] + (e * n_heads + (head + half) % n_heads) * 2 * tokens + which * tokens
             mine = kv_at + head * 2 * tokens + which * tokens
             return jnp.concatenate([other[base : base + tokens, :], requests[e][mine : mine + tokens, :]], axis=0)
 
         def score_stretch(work, q, slot, top):
-            for e in range(2):
-                key = stretch_rows(work, e, 0)
-                key = jnp.concatenate([key, key], axis=1)
-                score = lax.dot_general(
-                    q[e * q_rows : (e + 1) * q_rows], key, (((1,), (1,)), ((), ())), preferred_element_type=f32
-                )
-                column = lax.broadcasted_iota(jnp.int32, score.shape, 1)
-                row = lax.broadcasted_iota(jnp.int32, score.shape, 0) // group
-                allowed = (column - tokens <= row) & (column >= tokens * (1 - inner))
-                tops.append(jnp.where(allowed, score, -jnp.inf))
-                slot[e * q_rows : (e + 1) * q_rows, lengths[work[0]] : lengths[work[0]] + extra] = tops[-1]
-            return fold(top, jnp.concatenate(tops[-2:], axis=0))
-
-        tops = []
+            key = stretch_rows(work, 0)
+            key = jnp.concatenate([key, key], axis=1)
+            score = lax.dot_general(q, key, (((1,), (1,)), ((), ())), preferred_element_type=f32)
+            column = lax.broadcasted_iota(jnp.int32, score.shape, 1)
+            row = lax.broadcasted_iota(jnp.int32, score.shape, 0) // group
+            allowed = (column - tokens <= row) & (column >= tokens * (1 - inner))
+            score = jnp.where(allowed, score, -jnp.inf)
+            slot[:, lengths[work[0]] : lengths[work[0]] + extra] = score
+            return fold(top, score)
 
         def weigh(slot, m, part, mixed, c, width, value):
             weights = []
@@ -270,14 +265,11 @@
                 part = part + weight
                 weights.append(weight.astype(bf16))
             weight = jnp.concatenate(weights, axis=1) if len(weights) > 1 else weights[0]
-            if isinstance(value, list):
-                new = [jnp.dot(weight[i * q_rows : (i + 1) * q_rows], v, preferred_element_type=f32) for i, v in enumerate(value)]
-                return part, mixed + jnp.concatenate(new, axis=0)
             return part, mixed + jnp.dot(weight, value, preferred_element_type=f32)
 
         def place_of(work):
-            g, k = work
-            return plan[g][0] + k
+            g, k, e = work
+            return plan[g][0] + k, slice(e * q_rows, (e + 1) * q_rows), slice(None)
 
         current = None
         for t in range(len(works) + 1):
@@ -292,10 +284,10 @@
                 if work is not None and work[0] in stretch[2]:
                     top = score_stretch(work, q, slot, top)
                 if current is not None and done[0] in stretch[2]:
-                    part, mixed = weigh(old, m, part, mixed, lengths[done[0]], extra, [stretch_rows(done, e, 1) for e in range(2)])
+                    part, mixed = weigh(old, m, part, mixed, lengths[done[0]], extra, stretch_rows(done, 1))
             ahead = parts(work) if work is not None else []
             behind = parts(done) if current is not None else []
-            first_steps = half * len(parts(works[0]))
+            first_steps = 2 * half * len(parts(works[0]))
             for i in range(max(len(ahead), len(behind))):
                 for _ in range(-(-len(blocks_in(1)) // first_steps) if later else 0):
                     if later:
@@ -309,17 +301,15 @@
                 if final:
                     head = plan[done[0]][0] + done[1]
                     result = mixed / jnp.sum(part, axis=1, keepdims=True)
-                    for e in range(2):
-                        result_e = result[e * q_rows : (e + 1) * q_rows].reshape(tokens, group, head_dim)
-                        results[e][head] = result_e.astype(bf16)
+                    results[done[2]][head] = result.reshape(tokens, group, head_dim).astype(bf16)
                 else:
                     for ref, value in zip(results, (m, part, mixed)):
                         ref[place_of(done)] = value
             if work is not None:
-                m = jnp.broadcast_to(jnp.max(top, axis=1, keepdims=True), (2 * q_rows, 128))
+                m = jnp.broadcast_to(jnp.max(top, axis=1, keepdims=True), (q_rows, 128))
                 if not groups_of[work[0]][3]:
-                    part = jnp.zeros((2 * q_rows, 128), f32)
-                    mixed = jnp.zeros((2 * q_rows, head_dim), f32)
+                    part = jnp.zeros((q_rows, 128), f32)
+                    mixed = jnp.zeros((q_rows, head_dim), f32)
                 else:
                     past = before[0][place_of(work)]
                     m = jnp.maximum(past, m)
@@ -334,7 +324,7 @@
         out_shape = (jax.ShapeDtypeStruct((n_heads, 2 * q_rows, 128), f32),) * 3
     alias = {1 + n_plain + j: j for j in range(3)} if state is not None and not final else {}
     pairs = 2 * half * q_rows * (sum(lengths) + (extra * len(stretch[2]) if stretch is not None else 0))
-    slot = pltpu.VMEM((2 * q_rows, max(lengths) + extra), f32)
+    slot = pltpu.VMEM((q_rows, max(lengths) + extra), f32)
     return pl.pallas_call(
         kernel,
         out_shape=out_shape,
@@ -445,7 +435,7 @@
     other_book, other_stretch = (y_pack, size), (y_pack, size + half * codes)
 
     state = call([(0, own_book, pieces(pack, x_pack, z_one[-1]), False)], stretch=None, state=None, final=False)
-    *z_one, diag, first, second, third = lax.optimization_barrier((*z_one, diag, *state))
+    *z_one, first, second, third = lax.optimization_barrier((*z_one, *state))
     state = (first, second, third)
     z_two, reached = [], [z_one[0]]
     for i, bits in enumerate(steps[1:]):

time: 50.8 us -> 50.9 us (level)
  transfers between devices with their start and end apart: 14 -> 14, of which waited for: 5 -> 5; matrix products, arithmetic and copies ran while one was open for 2% -> 2% of each run, Pallas kernels for 33% -> 32%
where the time goes in v7:
time: 50.9 us; the launch traced here: 50.7 us
  Pallas kernels  26.1 us (51%)
  starting transfers between devices  17.5 us (34%)
  waiting for transfers between devices  4.84 us (10%)
  local copies, waits for them, and re-layouts  1.07 us (2%)
  between operations  1.05 us (2%)
    pallas_call x4, Pallas kernels, attend(): pl.pallas_call(kernel, out_shape=out_shape, in_specs=[whole(pltpu.SMEM)]...  20.2 us
    ppermute x14, starting transfers between devices, swap(): lax.ppermute(x, axes, [(2 * o + i, 2 * (o ^ outer_bits) + (i ^ inner_bits...  17.5 us
    ppermute x14, waiting for transfers between devices, swap(): lax.ppermute(x, axes, [(2 * o + i, 2 * (o ^ outer_bits) + (i ^ inner_bits...  4.84 us
    pallas_call x1, Pallas kernels, prepare(): pl.pallas_call(kernel, out_shape=(shape, shape), in_specs=[whole(pltpu.SM...  3.17 us
    pallas_call x2, Pallas kernels, lay_out(): pl.pallas_call(kernel, out_shape=jax.ShapeDtypeStruct((tokens, 2 * n_out,...  2.73 us
  transfers between devices with their start and end apart: 14, of which 5 were waited for; matrix products, arithmetic and copies ran while one was open for 2% of the time, Pallas kernels for 32%

profile of v7, /device:TPU:0, one launch (start us, length us, event | category | flops | bytes accessed | tf_op | source)
XLA Modules:
  0.0 50.7 jit_solution(7433618802208430615)
XLA Ops:
  0.0 0.0 copy-start.1
  0.0 0.0 copy-start.2
  0.0 0.0 copy-start.3
  0.0 0.0 copy-start.4
  0.0 0.0 copy-start
  0.7 0.1 pad_add_fusion.place
  0.8 3.2 %prepare.1 = (bf16[2864,128]{1,0:T(8,128)(2,1)S(1)}, bf16[2864,128]{1,0:T(8,128)(2,1)S(1)}) custom-call(s32[2]{0:T(128)S(1)} %pad_add_fusion.place, s32[1]{0:T(128)S(6)} %copy.34.ids, s32[4,16,128]{2,1,0:T(8,128)} %bitcast.8, bf16[128,4,128]{2,1,0:T(4,128)(2,1)} %refs_1_.1, f32[4,128]{1,0:T(4,128)} %bitcast.9, bf16[64,10,8,128]{3,2,1,0:T(8,128)(2,1)} %bitcast.6, ...), custom_call_target="tpu_custom_call" | custom-call | tf_op jit(solution)/shard_map/prepare/pallas_call | solution.py:108
  4.0 0.5 %collective-permute-start = (bf16[2864,128]{1,0:T(8,128)(2,1)S(1)}, bf16[2864,128]{1,0:T(8,128)(2,1)S(1)}, u32[]{:S(2)}, u32[]{:S(2)}) collective-permute-start(bf16[2864,128]{1,0:T(8,128)(2,1)S(1)} %get-tuple-element.28), channel_id=1, source_target_pairs={{0,2},{1,3},{2,0},{3,1},{4,6},{5,7},{6,4},{7,5},{8,10},{9,11},{10,... | collective-permute-start | bytes 2199560 | tf_op jit(solution)/shard_map/ppermute | solution.py:385
  4.5 0.9 %constant_dynamic-slice_fusion = bf16[2,256,128]{2,1,0:T(8,128)(2,1)S(1)} fusion(bf16[4,256,128]{2,1,0:T(8,128)(2,1)} %refs_0_.7, s32[]{:T(128)S(6)} %select_n.11), kind=kLoop, calls=%fused_computation.12 | loop fusion | bytes 262148 | tf_op jit(solution)/shard_map/dynamic_slice | solution.py:410
  5.4 0.9 %collective-permute-done.refs_9_.refs_11_.refs_10_ = bf16[2864,128]{1,0:T(8,128)(2,1)S(1)} collective-permute-done((bf16[2864,128]{1,0:T(8,128)(2,1)S(1)}, bf16[2864,128]{1,0:T(8,128)(2,1)S(1)}, u32[]{:S(2)}, u32[]{:S(2)}) %collective-permute-start) | collective-permute-done | bytes 733216 | tf_op jit(solution)/shard_map/ppermute | solution.py:385
  6.5 3.0 %collective-permute-start.6 = (bf16[2128,128]{1,0:T(8,128)(2,1)S(1)}, bf16[2128,128]{1,0:T(8,128)(2,1)S(1)}, u32[]{:S(2)}, u32[]{:S(2)}) collective-permute-start(bf16[2128,128]{1,0:T(8,128)(2,1)S(1)} %slice_dynamic-update-slice_fusion), channel_id=1, source_target_pairs={{0,1},{1,0},{2,3},{3,2},{4,5},{5,4},{6,7},{7,6},{8,9},{9,8},{10,11... | collective-permute-start | bytes 1634312 | tf_op jit(solution)/shard_map/ppermute | solution.py:385
  9.4 1.6 %collective-permute-start.2 = (bf16[592,128]{1,0:T(8,128)(2,1)S(1)}, bf16[592,128]{1,0:T(8,128)(2,1)S(1)}, u32[]{:S(2)}, u32[]{:S(2)}) collective-permute-start(bf16[592,128]{1,0:T(8,128)(2,1)S(1)} %pad_maximum_fusion.1.refs_1_), channel_id=1, source_target_pairs={{0,8},{1,9},{2,10},{3,11},{4,12},{5,13},{6,14},{7,15},{8,0},{9,1},... | collective-permute-start | bytes 454664 | tf_op jit(solution)/shard_map/ppermute | solution.py:385
  11.1 1.5 %collective-permute-start.3 = (bf16[592,128]{1,0:T(8,128)(2,1)S(1)}, bf16[592,128]{1,0:T(8,128)(2,1)S(1)}, u32[]{:S(2)}, u32[]{:S(2)}) collective-permute-start(bf16[592,128]{1,0:T(8,128)(2,1)S(1)} %pad_maximum_fusion.1.refs_1_), channel_id=1, source_target_pairs={{0,4},{1,5},{2,6},{3,7},{4,0},{5,1},{6,2},{7,3},{8,12},{9,13},{10,... | collective-permute-start | bytes 454664 | tf_op jit(solution)/shard_map/ppermute | solution.py:385
  12.6 2.6 %collective-permute-start.1 = (bf16[592,128]{1,0:T(8,128)(2,1)S(1)}, bf16[592,128]{1,0:T(8,128)(2,1)S(1)}, u32[]{:S(2)}, u32[]{:S(2)}) collective-permute-start(bf16[592,128]{1,0:T(8,128)(2,1)S(1)} %pad_maximum_fusion.1.refs_1_), channel_id=1, source_target_pairs={{0,16},{1,17},{2,18},{3,19},{4,20},{5,21},{6,22},{7,23},{8,24},{9,... | collective-permute-start | bytes 454664 | tf_op jit(solution)/shard_map/ppermute | solution.py:385
  15.2 0.5 collective-permute-start.7
  15.6 0.0 collective-permute-done.2.refs_3_
  15.6 0.9 %collective-permute-done.3.refs_2_ = bf16[592,128]{1,0:T(8,128)(2,1)S(1)} collective-permute-done((bf16[592,128]{1,0:T(8,128)(2,1)S(1)}, bf16[592,128]{1,0:T(8,128)(2,1)S(1)}, u32[]{:S(2)}, u32[]{:S(2)}) %collective-permute-start.3) | collective-permute-done | bytes 151584 | tf_op jit(solution)/shard_map/ppermute | solution.py:385
  16.5 0.0 copy-done.1
  16.5 0.0 copy-done.2
  16.5 0.0 copy-done.3
  16.5 0.0 copy-done.4
  16.5 0.0 copy-done
  16.5 3.4 %attend.4 = (f32[4,1024,128]{2,1,0:T(8,128)S(1)}, f32[4,1024,128]{2,1,0:T(8,128)S(1)}, f32[4,1024,128]{2,1,0:T(8,128)S(1)}) custom-call(s32[2]{0:T(128)S(1)} %pad_add_fusion.place, bf16[4,256,128]{2,1,0:T(8,128)(2,1)S(1)} %copy-done, bf16[592,128]{1,0:T(8,128)(2,1)S(1)} %pad_maximum_fusion.1.refs_1_, bf16[592,128]{1,0:T(8,128)(2,1)S(1)} %collective-permute-done.3.refs_2_, ...), custom_call_target="tpu_custom_call" | custom-call | flops 1610612736 | bytes 4194304 | tf_op jit(solution)/shard_map/attend/pallas_call | solution.py:328
  19.9 2.0 %collective-permute-done.1.refs_1_ = bf16[592,128]{1,0:T(8,128)(2,1)S(1)} collective-permute-done((bf16[592,128]{1,0:T(8,128)(2,1)S(1)}, bf16[592,128]{1,0:T(8,128)(2,1)S(1)}, u32[]{:S(2)}, u32[]{:S(2)}) %collective-permute-start.1) | collective-permute-done | bytes 151584 | tf_op jit(solution)/shard_map/ppermute | solution.py:385
  21.9 0.0 collective-permute-start.4
  22.0 0.8 %collective-permute-start.11 = (bf16[1184,128]{1,0:T(8,128)(2,1)S(1)}, bf16[1184,128]{1,0:T(8,128)(2,1)S(1)}, u32[]{:S(2)}, u32[]{:S(2)}) collective-permute-start(bf16[1184,128]{1,0:T(8,128)(2,1)S(1)} %constant_dynamic-update-slice_fusion.5), channel_id=1, source_target_pairs={{0,4},{1,5},{2,6},{3,7},{4,0},{5,1},{6,2},{7,3},{8,12},{9,13},{10,... | collective-permute-start | bytes 909320 | tf_op jit(solution)/shard_map/ppermute | solution.py:385
  22.8 0.5 collective-permute-start.12
  23.2 0.0 collective-permute-done.7.refs_3_
  23.2 3.5 %collective-permute-start.8 = (bf16[592,128]{1,0:T(8,128)(2,1)S(1)}, bf16[592,128]{1,0:T(8,128)(2,1)S(1)}, u32[]{:S(2)}, u32[]{:S(2)}) collective-permute-start(bf16[592,128]{1,0:T(8,128)(2,1)S(1)} %collective-permute-done.7.refs_3_), channel_id=1, source_target_pairs={{0,16},{1,17},{2,18},{3,19},{4,20},{5,21},{6,22},{7,23},{8,24},{9,... | collective-permute-start | bytes 454664 | tf_op jit(solution)/shard_map/ppermute | solution.py:385
  26.8 0.6 %collective-permute-done.4.refs_1_ = bf16[592,128]{1,0:T(8,128)(2,1)S(1)} collective-permute-done((bf16[592,128]{1,0:T(8,128)(2,1)S(1)}, bf16[592,128]{1,0:T(8,128)(2,1)S(1)}, u32[]{:S(2)}, u32[]{:S(2)}) %collective-permute-start.4) | collective-permute-done | bytes 151584 | tf_op jit(solution)/shard_map/ppermute | solution.py:385
  27.3 1.0 %collective-permute-start.10 = (bf16[592,128]{1,0:T(8,128)(2,1)S(1)}, bf16[592,128]{1,0:T(8,128)(2,1)S(1)}, u32[]{:S(2)}, u32[]{:S(2)}) collective-permute-start(bf16[592,128]{1,0:T(8,128)(2,1)S(1)} %collective-permute-done.4.refs_1_), channel_id=1, source_target_pairs={{0,1},{1,0},{2,3},{3,2},{4,5},{5,4},{6,7},{7,6},{8,9},{9,8},{10,11... | collective-permute-start | bytes 454664 | tf_op jit(solution)/shard_map/ppermute | solution.py:385
  28.3 0.0 collective-permute-done.6.refs_2_.refs_3_
  28.3 0.8 %collective-permute-start.5 = (bf16[592,128]{1,0:T(8,128)(2,1)S(1)}, bf16[592,128]{1,0:T(8,128)(2,1)S(1)}, u32[]{:S(2)}, u32[]{:S(2)}) collective-permute-start(bf16[592,128]{1,0:T(8,128)(2,1)S(1)} %collective-permute-done.4.refs_1_), channel_id=1, source_target_pairs={{0,4},{1,5},{2,6},{3,7},{4,0},{5,1},{6,2},{7,3},{8,12},{9,13},{10,... | collective-permute-start | bytes 454664 | tf_op jit(solution)/shard_map/ppermute | solution.py:385
  29.1 4.4 %attend.5 = (f32[4,1024,128]{2,1,0:T(8,128)S(1)}, f32[4,1024,128]{2,1,0:T(8,128)S(1)}, f32[4,1024,128]{2,1,0:T(8,128)S(1)}) custom-call(s32[2]{0:T(128)S(1)} %pad_add_fusion.place, bf16[4,256,128]{2,1,0:T(8,128)(2,1)S(1)} %copy-done, ...), custom_call_target="tpu_custom_call", output_to_operand_aliasing={{0}: (11, {}), {1}: (12, {}), {2}: (13, {})} | custom-call | flops 1879048192 | bytes 4194304 | tf_op jit(solution)/shard_map/attend/pallas_call | solution.py:328
  33.5 0.0 collective-permute-done.8.refs_4_
  33.6 1.2 %collective-permute-start.9 = (bf16[1184,128]{1,0:T(8,128)(2,1)S(1)}, bf16[1184,128]{1,0:T(8,128)(2,1)S(1)}, u32[]{:S(2)}, u32[]{:S(2)}) collective-permute-start(bf16[1184,128]{1,0:T(8,128)(2,1)S(1)} %pad_maximum_fusion), channel_id=1, source_target_pairs={{0,8},{1,9},{2,10},{3,11},{4,12},{5,13},{6,14},{7,15},{8,0},{9,1},... | collective-permute-start | bytes 909320 | tf_op jit(solution)/shard_map/ppermute | solution.py:385
  34.8 0.0 collective-permute-done.11.refs_2_
  34.8 0.0 collective-permute-done.12.refs_5_
  34.8 7.2 %attend.6 = (f32[4,1024,128]{2,1,0:T(8,128)S(1)}, f32[4,1024,128]{2,1,0:T(8,128)S(1)}, f32[4,1024,128]{2,1,0:T(8,128)S(1)}) custom-call(s32[2]{0:T(128)S(1)} %pad_add_fusion.place, bf16[4,256,128]{2,1,0:T(8,128)(2,1)S(1)} %copy-done, ...), custom_call_target="tpu_custom_call", output_to_operand_aliasing={{0}: (13, {}), {1}: (14, {}), {2}: (15, {})} | custom-call | flops 3489660928 | bytes 4194304 | tf_op jit(solution)/shard_map/attend/pallas_call | solution.py:328
  42.0 0.0 collective-permute-done.10.refs_4_
  42.0 0.0 collective-permute-done.5.refs_1_
  42.0 0.0 collective-permute-done.9.refs_3_
  42.0 5.2 %attend.7 = (bf16[4,64,8,128]{3,2,1,0:T(8,128)(2,1)S(1)}, bf16[4,64,8,128]{3,2,1,0:T(8,128)(2,1)S(1)}) custom-call(s32[2]{0:T(128)S(1)} %pad_add_fusion.place, bf16[4,256,128]{2,1,0:T(8,128)(2,1)S(1)} %copy-done, bf16[592,128]{1,0:T(8,128)(2,1)S(1)} %collective-permute-done.5.refs_1_, bf16[2128,128]{1,0:T(8,128)(2,1)S(1)} %collective-permute-done.6.refs_2_.refs_3_, ...), custom_call_target="tpu_custom_call" | custom-call | flops 2147483648 | bytes 4194304 | tf_op jit(solution)/shard_map/attend/pallas_call | solution.py:328
  47.2 0.1 collective-permute-start.13
  47.3 1.4 %lay_out.2.refs_0_ = bf16[64,8,8,128]{3,2,1,0:T(8,128)(2,1)} custom-call(s32[2]{0:T(128)S(1)} %pad_add_fusion.place, bf16[4,64,8,128]{3,2,1,0:T(8,128)(2,1)S(1)} %get-tuple-element.48.source), custom_call_target="tpu_custom_call" | custom-call | tf_op jit(solution)/shard_map/lay_out/pallas_call | solution.py:359
  48.7 0.5 %collective-permute-done.13.source = bf16[4,64,8,128]{3,2,1,0:T(8,128)(2,1)S(1)} collective-permute-done((bf16[4,64,8,128]{3,2,1,0:T(8,128)(2,1)S(1)}, bf16[4,64,8,128]{3,2,1,0:T(8,128)(2,1)S(1)}, u32[]{:S(2)}, u32[]{:S(2)}) %collective-permute-start.13) | collective-permute-done | bytes 524320 | tf_op jit(solution)/shard_map/ppermute | solution.py:385
  49.2 1.4 %lay_out.3 = bf16[64,8,8,128]{3,2,1,0:T(8,128)(2,1)} custom-call(s32[2]{0:T(128)S(1)} %pad_add_fusion.place, bf16[4,64,8,128]{3,2,1,0:T(8,128)(2,1)S(1)} %collective-permute-done.13.source, bf16[64,8,8,128]{3,2,1,0:T(8,128)(2,1)} %lay_out.2.refs_0_), custom_call_target="tpu_custom_call", output_to_operand_aliasing={{}: (2, {})} | custom-call | tf_op jit(solution)/shard_map/lay_out/pallas_call | solution.py:359
  (11 shorter events, 0.2 us)
Async XLA Ops:
  0.0 16.5 %copy-start.1 = (f32[64,128]{1,0:T(8,128)S(1)}, f32[64,128]{1,0:T(8,128)}, u32[]{:S(2)}) copy-start(f32[64,128]{1,0:T(8,128)} %constant.38.clone.refs_4_.refs_6_.refs_5_) | copy-start | bytes 98308
  0.0 16.5 %copy-start.2 = (f32[64,128]{1,0:T(8,128)S(1)}, f32[64,128]{1,0:T(8,128)}, u32[]{:S(2)}) copy-start(f32[64,128]{1,0:T(8,128)} %constant.39.clone.refs_5_.refs_7_.refs_6_) | copy-start | bytes 98308
  0.0 16.5 %copy-start.3 = (f32[64,128]{1,0:T(8,128)S(1)}, f32[64,128]{1,0:T(8,128)}, u32[]{:S(2)}) copy-start(f32[64,128]{1,0:T(8,128)} %constant.40.clone.refs_6_.refs_8_.refs_7_) | copy-start | bytes 98308
  0.0 16.5 %copy-start.4 = (f32[64,128]{1,0:T(8,128)S(1)}, f32[64,128]{1,0:T(8,128)}, u32[]{:S(2)}) copy-start(f32[64,128]{1,0:T(8,128)} %constant.41.clone.refs_7_.refs_9_.refs_8_) | copy-start | bytes 98308
  0.0 16.5 %copy-start = (bf16[4,256,128]{2,1,0:T(8,128)(2,1)S(1)}, bf16[4,256,128]{2,1,0:T(8,128)(2,1)}, u32[]{:S(2)}) copy-start(bf16[4,256,128]{2,1,0:T(8,128)(2,1)} %refs_0_.7) | copy-start | bytes 786436
  4.0 2.4 %collective-permute-start = (bf16[2864,128]{1,0:T(8,128)(2,1)S(1)}, bf16[2864,128]{1,0:T(8,128)(2,1)S(1)}, u32[]{:S(2)}, u32[]{:S(2)}) collective-permute-start(bf16[2864,128]{1,0:T(8,128)(2,1)S(1)} %get-tuple-element.28), channel_id=1, source_target_pairs={{0,2},{1,3},{2,0},{3,1},{4,6},{5,7},{6,4},{7,5},{8,10},{9,11},{10,... | collective-permute-start | bytes 2199560 | tf_op jit(solution)/shard_map/ppermute | solution.py:385
  6.5 21.8 %collective-permute-start.6 = (bf16[2128,128]{1,0:T(8,128)(2,1)S(1)}, bf16[2128,128]{1,0:T(8,128)(2,1)S(1)}, u32[]{:S(2)}, u32[]{:S(2)}) collective-permute-start(bf16[2128,128]{1,0:T(8,128)(2,1)S(1)} %slice_dynamic-update-slice_fusion), channel_id=1, source_target_pairs={{0,1},{1,0},{2,3},{3,2},{4,5},{5,4},{6,7},{7,6},{8,9},{9,8},{10,11... | collective-permute-start | bytes 1634312 | tf_op jit(solution)/shard_map/ppermute | solution.py:385
  9.4 6.2 %collective-permute-start.2 = (bf16[592,128]{1,0:T(8,128)(2,1)S(1)}, bf16[592,128]{1,0:T(8,128)(2,1)S(1)}, u32[]{:S(2)}, u32[]{:S(2)}) collective-permute-start(bf16[592,128]{1,0:T(8,128)(2,1)S(1)} %pad_maximum_fusion.1.refs_1_), channel_id=1, source_target_pairs={{0,8},{1,9},{2,10},{3,11},{4,12},{5,13},{6,14},{7,15},{8,0},{9,1},... | collective-permute-start | bytes 454664 | tf_op jit(solution)/shard_map/ppermute | solution.py:385
  11.1 5.4 %collective-permute-start.3 = (bf16[592,128]{1,0:T(8,128)(2,1)S(1)}, bf16[592,128]{1,0:T(8,128)(2,1)S(1)}, u32[]{:S(2)}, u32[]{:S(2)}) collective-permute-start(bf16[592,128]{1,0:T(8,128)(2,1)S(1)} %pad_maximum_fusion.1.refs_1_), channel_id=1, source_target_pairs={{0,4},{1,5},{2,6},{3,7},{4,0},{5,1},{6,2},{7,3},{8,12},{9,13},{10,... | collective-permute-start | bytes 454664 | tf_op jit(solution)/shard_map/ppermute | solution.py:385
  12.6 9.3 %collective-permute-start.1 = (bf16[592,128]{1,0:T(8,128)(2,1)S(1)}, bf16[592,128]{1,0:T(8,128)(2,1)S(1)}, u32[]{:S(2)}, u32[]{:S(2)}) collective-permute-start(bf16[592,128]{1,0:T(8,128)(2,1)S(1)} %pad_maximum_fusion.1.refs_1_), channel_id=1, source_target_pairs={{0,16},{1,17},{2,18},{3,19},{4,20},{5,21},{6,22},{7,23},{8,24},{9,... | collective-permute-start | bytes 454664 | tf_op jit(solution)/shard_map/ppermute | solution.py:385
  15.2 8.1 %collective-permute-start.7 = (bf16[592,128]{1,0:T(8,128)(2,1)S(1)}, bf16[592,128]{1,0:T(8,128)(2,1)S(1)}, u32[]{:S(2)}, u32[]{:S(2)}) collective-permute-start(bf16[592,128]{1,0:T(8,128)(2,1)S(1)} %pad_maximum_fusion.1.refs_1_), channel_id=1, source_target_pairs={{0,5},{1,4},{2,7},{3,6},{4,1},{5,0},{6,3},{7,2},{8,13},{9,12},{10,... | collective-permute-start | bytes 454664 | tf_op jit(solution)/shard_map/ppermute | solution.py:385
  21.9 5.4 %collective-permute-start.4 = (bf16[592,128]{1,0:T(8,128)(2,1)S(1)}, bf16[592,128]{1,0:T(8,128)(2,1)S(1)}, u32[]{:S(2)}, u32[]{:S(2)}) collective-permute-start(bf16[592,128]{1,0:T(8,128)(2,1)S(1)} %collective-permute-done.1.refs_1_), channel_id=1, source_target_pairs={{0,8},{1,9},{2,10},{3,11},{4,12},{5,13},{6,14},{7,15},{8,0},{9,1},... | collective-permute-start | bytes 454664 | tf_op jit(solution)/shard_map/ppermute | solution.py:385
  22.0 12.8 %collective-permute-start.11 = (bf16[1184,128]{1,0:T(8,128)(2,1)S(1)}, bf16[1184,128]{1,0:T(8,128)(2,1)S(1)}, u32[]{:S(2)}, u32[]{:S(2)}) collective-permute-start(bf16[1184,128]{1,0:T(8,128)(2,1)S(1)} %constant_dynamic-update-slice_fusion.5), channel_id=1, source_target_pairs={{0,4},{1,5},{2,6},{3,7},{4,0},{5,1},{6,2},{7,3},{8,12},{9,13},{10,... | collective-permute-start | bytes 909320 | tf_op jit(solution)/shard_map/ppermute | solution.py:385
  22.8 12.0 %collective-permute-start.12 = (bf16[1184,128]{1,0:T(8,128)(2,1)S(1)}, bf16[1184,128]{1,0:T(8,128)(2,1)S(1)}, u32[]{:S(2)}, u32[]{:S(2)}) collective-permute-start(bf16[1184,128]{1,0:T(8,128)(2,1)S(1)} %constant_dynamic-update-slice_fusion.5), channel_id=1, source_target_pairs={{0,1},{1,0},{2,3},{3,2},{4,5},{5,4},{6,7},{7,6},{8,9},{9,8},{10,11... | collective-permute-start | bytes 909320 | tf_op jit(solution)/shard_map/ppermute | solution.py:385
  23.2 10.3 %collective-permute-start.8 = (bf16[592,128]{1,0:T(8,128)(2,1)S(1)}, bf16[592,128]{1,0:T(8,128)(2,1)S(1)}, u32[]{:S(2)}, u32[]{:S(2)}) collective-permute-start(bf16[592,128]{1,0:T(8,128)(2,1)S(1)} %collective-permute-done.7.refs_3_), channel_id=1, source_target_pairs={{0,16},{1,17},{2,18},{3,19},{4,20},{5,21},{6,22},{7,23},{8,24},{9,... | collective-permute-start | bytes 454664 | tf_op jit(solution)/shard_map/ppermute | solution.py:385
  27.3 14.7 %collective-permute-start.10 = (bf16[592,128]{1,0:T(8,128)(2,1)S(1)}, bf16[592,128]{1,0:T(8,128)(2,1)S(1)}, u32[]{:S(2)}, u32[]{:S(2)}) collective-permute-start(bf16[592,128]{1,0:T(8,128)(2,1)S(1)} %collective-permute-done.4.refs_1_), channel_id=1, source_target_pairs={{0,1},{1,0},{2,3},{3,2},{4,5},{5,4},{6,7},{7,6},{8,9},{9,8},{10,11... | collective-permute-start | bytes 454664 | tf_op jit(solution)/shard_map/ppermute | solution.py:385
  28.3 13.7 %collective-permute-start.5 = (bf16[592,128]{1,0:T(8,128)(2,1)S(1)}, bf16[592,128]{1,0:T(8,128)(2,1)S(1)}, u32[]{:S(2)}, u32[]{:S(2)}) collective-permute-start(bf16[592,128]{1,0:T(8,128)(2,1)S(1)} %collective-permute-done.4.refs_1_), channel_id=1, source_target_pairs={{0,4},{1,5},{2,6},{3,7},{4,0},{5,1},{6,2},{7,3},{8,12},{9,13},{10,... | collective-permute-start | bytes 454664 | tf_op jit(solution)/shard_map/ppermute | solution.py:385
  33.6 8.5 %collective-permute-start.9 = (bf16[1184,128]{1,0:T(8,128)(2,1)S(1)}, bf16[1184,128]{1,0:T(8,128)(2,1)S(1)}, u32[]{:S(2)}, u32[]{:S(2)}) collective-permute-start(bf16[1184,128]{1,0:T(8,128)(2,1)S(1)} %pad_maximum_fusion), channel_id=1, source_target_pairs={{0,8},{1,9},{2,10},{3,11},{4,12},{5,13},{6,14},{7,15},{8,0},{9,1},... | collective-permute-start | bytes 909320 | tf_op jit(solution)/shard_map/ppermute | solution.py:385
  47.2 2.0 %collective-permute-start.13 = (bf16[4,64,8,128]{3,2,1,0:T(8,128)(2,1)S(1)}, bf16[4,64,8,128]{3,2,1,0:T(8,128)(2,1)S(1)}, u32[]{:S(2)}, u32[]{:S(2)}) collective-permute-start(bf16[4,64,8,128]{3,2,1,0:T(8,128)(2,1)S(1)} %get-tuple-element.47), channel_id=1, source_target_pairs={{0,2},{1,3},{2,0},{3,1},{4,6},{5,7},{6,4},{7,5},{8,10},{9,11},{10,... | collective-permute-start | bytes 1572872 | tf_op jit(solution)/shard_map/ppermute | solution.py:385
